TPU v7x, 32 devices: a whole 2x2x4 slice. The times are simulated.
32 devices in a mesh: dp: 4 (over y, x), sp: 8 (over z, core).
Axes of the slice: x: 2, y: 2, z: 4, core: 2. Of those that a mesh axis runs over, the one named last changes fastest.
Arguments:
- block_input: bfloat16 [4, 1024, 2048], P('dp', 'sp'), may hold values from -6 to 6
- segments: int32 [4, 1024], P('dp', 'sp'), may hold values from 0 to 4, as said below
- out_grad: bfloat16 [4, 1024, 2048], P('dp', 'sp'), may hold values from -6 to 6
- ln1_gain: bfloat16 [2048], P(('dp', 'sp')), may hold values from 0.5 to 1.5
- ln1_bias: bfloat16 [2048], P(('dp', 'sp')), may hold values from -1 to 1
- w_qkv: bfloat16 [2048, 6144], P(('dp', 'sp')), may hold values from -0.1875 to 0.1875
- b_qkv: bfloat16 [6144], P(('dp', 'sp')), may hold values from -1 to 1
- w_attn_out: bfloat16 [2048, 2048], P(('dp', 'sp')), may hold values from -0.5 to 0.5
- b_attn_out: bfloat16 [2048], P(('dp', 'sp')), may hold values from -1 to 1
- ln2_gain: bfloat16 [2048], P(('dp', 'sp')), may hold values from 0.5 to 1.5
- ln2_bias: bfloat16 [2048], P(('dp', 'sp')), may hold values from -1 to 1
- w_up: bfloat16 [2048, 8192], P(('dp', 'sp')), may hold values from -0.125 to 0.125
- b_up: bfloat16 [8192], P(('dp', 'sp')), may hold values from -1.5 to 1.5
- w_down: bfloat16 [8192, 2048], P(('dp', 'sp')), may hold values from -0.0625 to 0.0625
- b_down: bfloat16 [2048], P(('dp', 'sp')), may hold values from -1 to 1
Outputs:
- block_output: float32 [4, 1024, 2048], P('dp', 'sp')
- input_grad: float32 [4, 1024, 2048], P('dp', 'sp')
- grad_ln1_gain: float32 [2048], P(('dp', 'sp'))
- grad_ln1_bias: float32 [2048], P(('dp', 'sp'))
- grad_w_qkv: float32 [2048, 6144], P(('dp', 'sp'))
- grad_b_qkv: float32 [6144], P(('dp', 'sp'))
- grad_w_attn_out: float32 [2048, 2048], P(('dp', 'sp'))
- grad_b_attn_out: float32 [2048], P(('dp', 'sp'))
- grad_ln2_gain: float32 [2048], P(('dp', 'sp'))
- grad_ln2_bias: float32 [2048], P(('dp', 'sp'))
- grad_w_up: float32 [2048, 8192], P(('dp', 'sp'))
- grad_b_up: float32 [8192], P(('dp', 'sp'))
- grad_w_down: float32 [8192, 2048], P(('dp', 'sp'))
- grad_b_down: float32 [2048], P(('dp', 'sp'))
Inputs may be any that keep to these rules, and one draw needn't show every extreme that they name: `segments`: segment numbers never fall along a sequence. In each sequence one document begins within the first 128 tokens and ends within the last 128 tokens; two shorter documents come before it and two after it.
All inputs are finite; a program needn't handle non-finite values.
Results may differ from a plain program's by a relative error of at most 0.012.
Values may be sent and summed in bfloat16 or wider, within the bound.
No kernel may reach another device: no remote copies, remote signals or barrier semaphores. Data moves between devices by JAX's collectives and lax.ppermute only.
A program may use at most 704 MiB of HBM per device.

v0:
```python
import math

import jax
import jax.numpy as jnp
from jax import lax
from jax.sharding import PartitionSpec as P

HEADS = 8
HEAD = 256
ROT = 64


def normalize(values):
    center = values - jnp.mean(values, axis=-1, keepdims=True)
    spread = jnp.mean(center * center, axis=-1, keepdims=True)
    return center * lax.rsqrt(spread + 1e-05)


def norm_layer(values, gain_vec, shift_vec):
    return normalize(values) * gain_vec + shift_vec


def both_norms(values, gain_one, shift_one, gain_two, shift_two):
    return (norm_layer(values, gain_one, shift_one), norm_layer(values, gain_two, shift_two))


def rotary_tables(positions):
    inverse_freq = 10000.0 ** (-jnp.arange(0, ROT, 2).astype(jnp.float32) / ROT)
    angles = positions[:, None] * inverse_freq[None, :]
    angles = jnp.concatenate([angles, angles], axis=1)
    return (jnp.cos(angles), jnp.sin(angles))


def rotate(values, cosine, sine):
    half_rot = ROT // 2
    rot_part = values[..., :ROT]
    turned = jnp.concatenate([-rot_part[..., half_rot:], rot_part[..., :half_rot]], axis=-1)
    rotated = rot_part * cosine[:, None, :] + turned * sine[:, None, :]
    return jnp.concatenate([rotated, values[..., ROT:]], axis=-1)


def over_blocks(update, carried, pieces):
    piece_rows = pieces[0].shape[0]
    block_size = math.gcd(piece_rows, 512)
    number = piece_rows // block_size
    stacked = tuple((piece.reshape((number, block_size) + piece.shape[1:]) for piece in pieces))

    def advance(state_now, block_item):
        block_index, blocks_now = block_item
        return (update(state_now, blocks_now, block_index * block_size), None)

    result, unused = lax.scan(advance, carried, (jnp.arange(number, dtype=jnp.int32), stacked))
    return result


def shards(
    block_input,
    segments,
    out_grad,
    ln1_gain,
    ln1_bias,
    w_qkv,
    b_qkv,
    w_attn_out,
    b_attn_out,
    ln2_gain,
    ln2_bias,
    w_up,
    b_up,
    w_down,
    b_down,
):
    inputs = block_input[0].astype(jnp.float32)
    tok_rows, model_width = inputs.shape
    seq_index = lax.axis_index("sp")
    seq_length = tok_rows * lax.axis_size("sp")
    query_pos = seq_index * tok_rows + jnp.arange(tok_rows, dtype=jnp.int32)
    rows_model = w_qkv.shape[0]
    rows_hidden = w_down.shape[0]
    cols_qkv = b_qkv.shape[0]
    cols_up = b_up.shape[0]
    joined_width = w_qkv.shape[1]
    hidden_width = w_up.shape[1]
    score_scale = 1.0 / math.sqrt(HEAD)
    normed = normalize(inputs)
    piece_qkv = lax.all_gather(w_qkv[None], ("dp", "sp"), axis=0, tiled=True)
    piece_up = lax.all_gather(w_up[None], ("dp", "sp"), axis=0, tiled=True)
    gain_one = lax.all_gather(ln1_gain[None], ("dp", "sp"), axis=0, tiled=True)
    shift_one = lax.all_gather(ln1_bias[None], ("dp", "sp"), axis=0, tiled=True)
    gain_two = lax.all_gather(ln2_gain[None], ("dp", "sp"), axis=0, tiled=True)
    shift_two = lax.all_gather(ln2_bias[None], ("dp", "sp"), axis=0, tiled=True)
    piece_bqkv = lax.all_gather(b_qkv[None], ("dp", "sp"), axis=0, tiled=True)
    piece_bup = lax.all_gather(b_up[None], ("dp", "sp"), axis=0, tiled=True)
    piece_count = piece_qkv.shape[0]
    norm_pieces = (
        jnp.stack([gain_one, shift_one, gain_two, shift_two])
        .astype(jnp.float32)
        .reshape(4, piece_count * rows_model)
    )
    low_one = (normed * norm_pieces[0] + norm_pieces[1]).astype(jnp.bfloat16)
    low_two = (normed * norm_pieces[2] + norm_pieces[3]).astype(jnp.bfloat16)
    joined = jnp.dot(
        low_one,
        piece_qkv.reshape(piece_count * rows_model, joined_width),
        preferred_element_type=jnp.float32,
    )
    hidden = jnp.dot(
        low_two,
        piece_up.reshape(piece_count * rows_model, hidden_width),
        preferred_element_type=jnp.float32,
    )
    norm_vecs = norm_pieces
    bias_qkv = piece_bqkv.astype(jnp.float32).reshape(piece_count * cols_qkv)
    bias_up = piece_bup.astype(jnp.float32).reshape(piece_count * cols_up)
    joined, hidden, first_in, second_in, norm_vecs, bias_qkv, bias_up = (
        joined,
        hidden,
        low_one,
        low_two,
        norm_vecs,
        bias_qkv,
        bias_up,
    )
    joined = joined + bias_qkv
    hidden = hidden + bias_up
    cosine, sine = rotary_tables(query_pos.astype(jnp.float32))
    split_heads = joined.reshape(tok_rows, 3, HEADS, HEAD)
    query_heads = rotate(split_heads[:, 0], cosine, sine).astype(jnp.bfloat16)
    key_low = (
        rotate(split_heads[:, 1], cosine, sine).astype(jnp.bfloat16).reshape(tok_rows, model_width)
    )
    value_low = split_heads[:, 2].astype(jnp.bfloat16).reshape(tok_rows, model_width)
    seg_low = segments[0].astype(jnp.bfloat16)

    def block_scores(key_blk, seg_blk, key_start):
        piece_rows = key_blk.shape[0]
        key_heads = key_blk.reshape(piece_rows, HEADS, HEAD)
        scores = (
            jnp.einsum("qhd,khd->hqk", query_heads, key_heads, preferred_element_type=jnp.float32)
            * score_scale
        )
        key_pos = key_start + jnp.arange(piece_rows, dtype=jnp.int32)
        allowed = (seg_blk[None, :] == seg_low[:, None]) & (key_pos[None, :] <= query_pos[:, None])
        return (key_heads, jnp.where(allowed[None], scores, -1e30), allowed[None])

    def forward_update(carried, pieces, key_start):
        acc_out, run_max, run_sum = carried
        key_blk, value_blk, seg_blk = pieces
        value_heads = value_blk.reshape(value_blk.shape[0], HEADS, HEAD)
        key_heads, masked, allowed = block_scores(key_blk, seg_blk, key_start)
        new_max = jnp.maximum(run_max, jnp.max(masked, axis=-1))
        weights = jnp.where(allowed, jnp.exp(masked - new_max[..., None]), 0.0)
        factor = jnp.exp(run_max - new_max)
        run_sum = run_sum * factor + jnp.sum(weights, axis=-1)
        acc_out = acc_out * jnp.transpose(factor)[:, :, None] + jnp.einsum(
            "hqk,khd->qhd",
            weights.astype(jnp.bfloat16),
            value_heads,
            preferred_element_type=jnp.float32,
        )
        return (acc_out, new_max, run_sum)

    def guarded(update, carried, pieces):
        result = over_blocks(update, carried, pieces)
        return result

    start_attend = (
        jnp.zeros((tok_rows, HEADS, HEAD), jnp.float32),
        jnp.full((HEADS, tok_rows), -1e30, jnp.float32),
        jnp.zeros((HEADS, tok_rows), jnp.float32),
    )
    acc_out, run_max, run_sum = guarded(
        forward_update,
        start_attend,
        (
            lax.all_gather(key_low, "sp", axis=0, tiled=True),
            lax.all_gather(value_low, "sp", axis=0, tiled=True),
            lax.all_gather(seg_low, "sp", axis=0, tiled=True),
        ),
    )
    context = acc_out / jnp.transpose(run_sum)[:, :, None]
    log_sum = run_max + jnp.log(run_sum)
    context_low = context.reshape(tok_rows, model_width).astype(jnp.bfloat16)
    active = jax.nn.gelu(hidden, approximate=False).astype(jnp.bfloat16)
    piece_out = lax.all_gather(w_attn_out[None], ("dp", "sp"), axis=0, tiled=True)
    piece_down = lax.all_gather(w_down[None], ("dp", "sp"), axis=0, tiled=True)
    piece_bout = lax.all_gather(b_attn_out[None], ("dp", "sp"), axis=0, tiled=True)
    piece_bdown = lax.all_gather(b_down[None], ("dp", "sp"), axis=0, tiled=True)
    piece_count = piece_out.shape[0]
    ctx_cols = context_low
    act_cols = active
    summed = jnp.dot(
        ctx_cols,
        piece_out.reshape(piece_count * rows_model, model_width),
        preferred_element_type=jnp.float32,
    )
    summed = summed + jnp.dot(
        act_cols,
        piece_down.reshape(piece_count * rows_hidden, model_width),
        preferred_element_type=jnp.float32,
    )
    both_bias = (piece_bout.astype(jnp.float32) + piece_bdown.astype(jnp.float32)).reshape(
        piece_count * rows_model
    )
    bias_out = both_bias
    summed, bias_out = (summed, bias_out)
    block_output = (inputs + summed + bias_out)[None]
    out_low = out_grad[0]
    out_float = out_low.astype(jnp.float32)
    pieces = (
        lax.all_gather(w_attn_out[None], ("dp", "sp"), axis=0, tiled=True),
        lax.all_gather(w_down[None], ("dp", "sp"), axis=0, tiled=True),
    )
    piece_out = pieces[0]
    piece_down = pieces[1]
    piece_count = piece_out.shape[0]
    part_ctx = jnp.einsum(
        "tc,rc->tr",
        out_low,
        piece_out.reshape(piece_count * rows_model, model_width),
        preferred_element_type=jnp.float32,
    )
    part_act = jnp.einsum(
        "tc,rc->tr",
        out_low,
        piece_down.reshape(piece_count * rows_hidden, model_width),
        preferred_element_type=jnp.float32,
    )
    d_context = part_ctx
    d_active = part_act
    d_context, d_active = (d_context, d_active)
    d_context_low = d_context.astype(jnp.bfloat16)
    dctx_heads = d_context_low.reshape(tok_rows, HEADS, HEAD)
    unused_value, gelu_pull = jax.vjp(lambda values: jax.nn.gelu(values, approximate=False), hidden)
    d_hidden = gelu_pull(d_active)[0].astype(jnp.bfloat16)
    row_delta = jnp.transpose(jnp.sum(dctx_heads.astype(jnp.float32) * context, axis=-1))

    def backward_update(carried, pieces, key_start):
        d_query, key_all, value_all = carried
        key_blk, value_blk, seg_blk = pieces
        piece_rows = key_blk.shape[0]
        value_heads = value_blk.reshape(piece_rows, HEADS, HEAD)
        key_heads, masked, allowed = block_scores(key_blk, seg_blk, key_start)
        probabilities = jnp.where(allowed, jnp.exp(masked - log_sum[..., None]), 0.0)
        d_probs = jnp.einsum(
            "qhd,khd->hqk", dctx_heads, value_heads, preferred_element_type=jnp.float32
        )
        d_scores = (probabilities * (d_probs - row_delta[..., None])).astype(jnp.bfloat16)
        d_query = (
            d_query
            + jnp.einsum("hqk,khd->qhd", d_scores, key_heads, preferred_element_type=jnp.float32)
            * score_scale
        )
        key_part = (
            jnp.einsum("hqk,qhd->khd", d_scores, query_heads, preferred_element_type=jnp.float32)
            * score_scale
        )
        value_part = jnp.einsum(
            "hqk,qhd->khd",
            probabilities.astype(jnp.bfloat16),
            dctx_heads,
            preferred_element_type=jnp.float32,
        )
        key_all = lax.dynamic_update_slice_in_dim(
            key_all, key_part.reshape(piece_rows, model_width), key_start, 0
        )
        value_all = lax.dynamic_update_slice_in_dim(
            value_all, value_part.reshape(piece_rows, model_width), key_start, 0
        )
        return (d_query, key_all, value_all)

    start_back = (
        jnp.zeros((tok_rows, HEADS, HEAD), jnp.float32),
        jnp.zeros((seq_length, model_width), jnp.float32),
        jnp.zeros((seq_length, model_width), jnp.float32),
    )
    d_query, key_all, value_all = guarded(
        backward_update,
        start_back,
        (
            lax.all_gather(key_low, "sp", axis=0, tiled=True),
            lax.all_gather(value_low, "sp", axis=0, tiled=True),
            lax.all_gather(seg_low, "sp", axis=0, tiled=True),
        ),
    )
    d_key, d_value = (
        lax.psum_scatter(
            key_all.astype(jnp.bfloat16), "sp", scatter_dimension=0, tiled=True
        ).astype(jnp.float32),
        lax.psum_scatter(
            value_all.astype(jnp.bfloat16), "sp", scatter_dimension=0, tiled=True
        ).astype(jnp.float32),
    )
    unused_rot, rotate_pull = jax.vjp(lambda values: rotate(values, cosine, sine), d_query)
    query_back = rotate_pull(d_query)[0]
    key_back = rotate_pull(d_key.reshape(tok_rows, HEADS, HEAD))[0]
    d_joined = (
        jnp.stack([query_back, key_back, d_value.reshape(tok_rows, HEADS, HEAD)], axis=1)
        .reshape(tok_rows, joined_width)
        .astype(jnp.bfloat16)
    )
    pieces = (
        lax.all_gather(w_qkv[None], ("dp", "sp"), axis=0, tiled=True),
        lax.all_gather(w_up[None], ("dp", "sp"), axis=0, tiled=True),
    )
    piece_qkv = pieces[0]
    piece_up = pieces[1]
    piece_count = piece_qkv.shape[0]
    part_one = jnp.einsum(
        "tc,rc->tr",
        d_joined,
        piece_qkv.reshape(piece_count * rows_model, joined_width),
        preferred_element_type=jnp.float32,
    )
    part_two = jnp.einsum(
        "tc,rc->tr",
        d_hidden,
        piece_up.reshape(piece_count * rows_model, hidden_width),
        preferred_element_type=jnp.float32,
    )
    d_first = part_one
    d_second = part_two
    d_first, d_second = (d_first, d_second)
    unused_norm, norm_pull = jax.vjp(
        both_norms, inputs, norm_vecs[0], norm_vecs[1], norm_vecs[2], norm_vecs[3]
    )
    d_inputs, d_gain_one, d_shift_one, d_gain_two, d_shift_two = norm_pull((d_first, d_second))
    input_grad = (out_float + d_inputs)[None]
    sum_qkv = jnp.sum(d_joined.astype(jnp.float32), axis=0)
    sum_up = jnp.sum(d_hidden.astype(jnp.float32), axis=0)
    sum_out = jnp.sum(out_float, axis=0)
    grad_g1, grad_s1, grad_g2, grad_s2, grad_bqkv, grad_bout, grad_bup = (
        lax.psum_scatter(d_gain_one, ("dp", "sp"), scatter_dimension=0, tiled=True),
        lax.psum_scatter(d_shift_one, ("dp", "sp"), scatter_dimension=0, tiled=True),
        lax.psum_scatter(d_gain_two, ("dp", "sp"), scatter_dimension=0, tiled=True),
        lax.psum_scatter(d_shift_two, ("dp", "sp"), scatter_dimension=0, tiled=True),
        lax.psum_scatter(sum_qkv, ("dp", "sp"), scatter_dimension=0, tiled=True),
        lax.psum_scatter(sum_out, ("dp", "sp"), scatter_dimension=0, tiled=True),
        lax.psum_scatter(sum_up, ("dp", "sp"), scatter_dimension=0, tiled=True),
    )
    term_qkv = jnp.einsum("tr,tc->rc", first_in, d_joined, preferred_element_type=jnp.float32)
    term_up = jnp.einsum("tr,tc->rc", second_in, d_hidden, preferred_element_type=jnp.float32)
    in_grads = lax.psum_scatter(
        jnp.concatenate([term_qkv, term_up], axis=1), ("dp", "sp"), scatter_dimension=0, tiled=True
    )
    block_rows = rows_model + rows_hidden
    number = lax.axis_size(("dp", "sp")) * block_rows // block_rows
    ctx_cols = context_low.reshape(tok_rows, number, rows_model)
    act_cols = active.reshape(tok_rows, number, rows_hidden)
    term_ctx = jnp.einsum("tnr,tc->nrc", ctx_cols, out_low, preferred_element_type=jnp.float32)
    term_act = jnp.einsum("tnr,tc->nrc", act_cols, out_low, preferred_element_type=jnp.float32)
    out_grads = lax.psum_scatter(
        jnp.concatenate([term_ctx, term_act], axis=1).reshape(number * block_rows, model_width),
        ("dp", "sp"),
        scatter_dimension=0,
        tiled=True,
    )
    return (
        block_output,
        input_grad,
        grad_g1,
        grad_s1,
        in_grads[:, :joined_width],
        grad_bqkv,
        out_grads[:rows_model],
        grad_bout,
        grad_g2,
        grad_s2,
        in_grads[:, joined_width:],
        grad_bup,
        out_grads[rows_model:],
        grad_bout,
    )


def solution(mesh):
    return jax.shard_map(
        shards,
        mesh=mesh,
        in_specs=(
            P("dp", "sp", None),
            P("dp", "sp"),
            P("dp", "sp", None),
            P(("dp", "sp")),
            P(("dp", "sp")),
            P(("dp", "sp"), None),
            P(("dp", "sp")),
            P(("dp", "sp"), None),
            P(("dp", "sp")),
            P(("dp", "sp")),
            P(("dp", "sp")),
            P(("dp", "sp"), None),
            P(("dp", "sp")),
            P(("dp", "sp"), None),
            P(("dp", "sp")),
        ),
        out_specs=(
            P("dp", "sp", None),
            P("dp", "sp", None),
            P(("dp", "sp")),
            P(("dp", "sp")),
            P(("dp", "sp"), None),
            P(("dp", "sp")),
            P(("dp", "sp"), None),
            P(("dp", "sp")),
            P(("dp", "sp")),
            P(("dp", "sp")),
            P(("dp", "sp"), None),
            P(("dp", "sp")),
            P(("dp", "sp"), None),
            P(("dp", "sp")),
        ),
        check_vma=False,
    )
```

profile of v0, /device:TPU:0, one launch (start us, length us, event | category | flops | bytes accessed | tf_op | source)
XLA Modules:
  0.0 3653.9 jit_solution(17355609263224084046)
XLA Ops:
  14.7 44.1 %all-reduce.24 = (bf16[6144]{0:T(1024)(128)(2,1)S(1)}, bf16[2048]{0:T(1024)(128)(2,1)S(1)}, bf16[2048]{0:T(1024)(128)(2,1)S(1)}, bf16[2048]{0:T(1024)(128)(2,1)S...) all-reduce(bf16[6144]{0:T(1024)(128)(2,1)S(1)} %dynamic-update-slic, ...), channel_id=8, replica_groups=mesh['dp'=4,'sp'=8] {'dp','sp'}, use_global_device_ids=true, to_apply=%add.12 | all-reduce | flops 18432 | bytes 73728
  61.8 108.1 %all-gather.25.cloned.1.call-done = bf16[2048,6144]{1,0:T(8,128)(2,1)} async-done(((bf16[64,6144]{1,0:T(8,128)(2,1)}), bf16[2048,6144]{1,0:T(8,128)(2,1)}) %all-gather.25.cloned.1.call-update) | async-done | bytes 25165840 | tf_op jit(solution)/shard_map/all_gather | solution.py:86
  169.9 10.3 convolution_add_fusion.1
  198.3 50.2 %all-gather.27.cloned.1.call-done = bf16[2048,2048]{1,0:T(8,128)(2,1)} async-done(((bf16[64,2048]{1,0:T(8,128)(2,1)}), bf16[2048,2048]{1,0:T(8,128)(2,1)}) %all-gather.27.cloned.1.call-update) | async-done | bytes 8388624 | tf_op jit(solution)/shard_map/all_gather | solution.py:185
  255.4 41.1 %all-gather.23.cloned.1.call-done = bf16[1024,2048]{1,0:T(8,128)(2,1)} async-done(((bf16[128,2048]{1,0:T(8,128)(2,1)}), bf16[1024,2048]{1,0:T(8,128)(2,1)}) %all-gather.23.cloned.1.call-update) | async-done | bytes 4194320 | tf_op jit(solution)/shard_map/all_gather | solution.py:177
  302.9 41.5 %all-gather.21.cloned.1.call-done = bf16[1024,2048]{1,0:T(8,128)(2,1)} async-done(((bf16[128,2048]{1,0:T(8,128)(2,1)}), bf16[1024,2048]{1,0:T(8,128)(2,1)}) %all-gather.21.cloned.1.call-update) | async-done | bytes 4194320 | tf_op jit(solution)/shard_map/all_gather | solution.py:176
  350.7 14.5 while.30
  372.4 29.2 while.31
  416.3 40.8 %all-gather.13 = bf16[32,1,256]{2,1,0:T(2,128)(2,1)S(1)} all-gather(bf16[1,1,256]{2,1,0:T(2,128)(2,1)S(1)} %reshape.512), channel_id=11, replica_groups=mesh['dp'=4,'sp'=8] {'dp','sp'}, dimensions={0}, use_global_device_ids=true | all-gather | bytes 16896 | tf_op jit(solution)/shard_map/all_gather | solution.py:93
  459.8 47.8 %reduce-scatter.12.cloned.1.call-done = bf16[128,2048]{1,0:T(8,128)(2,1)} async-done(((bf16[1024,2048]{1,0:T(8,128)(2,1)}), bf16[128,2048]{1,0:T(8,128)(2,1)}) %reduce-scatter.12.cloned.1.call-update) | async-done | bytes 524304
  513.2 20.6 fusion.93
  533.8 169.7 %all-gather.29.cloned.1.call-done = bf16[2048,8192]{1,0:T(8,128)(2,1)} async-done(((bf16[64,8192]{1,0:T(8,128)(2,1)}), bf16[2048,8192]{1,0:T(8,128)(2,1)}) %all-gather.29.cloned.1.call-update) | async-done | bytes 33554448 | tf_op jit(solution)/shard_map/all_gather | solution.py:87
  703.5 21.8 multiply_convert_fusion
  725.3 174.2 %all-gather.31.cloned.1.call-done = bf16[8192,2048]{1,0:T(8,128)(2,1)} async-done(((bf16[256,2048]{1,0:T(8,128)(2,1)}), bf16[8192,2048]{1,0:T(8,128)(2,1)}) %all-gather.31.cloned.1.call-update) | async-done | bytes 33554448 | tf_op jit(solution)/shard_map/all_gather | solution.py:186
  899.5 26.7 convert_reduce_fusion
  926.2 24.9 fusion.66
  951.1 15.9 fusion.105
  967.0 15.5 fusion.99
  989.1 76.0 %pad_maximum_fusion = f32[2048,14336]{1,0:T(8,128)} fusion(f32[2048,8192]{1,0:T(8,128)} %fusion.66, f32[2048,6144]{1,0:T(8,128)} %fusion.93), kind=kLoop, calls=%fused_computation.49 | loop fusion | flops 29360128 | bytes 234881024 | tf_op jit(solution)/shard_map/concatenate | solution.py:344
  1077.1 24.8 fusion.68
  1101.9 56.4 %pad_maximum_fusion.1 = f32[32,320,2048]{2,1,0:T(8,128)} fusion(f32[32,256,2048]{2,1,0:T(8,128)} %fusion.68, f32[32,64,2048]{2,1,0:T(8,128)} %fusion.70), kind=kLoop, calls=%fused_computation.50 | loop fusion | flops 20971520 | bytes 167772160 | tf_op jit(solution)/shard_map/concatenate | solution.py:353
  1163.8 15.9 fusion.35
  1188.1 1568.4 %all-reduce.28.cloned.1.call-done = f32[2048,14336]{1,0:T(8,128)} async-done(((f32[2048,14336]{1,0:T(8,128)}), f32[2048,14336]{1,0:T(8,128)}) %all-reduce.28.cloned.1.call-update) | async-done | bytes 117440528
  2762.7 878.7 %reduce-scatter.8.cloned.1.call-done = f32[320,2048]{1,0:T(8,128)} async-done(((f32[10240,2048]{1,0:T(8,128)}), f32[320,2048]{1,0:T(8,128)}) %reduce-scatter.8.cloned.1.call-update) | async-done | bytes 2621456 | tf_op jit(solution)/shard_map/reduce_scatter | solution.py:352
  (238 shorter events, 162.7 us)
Async XLA Ops:
  7.2 162.7 %all-gather.25.cloned.1.call-start = ((), (), s32[]{:S(2)}) async-start(), calls=%async_computation.6 | async-start | bytes 25952256 | tf_op jit(solution)/shard_map/all_gather | solution.py:86
  7.9 240.6 %all-gather.27.cloned.1.call-start = ((), (), s32[]{:S(2)}) async-start(), calls=%async_computation.7 | async-start | bytes 8650752 | tf_op jit(solution)/shard_map/all_gather | solution.py:185
  8.7 287.8 %all-gather.23.cloned.1.call-start = ((), (), s32[]{:S(2)}) async-start(), calls=%async_computation.4 | async-start | bytes 4718592 | tf_op jit(solution)/shard_map/all_gather | solution.py:177
  61.8 118.4 %copy-start.18 = (f32[128]{0:T(128)}, f32[128]{0:T(128)S(1)}, u32[]{:S(2)}) copy-start(f32[128]{0:T(128)S(1)} %fusion.51) | copy-start | bytes 1540
  182.2 162.2 %all-gather.21.cloned.1.call-start = ((), (), s32[]{:S(2)}) async-start(), calls=%async_computation.3 | async-start | bytes 4718592 | tf_op jit(solution)/shard_map/all_gather | solution.py:176
  185.5 3.0 copy-start.20
  185.5 63.0 %copy-start.9 = (bf16[1,128,2048]{2,1,0:T(8,128)(2,1)S(1)}, bf16[1,128,2048]{2,1,0:T(8,128)(2,1)}, u32[]{:S(2)}) copy-start(bf16[1,128,2048]{2,1,0:T(8,128)(2,1)} %param.21) | copy-start | bytes 1572868
  188.4 269.0 %reduce-scatter.10.cloned.1.call-start = ((), (), s32[]{:S(2)}) async-start(), calls=%async_computation.10 | async-start | bytes 4718592
  379.6 3.5 copy-start.5
  383.7 3.3 copy-start.6
  394.2 3.5 copy-start.5
  398.3 3.3 copy-start.6
  408.1 99.5 %reduce-scatter.12.cloned.1.call-start = ((), (), s32[]{:S(2)}) async-start(), calls=%async_computation.11 | async-start | bytes 4718592
  414.7 288.8 %all-gather.29.cloned.1.call-start = ((), (), s32[]{:S(2)}) async-start(), calls=%async_computation.8 | async-start | bytes 34603008 | tf_op jit(solution)/shard_map/all_gather | solution.py:87
  415.5 484.0 %all-gather.31.cloned.1.call-start = ((), (), s32[]{:S(2)}) async-start(), calls=%async_computation.9 | async-start | bytes 34603008 | tf_op jit(solution)/shard_map/all_gather | solution.py:186
  416.2 763.4 %all-reduce.30.cloned.1.call-start = ((), (), s32[]{:S(2)}) async-start(), calls=%async_computation.13 | async-start | bytes 196608
  703.5 196.0 %copy-start.10 = (bf16[1,128,2048]{2,1,0:T(8,128)(2,1)S(1)}, bf16[1,128,2048]{2,1,0:T(8,128)(2,1)}, u32[]{:S(2)}) copy-start(bf16[1,128,2048]{2,1,0:T(8,128)(2,1)} %param.21) | copy-start | bytes 1572868
  926.2 24.9 copy-start.7
  967.0 15.6 copy-start.19
  989.1 1767.4 %all-reduce.28.cloned.1.call-start = ((), (), s32[]{:S(2)}) async-start(), calls=%async_computation.12 | async-start | bytes 234881024
  1065.2 2576.2 %reduce-scatter.8.cloned.1.call-start = ((), (), s32[]{:S(2)}) async-start(), calls=%async_computation.5 | async-start | bytes 86507520 | tf_op jit(solution)/shard_map/reduce_scatter | solution.py:352
  1066.4 8.1 copy-start.8
  1159.0 4.8 copy-start.2
  1181.7 2464.7 %copy-start.22 = (f32[64]{0:T(128)}, f32[64]{0:T(128)S(1)}, u32[]{:S(2)}) copy-start(f32[64]{0:T(128)S(1)} %dynamic-slice.4) | copy-start | bytes 772
  (17 other events, 28.5 us)
Sparse Core Ops, SparseCore 0:
  11.0 158.8 all-gather.24
  172.9 75.5 all-gather.26
  250.7 45.7 all-gather.22
  298.5 45.8 all-gather.20
  408.2 49.0 reduce-scatter.9
  459.4 48.1 reduce-scatter.11
  510.6 192.8 all-gather.28
  706.5 192.9 all-gather.30
  989.2 122.1 all-reduce.29
  1118.8 1637.6 all-reduce.27
  2758.9 882.4 reduce-scatter.7
where the time goes:
time: 3660 us; the launch traced here: 3650 us
  waiting for transfers between devices  3080 us (84%)
  matrix products  208 us (6%)
  other arithmetic  150 us (4%)
  local copies, waits for them, and re-layouts  100 us (3%)
  blocking collectives  94.7 us (3%)
    unnamed x15, waiting for transfers between devices  1620 us
    reduce_scatter x1, waiting for transfers between devices, shards(): lax.psum_scatter(jnp.concatenate([term_ctx, term_act], axis=1).reshape(nu...  879 us
    all_gather x1, waiting for transfers between devices, shards(): piece_down = lax.all_gather(w_down[None], ('dp', 'sp'), axis=0, tiled=True)  174 us
    all_gather x1, waiting for transfers between devices, shards(): piece_up = lax.all_gather(w_up[None], ('dp', 'sp'), axis=0, tiled=True)  170 us
    all_gather x1, waiting for transfers between devices, shards(): piece_qkv = lax.all_gather(w_qkv[None], ('dp', 'sp'), axis=0, tiled=True)  108 us
    concatenate x1, other arithmetic, shards(): jnp.concatenate([term_qkv, term_up], axis=1)  76 us
  transfers between devices with their start and end apart: 11, of which 9 were waited for; matrix products, arithmetic and copies ran while one was open for 8% of the time, Pallas kernels for 0%

commit v1 on v0

v1 whole, which is shorter than its diff:
```python
import math

import jax
import jax.numpy as jnp
from jax import lax
from jax.sharding import PartitionSpec as P

HEADS = 8
HEAD = 256
ROT = 64
BF16 = jnp.bfloat16
F32 = jnp.float32


def normalize(values):
    center = values - jnp.mean(values, axis=-1, keepdims=True)
    spread = jnp.mean(center * center, axis=-1, keepdims=True)
    scale = lax.rsqrt(spread + 1e-05)
    return center * scale, scale


def rotary_tables(positions):
    inverse_freq = 10000.0 ** (-jnp.arange(0, ROT, 2).astype(F32) / ROT)
    angles = positions[:, None] * inverse_freq[None, :]
    angles = jnp.concatenate([angles, angles], axis=1)
    return (jnp.cos(angles), jnp.sin(angles))


def rotate(values, cosine, sine):
    half_rot = ROT // 2
    rot_part = values[..., :ROT]
    turned = jnp.concatenate([-rot_part[..., half_rot:], rot_part[..., :half_rot]], axis=-1)
    rotated = rot_part * cosine + turned * sine
    return jnp.concatenate([rotated, values[..., ROT:]], axis=-1)


def pick(array, index, axis=0):
    return lax.dynamic_index_in_dim(array, index, axis, keepdims=False)


def put(array, piece, index):
    return lax.dynamic_update_slice_in_dim(array, piece[None], index, 0)


def swap(extent, mask):
    return [(i, i ^ mask) for i in range(extent)]


class LineGrid:
    def __init__(self):
        self.dp = lax.axis_index("dp")
        self.sp = lax.axis_index("sp")
        self.line = self.sp // 2
        self.core = self.sp % 2
        self.part = 0

    def gather_dp(self, block):
        half = block.shape[0] // 2
        along_x = lax.ppermute(block, "dp", swap(4, 1))
        along_y = lax.ppermute(block, "dp", swap(4, 2))
        far_one = lax.ppermute(along_y[:half], "dp", swap(4, 1))
        far_two = lax.ppermute(along_x[half:], "dp", swap(4, 2))
        far = jnp.concatenate([far_one, far_two], axis=0)
        out = jnp.zeros((4,) + block.shape, block.dtype)
        for mask, piece in enumerate((block, along_x, along_y, far)):
            out = put(out, piece, self.dp ^ mask)
        return out

    def reduce_dp(self, terms):
        half = terms.shape[1] // 2
        own, to_x, to_y, to_far = (pick(terms, self.dp ^ mask) for mask in range(4))
        far_x = lax.ppermute(to_far[:half], "dp", swap(4, 1))
        far_y = lax.ppermute(to_far[half:], "dp", swap(4, 2))
        top_x = lax.ppermute(to_x[:half], "dp", swap(4, 1))
        low_y = lax.ppermute(to_y[half:], "dp", swap(4, 2))
        top_y = lax.ppermute(
            (to_y[:half].astype(F32) + far_x.astype(F32)).astype(BF16), "dp", swap(4, 2)
        )
        low_x = lax.ppermute(
            (to_x[half:].astype(F32) + far_y.astype(F32)).astype(BF16), "dp", swap(4, 1)
        )
        others = jnp.concatenate(
            [top_x.astype(F32) + top_y.astype(F32), low_x.astype(F32) + low_y.astype(F32)], axis=0
        )
        return own.astype(F32) + others

    def gather_sp(self, block):
        right = [(i, i + 2) for i in range(6)]
        left = [(i + 2, i) for i in range(6)]
        from_left, from_right = [block], [block]
        for step in range(3):
            from_left.append(lax.ppermute(from_left[-1], "sp", right[2 * step :]))
            from_right.append(lax.ppermute(from_right[-1], "sp", left[: 6 - 2 * step]))
        mine = put(jnp.zeros((4,) + block.shape, block.dtype), block, self.line)
        for step in range(1, 4):
            piece = jnp.where(self.line >= step, from_left[step], from_right[4 - step])
            mine = put(mine, piece, (self.line - step) % 4)
        other = lax.ppermute(mine, "sp", swap(8, 1))
        pair = jnp.stack(
            [jnp.where(self.core == 0, mine, other), jnp.where(self.core == 0, other, mine)], axis=1
        )
        return pair.reshape((8 * block.shape[0],) + block.shape[1:])

    def reduce_sp(self, terms):
        rows = terms.shape[0] // 8
        pairs = terms.reshape((4, 2, rows) + terms.shape[1:])
        other = lax.ppermute(pick(pairs, 1 - self.core, 1), "sp", swap(8, 1))
        mine = (pick(pairs, self.core, 1).astype(F32) + other.astype(F32)).astype(BF16)
        right = [(i, i + 2) for i in range(6)]
        left = [(i + 2, i) for i in range(6)]
        going_right = going_left = None
        for step in range(1, 4):
            for_right = pick(mine, jnp.minimum(self.line + 4 - step, 3))
            for_left = pick(mine, jnp.maximum(self.line - 4 + step, 0))
            if step > 1:
                for_right = (for_right.astype(F32) + going_right.astype(F32)).astype(BF16)
                for_left = (for_left.astype(F32) + going_left.astype(F32)).astype(BF16)
            going_right = lax.ppermute(for_right, "sp", right[: 2 * step])
            going_left = lax.ppermute(for_left, "sp", left[6 - 2 * step :])
        return pick(mine, self.line).astype(F32) + going_right.astype(F32) + going_left.astype(F32)

    def exchange_sp(self, blocks):
        pairs = blocks.reshape((4, 2) + blocks.shape[1:])
        keep = pick(pairs, self.core, 1)
        other = lax.ppermute(pick(pairs, 1 - self.core, 1), "sp", swap(8, 1))
        out = jnp.stack(
            [jnp.where(self.core == 0, keep, other), jnp.where(self.core == 0, other, keep)], axis=1
        )
        moved = [
            lax.ppermute(pick(out, self.line ^ step), "sp", swap(8, 2 * step))
            for step in range(1, 4)
        ]
        for step in range(1, 4):
            out = put(out, moved[step - 1], self.line ^ step)
        return out.reshape(blocks.shape)

    def exchange_four(self, blocks):
        place = self.sp % 4
        moved = [
            lax.ppermute(pick(blocks, place ^ step), "sp", swap(8, step)) for step in range(1, 4)
        ]
        for step in range(1, 4):
            blocks = put(blocks, moved[step - 1], place ^ step)
        return blocks

    def gather_small(self, vector):
        out = jnp.zeros((8, 4) + vector.shape, vector.dtype)
        other = lax.ppermute(vector, "sp", swap(8, 1))
        pair = jnp.stack(
            [jnp.where(self.core == 0, vector, other), jnp.where(self.core == 0, other, vector)]
        )
        out = put(jnp.zeros((4,) + pair.shape, pair.dtype), pair, self.line)
        for step in range(1, 4):
            out = put(out, lax.ppermute(pair, "sp", swap(8, 2 * step)), self.line ^ step)
        whole = put(jnp.zeros((4,) + out.shape, out.dtype), out, self.dp)
        for step in range(1, 4):
            whole = put(whole, lax.ppermute(out, "dp", swap(4, step)), self.dp ^ step)
        return whole.reshape((32,) + vector.shape)

    def reduce_small(self, terms):
        blocks = terms.reshape((4, 8) + terms.shape[1:])
        total = pick(blocks, self.dp)
        for step in range(1, 4):
            total = total + lax.ppermute(pick(blocks, self.dp ^ step), "dp", swap(4, step))
        pairs = total.reshape((4, 2) + terms.shape[1:])
        pair = pick(pairs, self.core, 1) + lax.ppermute(
            pick(pairs, 1 - self.core, 1), "sp", swap(8, 1)
        )
        total = pick(pair, self.line)
        for step in range(1, 4):
            total = total + lax.ppermute(pick(pair, self.line ^ step), "sp", swap(8, 2 * step))
        return total

    def gather_out(self, block):
        return self.exchange_four(self.gather_dp(block)).reshape(HEAD, block.shape[1])

    def reduce_out(self, terms):
        return self.reduce_dp(self.exchange_four(terms.reshape(4, HEAD // 4, terms.shape[1])))

    def whole_keys(self, block):
        return block

    def reduce_keys(self, terms):
        return terms


class AnyGrid:
    def __init__(self):
        self.dp = lax.axis_index("dp")
        self.sp = lax.axis_index("sp")
        self.dps = lax.axis_size("dp")
        self.sps = lax.axis_size("sp")
        self.parts = self.sps // HEADS
        self.part = self.sp // HEADS
        self.team = [
            [part * HEADS + rank for rank in range(HEADS)] for part in range(self.parts)
        ]
        self.peers = [
            [part * HEADS + rank for part in range(self.parts)] for rank in range(HEADS)
        ]

    def gather_dp(self, block):
        block = lax.all_gather(block, "sp", axis=0, axis_index_groups=self.peers)
        block = lax.all_gather(block, "dp", axis=0)
        return block.reshape((self.dps * self.parts,) + block.shape[2:])

    def reduce_dp(self, terms):
        block = terms.reshape((self.dps, self.parts) + terms.shape[1:])
        block = lax.psum_scatter(block, "dp", scatter_dimension=0)
        return lax.psum_scatter(
            block, "sp", scatter_dimension=0, axis_index_groups=self.peers
        ).astype(F32)

    def gather_sp(self, block):
        return lax.all_gather(block, "sp", axis=0, tiled=True, axis_index_groups=self.team)

    def reduce_sp(self, terms):
        return lax.psum_scatter(
            terms, "sp", scatter_dimension=0, tiled=True, axis_index_groups=self.team
        ).astype(F32)

    def exchange_sp(self, blocks):
        return lax.all_to_all(
            blocks, "sp", split_axis=0, concat_axis=0, tiled=True, axis_index_groups=self.team
        )

    def gather_small(self, vector):
        return lax.all_gather(vector, ("dp", "sp"), axis=0)

    def reduce_small(self, terms):
        return lax.psum_scatter(terms, ("dp", "sp"), scatter_dimension=0)

    def gather_out(self, block):
        whole = lax.all_gather(block, ("dp", "sp"), axis=0, tiled=True)
        return lax.dynamic_slice_in_dim(whole, head_of(self.sp % HEADS) * HEAD, HEAD, 0)

    def reduce_out(self, terms):
        whole = jnp.zeros((HEADS * HEAD, terms.shape[1]), terms.dtype)
        whole = lax.dynamic_update_slice_in_dim(whole, terms, head_of(self.sp % HEADS) * HEAD, 0)
        return lax.psum_scatter(
            whole, ("dp", "sp"), scatter_dimension=0, tiled=True
        ).astype(F32)

    def whole_keys(self, block):
        return lax.all_gather(block, "sp", axis=0, tiled=True, axis_index_groups=self.peers)

    def reduce_keys(self, terms):
        return lax.psum_scatter(
            terms, "sp", scatter_dimension=0, tiled=True, axis_index_groups=self.peers
        )


def head_of(rank):
    return 2 * (rank % 4) + rank // 4


HEAD_ORDER = [2 * (rank % 4) + rank // 4 for rank in range(HEADS)]
RANK_ORDER = [HEAD_ORDER.index(head) for head in range(HEADS)]


def dot(left, right, contract):
    return lax.dot_general(
        left, right, (((contract[0],), (contract[1],)), ((), ())), preferred_element_type=F32
    )


def shards(
    block_input,
    segments,
    out_grad,
    ln1_gain,
    ln1_bias,
    w_qkv,
    b_qkv,
    w_attn_out,
    b_attn_out,
    ln2_gain,
    ln2_bias,
    w_up,
    b_up,
    w_down,
    b_down,
):
    dps, sps = lax.axis_size("dp"), lax.axis_size("sp")
    devices = dps * sps
    grid = LineGrid() if (dps, sps) == (4, 8) else AnyGrid()
    groups = devices // HEADS
    x_own = block_input[0]
    g_own = out_grad[0]
    tokens, width = x_own.shape
    rows = w_qkv.shape[0]
    cols_up = b_up.shape[0]
    cols_qkv = b_qkv.shape[0]
    length = tokens * HEADS
    scale = 1.0 / math.sqrt(HEAD)

    packed = jnp.concatenate(
        [
            ln1_gain,
            ln1_bias,
            ln2_gain,
            ln2_bias,
            b_attn_out,
            b_down,
            b_qkv,
            b_up,
            segments[0].astype(BF16),
        ]
    )
    small = grid.gather_small(packed)
    vectors = [
        small[:, k * rows : (k + 1) * rows].reshape(width).astype(F32) for k in range(6)
    ]
    gain_one, shift_one, gain_two, shift_two, bias_out, bias_down = vectors
    at = 6 * rows
    rank = grid.sp % HEADS
    bias_qkv = small[:, at : at + cols_qkv].reshape(3, HEADS, HEAD)
    bias_qkv = pick(bias_qkv, head_of(rank), 1).astype(F32).reshape(3 * HEAD)
    at += cols_qkv
    bias_up = small[:, at : at + cols_up].reshape(groups, HEADS, cols_up)
    bias_up = pick(bias_up, rank, 1).astype(F32).reshape(groups * cols_up)
    at += cols_up
    seg_all = pick(small[:, at:].reshape(dps, sps * tokens), grid.dp)
    seg_mine = lax.dynamic_slice_in_dim(seg_all, grid.part * length, length, 0)

    x_all = grid.gather_sp(x_own)
    up_blocks = w_up.reshape(rows, groups, HEADS, cols_up).transpose(2, 0, 1, 3)
    up_blocks = up_blocks.reshape(HEADS, rows, groups * cols_up)
    up_rows = grid.exchange_sp(up_blocks).reshape(HEADS * rows, groups * cols_up)
    weight_down = grid.gather_dp(w_down).reshape(groups * cols_up, width)
    weight_up = grid.gather_dp(up_rows).reshape(width, groups * cols_up)
    qkv_blocks = w_qkv.reshape(rows, 3, HEADS, HEAD)
    qkv_blocks = jnp.stack([qkv_blocks[:, :, head] for head in HEAD_ORDER])
    qkv_blocks = qkv_blocks.reshape(HEADS, rows, 3 * HEAD)
    qkv_rows = grid.exchange_sp(qkv_blocks).reshape(HEADS * rows, 3 * HEAD)
    weight_qkv = grid.gather_dp(qkv_rows).reshape(width, 3 * HEAD)
    weight_out = grid.gather_out(w_attn_out)
    g_all = grid.gather_sp(g_own)

    normed, _ = normalize(x_all.astype(F32))
    first_in = (normed * gain_one + shift_one).astype(BF16)
    second_in = (normed * gain_two + shift_two).astype(BF16)

    hidden = dot(second_in, weight_up, (1, 0)) + bias_up
    active_wide, gelu_pull = jax.vjp(lambda v: jax.nn.gelu(v, approximate=False), hidden)
    active = active_wide.astype(BF16)
    d_active = dot(g_all, weight_down, (1, 1))
    d_hidden = gelu_pull(d_active)[0].astype(BF16)
    term_down = dot(active, g_all, (0, 0)).astype(BF16)
    term_up = dot(second_in, d_hidden, (0, 0)).astype(BF16)

    joined = dot(first_in, weight_qkv, (1, 0)) + bias_qkv
    position = grid.part * length + jnp.arange(length, dtype=jnp.int32)
    cosine, sine = rotary_tables(position.astype(F32))
    queries = rotate(joined[:, :HEAD], cosine, sine).astype(BF16)
    key_rows = grid.whole_keys(rotate(joined[:, HEAD : 2 * HEAD], cosine, sine).astype(BF16))
    value_rows = grid.whole_keys(joined[:, 2 * HEAD :].astype(BF16))
    key_position = jnp.arange(key_rows.shape[0], dtype=jnp.int32)
    allowed = (seg_mine[:, None] == seg_all[None, :]) & (
        key_position[None, :] <= position[:, None]
    )
    scores = jnp.where(allowed, dot(queries, key_rows, (1, 1)) * scale, -1e30)
    top = jnp.max(scores, axis=-1, keepdims=True)
    weights = jnp.where(allowed, jnp.exp(scores - top), 0.0)
    weight_sum = jnp.sum(weights, axis=-1, keepdims=True)
    log_sum = top + jnp.log(weight_sum)
    context = dot(weights.astype(BF16), value_rows, (1, 0)) / weight_sum
    context_low = context.astype(BF16)

    out_terms = dot(context_low, weight_out, (1, 0)) + dot(active, weight_down, (1, 0))
    out_sum = grid.reduce_sp(out_terms.astype(BF16))
    block_output = (x_own.astype(F32) + out_sum + (bias_out + bias_down))[None]

    d_context = dot(g_all, weight_out, (1, 1)).astype(BF16)
    row_delta = jnp.sum(d_context.astype(F32) * context, axis=-1, keepdims=True)
    probs = jnp.where(allowed, jnp.exp(scores - log_sum), 0.0)
    d_probs = dot(d_context, value_rows, (1, 1))
    d_scores = (probs * (d_probs - row_delta)).astype(BF16)
    d_queries = dot(d_scores, key_rows, (1, 0)) * scale
    d_keys = grid.reduce_keys(dot(d_scores, queries, (0, 0)) * scale)
    d_values = grid.reduce_keys(dot(probs.astype(BF16), d_context, (0, 0)))
    d_joined = jnp.concatenate(
        [rotate(d_queries, cosine, -sine), rotate(d_keys, cosine, -sine), d_values], axis=1
    ).astype(BF16)

    d_first = dot(d_joined, weight_qkv, (1, 1))
    d_second = dot(d_hidden, weight_up, (1, 1))
    u_terms = d_first * gain_one + d_second * gain_two
    u_sum = grid.reduce_sp(u_terms.astype(BF16))
    normed_own, scale_own = normalize(x_own.astype(F32))
    u_mean = jnp.mean(u_sum, axis=-1, keepdims=True)
    u_along = jnp.mean(u_sum * normed_own, axis=-1, keepdims=True)
    input_grad = (g_own.astype(F32) + (u_sum - u_mean - normed_own * u_along) * scale_own)[None]

    term_qkv = dot(first_in, d_joined, (0, 0)).astype(BF16)
    term_out = dot(context_low, g_all, (0, 0)).astype(BF16)
    grad_down = grid.reduce_dp(term_down.reshape(groups, cols_up, width))
    up_sum = grid.reduce_dp(term_up.reshape(groups, HEADS * rows, groups * cols_up))
    up_back = grid.exchange_sp(up_sum.astype(BF16).reshape(HEADS, rows, groups * cols_up))
    grad_up = (
        up_back.astype(F32)
        .reshape(HEADS, rows, groups, cols_up)
        .transpose(1, 2, 0, 3)
        .reshape(rows, devices * cols_up)
    )
    grad_out = grid.reduce_out(term_out)
    qkv_sum = grid.reduce_dp(term_qkv.reshape(groups, HEADS * rows, 3 * HEAD))
    qkv_back = grid.exchange_sp(qkv_sum.astype(BF16).reshape(HEADS, rows, 3, HEAD)).astype(F32)
    grad_qkv = jnp.stack([qkv_back[place] for place in RANK_ORDER], axis=2)
    grad_qkv = grad_qkv.reshape(rows, 3 * HEADS * HEAD)

    sum_qkv = jnp.zeros((3, HEADS, HEAD), F32)
    sum_qkv = lax.dynamic_update_slice(
        sum_qkv,
        jnp.sum(d_joined.astype(F32), axis=0).reshape(3, 1, HEAD),
        (0, head_of(rank), 0),
    )
    sum_up = jnp.zeros((groups, HEADS, cols_up), F32)
    sum_up = lax.dynamic_update_slice(
        sum_up,
        jnp.sum(d_hidden.astype(F32), axis=0).reshape(groups, 1, cols_up),
        (0, rank, 0),
    )
    totals = [
        jnp.sum(d_first * normed, axis=0),
        jnp.sum(d_first, axis=0),
        jnp.sum(d_second * normed, axis=0),
        jnp.sum(d_second, axis=0),
        jnp.sum(g_own.astype(F32), axis=0),
        sum_qkv,
        sum_up,
    ]
    totals = jnp.concatenate([total.reshape(devices, -1) for total in totals], axis=1)
    owned = grid.reduce_small(totals)
    parts = [owned[k * rows : (k + 1) * rows] for k in range(5)]
    grad_g1, grad_s1, grad_g2, grad_s2, grad_bout = parts
    grad_bqkv = owned[5 * rows : 5 * rows + cols_qkv]
    grad_bup = owned[5 * rows + cols_qkv :]
    return (
        block_output,
        input_grad,
        grad_g1,
        grad_s1,
        grad_qkv,
        grad_bqkv,
        grad_out,
        grad_bout,
        grad_g2,
        grad_s2,
        grad_up,
        grad_bup,
        grad_down,
        grad_bout,
    )


def solution(mesh):
    tokens = P("dp", "sp", None)
    split = P(("dp", "sp"))
    matrix = P(("dp", "sp"), None)
    return jax.shard_map(
        shards,
        mesh=mesh,
        in_specs=(
            tokens,
            P("dp", "sp"),
            tokens,
            split,
            split,
            matrix,
            split,
            matrix,
            split,
            split,
            split,
            matrix,
            split,
            matrix,
            split,
        ),
        out_specs=(
            tokens,
            tokens,
            split,
            split,
            matrix,
            split,
            matrix,
            split,
            split,
            split,
            matrix,
            split,
            matrix,
            split,
        ),
        check_vma=False,
    )
```

time: 3660 us -> 696 us (0.19)
  waiting for transfers between devices: 3080 us -> 285 us
  starting transfers between devices: 0.44 us -> 154 us
  matrix products: 208 us -> 94.6 us
  other arithmetic: 150 us -> 55 us
  blocking collectives: 94.7 us -> 0 us
    unnamed x15 -> x0, waiting for transfers between devices: 1620 us -> none
    reduce_scatter x1 -> x0, waiting for transfers between devices: 879 us -> none  [shards(): lax.psum_scatter(jnp.concatenate([term_ctx, term_act], axis=1).reshape(nu...]
    all_gather x6 -> x0, waiting for transfers between devices: 585 us -> none  [the longest x1 174 us: shards(): piece_down = lax.all_gather(w_down[None], ('dp', 'sp'), axis=0, tiled=True)]
    ppermute x0 -> x104, waiting for transfers between devices: none -> 285 us  [the longest x6 54.3 us: reduce_sp(): going_right = lax.ppermute(for_right, 'sp', right[:2 * step])]
    ppermute x0 -> x104, starting transfers between devices: none -> 154 us  [the longest x6 26.6 us: reduce_sp(): going_right = lax.ppermute(for_right, 'sp', right[:2 * step])]
    concatenate x4 -> x2, other arithmetic: 133 us -> 1.48 us  [reduce_dp(): jnp.concatenate([top_x.astype(F32) + top_y.astype(F32), low_x.astype(F32)...]
    dot_general x26 -> x18, matrix products: 208 us -> 94.6 us  [dot(): lax.dot_general(left, right, (((contract[0],), (contract[1],)), ((), ()))...]
    all_gather x2 -> x0, blocking collectives: 50.6 us -> none  [the longest x1 40.8 us: shards(): piece_bup = lax.all_gather(b_up[None], ('dp', 'sp'), axis=0, tiled=True)]
  transfers between devices with their start and end apart: 11 -> 104, of which waited for: 9 -> 51; matrix products, arithmetic and copies ran while one was open for 8% -> 18% of each run, Pallas kernels for 0% -> 0%
where the time goes in v1:
time: 696 us; the launch traced here: 685 us
  waiting for transfers between devices  285 us (41%)
  starting transfers between devices  154 us (22%)
  matrix products  94.6 us (14%)
  local copies, waits for them, and re-layouts  93.9 us (13%)
  other arithmetic  55 us (8%)
    dot_general x18, matrix products, dot(): lax.dot_general(left, right, (((contract[0],), (contract[1],)), ((), ()))...  94.6 us
    ppermute x6, waiting for transfers between devices, reduce_sp(): going_right = lax.ppermute(for_right, 'sp', right[:2 * step])  54.3 us
    ppermute x12, waiting for transfers between devices, exchange_sp(): lax.ppermute(pick(out, self.line ^ step), 'sp', swap(8, 2 * step))  53.8 us
    ppermute x6, waiting for transfers between devices, gather_sp(): from_right.append(lax.ppermute(from_right[-1], 'sp', left[:6 - 2 * step]))  29.1 us
    ppermute x6, starting transfers between devices, reduce_sp(): going_right = lax.ppermute(for_right, 'sp', right[:2 * step])  26.6 us
    ppermute x4, waiting for transfers between devices, reduce_dp(): lax.ppermute((to_y[:half].astype(F32) + far_x.astype(F32)).astype(BF16),...  25.1 us
    ppermute x6, waiting for transfers between devices, exchange_four(): lax.ppermute(pick(blocks, place ^ step), 'sp', swap(8, step))  23.7 us
    ppermute x4, waiting for transfers between devices, gather_dp(): far_two = lax.ppermute(along_x[half:], 'dp', swap(4, 2))  22.2 us
  transfers between devices with their start and end apart: 104, of which 51 were waited for; matrix products, arithmetic and copies ran while one was open for 18% of the time, Pallas kernels for 0%

profile of v1, /device:TPU:0, one launch (start us, length us, event | category | flops | bytes accessed | tf_op | source)
XLA Modules:
  0.0 684.9 jit_solution(14175159227825593228)
XLA Ops:
  89.8 10.4 %collective-permute-done.16 = bf16[2,64,768]{2,1,0:T(8,128)(2,1)S(1)} collective-permute-done((bf16[2,64,768]{2,1,0:T(8,128)(2,1)S(1)}, bf16[2,64,768]{2,1,0:T(8,128)(2,1)S(1)}, u32[]{:S(2)}, u32[]{:S(2)}) %collective-permute-start.16) | collective-permute-done | bytes 196640 | tf_op jit(solution)/shard_map/ppermute | solution.py:130
  113.5 7.1 %collective-permute-done.30 = bf16[2,64,1024]{2,1,0:T(8,128)(2,1)S(1)} collective-permute-done((bf16[2,64,1024]{2,1,0:T(8,128)(2,1)S(1)}, bf16[2,64,1024]{2,1,0:T(8,128)(2,1)S(1)}, u32[]{:S(2)}, u32[]{:S(2)}) %collective-permute-start.30) | collective-permute-done | bytes 262176 | tf_op jit(solution)/shard_map/ppermute | solution.py:130
  122.6 7.3 %collective-permute-done.31 = bf16[2,64,1024]{2,1,0:T(8,128)(2,1)S(1)} collective-permute-done((bf16[2,64,1024]{2,1,0:T(8,128)(2,1)S(1)}, bf16[2,64,1024]{2,1,0:T(8,128)(2,1)S(1)}, u32[]{:S(2)}, u32[]{:S(2)}) %collective-permute-start.31) | collective-permute-done | bytes 262176 | tf_op jit(solution)/shard_map/ppermute | solution.py:130
  141.1 7.6 %collective-permute-done.28 = bf16[64,2048]{1,0:T(8,128)(2,1)S(1)} collective-permute-done((bf16[64,2048]{1,0:T(8,128)(2,1)S(1)}, bf16[64,2048]{1,0:T(8,128)(2,1)S(1)}, u32[]{:S(2)}, u32[]{:S(2)}) %collective-permute-start.28) | collective-permute-done | bytes 262176 | tf_op jit(solution)/shard_map/ppermute | solution.py:140
  167.8 8.3 %collective-permute-done.19 = bf16[512,768]{1,0:T(8,128)(2,1)S(1)} collective-permute-done((bf16[512,768]{1,0:T(8,128)(2,1)S(1)}, bf16[512,768]{1,0:T(8,128)(2,1)S(1)}, u32[]{:S(2)}, u32[]{:S(2)}) %collective-permute-start.19) | collective-permute-done | bytes 786464 | tf_op jit(solution)/shard_map/ppermute | solution.py:60
  180.5 7.4 %collective-permute-done.50 = bf16[128,2048]{1,0:T(8,128)(2,1)S(1)} collective-permute-done((bf16[128,2048]{1,0:T(8,128)(2,1)S(1)}, bf16[128,2048]{1,0:T(8,128)(2,1)S(1)}, u32[]{:S(2)}, u32[]{:S(2)}) %collective-permute-start.50) | collective-permute-done | bytes 524320 | tf_op jit(solution)/shard_map/ppermute | solution.py:93
  188.6 9.7 %collective-permute-done.10 = bf16[128,2048]{1,0:T(8,128)(2,1)S(1)} collective-permute-done((bf16[128,2048]{1,0:T(8,128)(2,1)S(1)}, bf16[128,2048]{1,0:T(8,128)(2,1)S(1)}, u32[]{:S(2)}, u32[]{:S(2)}) %collective-permute-start.10) | collective-permute-done | bytes 524320 | tf_op jit(solution)/shard_map/ppermute | solution.py:93
  203.3 9.9 %collective-permute-done.51 = bf16[128,2048]{1,0:T(8,128)(2,1)S(1)} collective-permute-done((bf16[128,2048]{1,0:T(8,128)(2,1)S(1)}, bf16[128,2048]{1,0:T(8,128)(2,1)S(1)}, u32[]{:S(2)}, u32[]{:S(2)}) %collective-permute-start.51) | collective-permute-done | bytes 524320 | tf_op jit(solution)/shard_map/ppermute | solution.py:93
  220.4 7.9 %collective-permute-done.20 = bf16[256,768]{1,0:T(8,128)(2,1)S(1)} collective-permute-done((bf16[256,768]{1,0:T(8,128)(2,1)S(1)}, bf16[256,768]{1,0:T(8,128)(2,1)S(1)}, u32[]{:S(2)}, u32[]{:S(2)}) %collective-permute-start.20) | collective-permute-done | bytes 393248 | tf_op jit(solution)/shard_map/ppermute | solution.py:61
  228.2 20.2 %collective-permute-done.21 = bf16[256,768]{1,0:T(8,128)(2,1)S(1)} collective-permute-done((bf16[256,768]{1,0:T(8,128)(2,1)S(1)}, bf16[256,768]{1,0:T(8,128)(2,1)S(1)}, u32[]{:S(2)}, u32[]{:S(2)}) %collective-permute-start.21) | collective-permute-done | bytes 393248 | tf_op jit(solution)/shard_map/ppermute | solution.py:62
  250.7 11.6 %collective-permute-done.35 = bf16[256,1024]{1,0:T(8,128)(2,1)S(1)} collective-permute-done((bf16[256,1024]{1,0:T(8,128)(2,1)S(1)}, bf16[256,1024]{1,0:T(8,128)(2,1)S(1)}, u32[]{:S(2)}, u32[]{:S(2)}) %collective-permute-start.35) | collective-permute-done | bytes 524320 | tf_op jit(solution)/shard_map/ppermute | solution.py:61
  303.3 18.0 %convert_reduce_fusion.1 = (f32[1024]{0:T(1024)}, bf16[1024,1024]{0,1:T(8,128)(2,1)}, f32[1024,1024]{0,1:T(8,128)}) fusion(f32[1024,1024]{0,1:T(8,128)S(1)} %fusion.159, f32[1024]{0:T(1024)S(1)} %bitcast.565, bf16[1024,2048]{1,0:T(8,128)(2,1)S(1)} %bitcast.534, bf16[1024,2048]{1,0:T(8,128)(2,1)} %bitcast.78), kind=kOutput, calls=%fused_computation.20 | convolution fusion | flops 4373609472 | bytes 18882560 | tf_op jit(solution)/shard_map/dot_general | solution.py:262
  321.3 16.6 %fusion.152 = (f32[2048]{0:T(1024)}, f32[2048]{0:T(1024)}, bf16[1024,2048]{1,0:T(8,128)(2,1)}, f32[2048]{0:T(1024)}, f32[2048]{0:T(1024)}, /*index=5*/bf16[1024,2048]{1,0:T(8,128)(2,1)}, bf16[1024,2048]{1,0:T(8,128)(2,1)}) fusion(f32[1024]{0:T(1024)S(1)} %bitcast.567, f32[1024]{0:T(1024)S(1)} %bitcast.564, ...), kind=kOutput, calls=%fused_computation.425 | convolution fusion | flops 4336902144 | bytes 31531008 | tf_op jit(solution)/shard_map/dot_general | solution.py:262
  338.0 7.4 %convolution_convert_fusion.1 = bf16[2048,1024]{1,0:T(8,128)(2,1)S(1)} fusion(bf16[1024,2048]{1,0:T(8,128)(2,1)} %get-tuple-element.32, bf16[1024,1024]{0,1:T(8,128)(2,1)} %get-tuple-element.25), kind=kOutput, calls=%fused_computation.43 | convolution fusion | flops 4297064448 | bytes 10485760 | tf_op jit(solution)/shard_map/dot_general | solution.py:262
  364.9 11.0 %fusion.160 = f32[1024,2048]{1,0:T(8,128)} fusion(bf16[1024,1024]{0,1:T(8,128)(2,1)S(1)} %multiply_convert_fusion.1, bf16[1024,2048]{1,0:T(8,128)(2,1)} %bitcast.78), kind=kOutput, calls=%fused_computation.432 | convolution fusion | flops 4294967296 | bytes 14680064 | tf_op jit(solution)/shard_map/dot_general | solution.py:262
  413.8 9.2 %collective-permute-done.72 = bf16[256,768]{1,0:T(8,128)(2,1)S(1)} collective-permute-done((bf16[256,768]{1,0:T(8,128)(2,1)S(1)}, bf16[256,768]{1,0:T(8,128)(2,1)S(1)}, u32[]{:S(2)}, u32[]{:S(2)}) %collective-permute-start.72) | collective-permute-done | bytes 393248 | tf_op jit(solution)/shard_map/ppermute | solution.py:73
  432.0 7.4 %collective-permute-done.81 = bf16[64,2048]{1,0:T(8,128)(2,1)S(1)} collective-permute-done((bf16[64,2048]{1,0:T(8,128)(2,1)S(1)}, bf16[64,2048]{1,0:T(8,128)(2,1)S(1)}, u32[]{:S(2)}, u32[]{:S(2)}) %collective-permute-start.81) | collective-permute-done | bytes 262176 | tf_op jit(solution)/shard_map/ppermute | solution.py:140
  506.9 10.1 %collective-permute-done.100 = bf16[128,2048]{1,0:T(8,128)(2,1)S(1)} collective-permute-done((bf16[128,2048]{1,0:T(8,128)(2,1)S(1)}, bf16[128,2048]{1,0:T(8,128)(2,1)S(1)}, u32[]{:S(2)}, u32[]{:S(2)}) %collective-permute-start.100) | collective-permute-done | bytes 524320 | tf_op jit(solution)/shard_map/ppermute | solution.py:76
  529.4 13.2 %collective-permute-done.77 = bf16[2,64,3,256]{3,1,2,0:T(8,128)(2,1)S(1)} collective-permute-done((bf16[2,64,3,256]{3,1,2,0:T(8,128)(2,1)S(1)}, bf16[2,64,3,256]{3,1,2,0:T(8,128)(2,1)S(1)}, u32[]{:S(2)}, u32[]{:S(2)}) %collective-permute-start.77) | collective-permute-done | bytes 196640 | tf_op jit(solution)/shard_map/ppermute | solution.py:130
  556.4 9.2 %collective-permute-done.56 = bf16[128,2048]{1,0:T(8,128)(2,1)S(1)} collective-permute-done((bf16[128,2048]{1,0:T(8,128)(2,1)S(1)}, bf16[128,2048]{1,0:T(8,128)(2,1)S(1)}, u32[]{:S(2)}, u32[]{:S(2)}) %collective-permute-start.56) | collective-permute-done | bytes 524320 | tf_op jit(solution)/shard_map/ppermute | solution.py:118
  589.3 9.1 %collective-permute-done.43 = bf16[128,2048]{1,0:T(8,128)(2,1)S(1)} collective-permute-done((bf16[128,2048]{1,0:T(8,128)(2,1)S(1)}, bf16[128,2048]{1,0:T(8,128)(2,1)S(1)}, u32[]{:S(2)}, u32[]{:S(2)}) %collective-permute-start.43) | collective-permute-done | bytes 524320 | tf_op jit(solution)/shard_map/ppermute | solution.py:118
  624.2 19.1 %collective-permute-done.44 = bf16[128,2048]{1,0:T(8,128)(2,1)S(1)} collective-permute-done((bf16[128,2048]{1,0:T(8,128)(2,1)S(1)}, bf16[128,2048]{1,0:T(8,128)(2,1)S(1)}, u32[]{:S(2)}, u32[]{:S(2)}) %collective-permute-start.44) | collective-permute-done | bytes 524320 | tf_op jit(solution)/shard_map/ppermute | solution.py:118
  643.3 7.7 %collective-permute-done.47 = bf16[128,2048]{1,0:T(8,128)(2,1)S(1)} collective-permute-done((bf16[128,2048]{1,0:T(8,128)(2,1)S(1)}, bf16[128,2048]{1,0:T(8,128)(2,1)S(1)}, u32[]{:S(2)}, u32[]{:S(2)}) %collective-permute-start.47) | collective-permute-done | bytes 524320 | tf_op jit(solution)/shard_map/ppermute | solution.py:119
  661.9 10.4 %collective-permute-start.66 = (f32[768]{0:T(1024)S(1)}, f32[768]{0:T(1024)S(1)}, u32[]{:S(2)}, u32[]{:S(2)}) collective-permute-start(f32[768]{0:T(1024)S(1)} %get-tuple-element.20), channel_id=1, source_target_pairs={{0,2},{1,3},{2,0},{3,1},{4,6},{5,7},{6,4},{7,5},{8,10},{9,11},{10,... | collective-permute-start | bytes 9224 | tf_op jit(solution)/shard_map/ppermute | solution.py:171
  (533 shorter events, 426.3 us)
Async XLA Ops:
  0.7 150.1 %collective-permute-start.8 = (bf16[128,2048]{1,0:T(8,128)(2,1)}, bf16[128,2048]{1,0:T(8,128)(2,1)}, u32[]{:S(2)}, u32[]{:S(2)}) collective-permute-start(bf16[128,2048]{1,0:T(8,128)(2,1)} %bitcast.510), channel_id=1, source_target_pairs={{2,0},{3,1},{4,2},{5,3},{6,4},{7,5},{10,8},{11,9},{12,10},{13,11},... | collective-permute-start | bytes 1572872 | tf_op jit(solution)/shard_map/ppermute | solution.py:93
  2.1 153.2 %collective-permute-start.7 = (bf16[128,2048]{1,0:T(8,128)(2,1)}, bf16[128,2048]{1,0:T(8,128)(2,1)}, u32[]{:S(2)}, u32[]{:S(2)}) collective-permute-start(bf16[128,2048]{1,0:T(8,128)(2,1)} %bitcast.511), channel_id=1, source_target_pairs={{0,2},{1,3},{2,4},{3,5},{4,6},{5,7},{8,10},{9,11},{10,12},{11,13},... | collective-permute-start | bytes 1572872 | tf_op jit(solution)/shard_map/ppermute | solution.py:92
  14.5 142.1 %collective-permute-start.37 = (bf16[256,2048]{1,0:T(8,128)(2,1)}, bf16[256,2048]{1,0:T(8,128)(2,1)}, u32[]{:S(2)}, u32[]{:S(2)}) collective-permute-start(bf16[256,2048]{1,0:T(8,128)(2,1)} %param.28), channel_id=1, source_target_pairs={{0,8},{8,0},{16,24},{24,16},{1,9},{9,1},{17,25},{25,17},{2,10},{10... | collective-permute-start | bytes 3145736 | tf_op jit(solution)/shard_map/ppermute | solution.py:59
  16.5 56.0 %collective-permute-start.22 = (bf16[64,2048]{1,0:T(8,128)(2,1)}, bf16[64,2048]{1,0:T(8,128)(2,1)}, u32[]{:S(2)}, u32[]{:S(2)}) collective-permute-start(bf16[64,2048]{1,0:T(8,128)(2,1)} %param.22), channel_id=1, source_target_pairs={{0,8},{8,0},{16,24},{24,16},{1,9},{9,1},{17,25},{25,17},{2,10},{10... | collective-permute-start | bytes 786440 | tf_op jit(solution)/shard_map/ppermute | solution.py:59
  80.4 30.2 %collective-permute-start.26 = (bf16[64,2048]{1,0:T(8,128)(2,1)S(1)}, bf16[64,2048]{1,0:T(8,128)(2,1)S(1)}, u32[]{:S(2)}, u32[]{:S(2)}) collective-permute-start(bf16[64,2048]{1,0:T(8,128)(2,1)S(1)} %dynamic-slice_bitcast_fusion.32), channel_id=1, source_target_pairs={{0,1},{1,0},{2,3},{3,2},{4,5},{5,4},{6,7},{7,6},{8,9},{9,8},{10,11... | collective-permute-start | bytes 786440 | tf_op jit(solution)/shard_map/ppermute | solution.py:140
  176.1 38.1 %collective-permute-start.52 = (bf16[128,2048]{1,0:T(8,128)(2,1)S(1)}, bf16[128,2048]{1,0:T(8,128)(2,1)S(1)}, u32[]{:S(2)}, u32[]{:S(2)}) collective-permute-start(bf16[128,2048]{1,0:T(8,128)(2,1)S(1)} %collective-permute-done.48), channel_id=1, source_target_pairs={{2,4},{3,5},{4,6},{5,7},{10,12},{11,13},{12,14},{13,15},{18,20},{1... | collective-permute-start | bytes 1572872 | tf_op jit(solution)/shard_map/ppermute | solution.py:92
  176.8 72.0 %collective-permute-start.33 = (bf16[512,1024]{1,0:T(8,128)(2,1)S(1)}, bf16[512,1024]{1,0:T(8,128)(2,1)S(1)}, u32[]{:S(2)}, u32[]{:S(2)}) collective-permute-start(bf16[512,1024]{1,0:T(8,128)(2,1)S(1)} %bitcast.528), channel_id=1, source_target_pairs={{0,8},{8,0},{16,24},{24,16},{1,9},{9,1},{17,25},{25,17},{2,10},{10... | collective-permute-start | bytes 3145736 | tf_op jit(solution)/shard_map/ppermute | solution.py:59
  180.0 36.2 %collective-permute-start.39 = (bf16[128,2048]{1,0:T(8,128)(2,1)S(1)}, bf16[128,2048]{1,0:T(8,128)(2,1)S(1)}, u32[]{:S(2)}, u32[]{:S(2)}) collective-permute-start(bf16[128,2048]{1,0:T(8,128)(2,1)S(1)} %slice.445), channel_id=1, source_target_pairs={{0,8},{8,0},{16,24},{24,16},{1,9},{9,1},{17,25},{25,17},{2,10},{10... | collective-permute-start | bytes 1572872 | tf_op jit(solution)/shard_map/ppermute | solution.py:61
  213.3 49.4 %collective-permute-start.13 = (bf16[4,128,2048]{2,1,0:T(8,128)(2,1)S(1)}, bf16[4,128,2048]{2,1,0:T(8,128)(2,1)S(1)}, u32[]{:S(2)}, u32[]{:S(2)}) collective-permute-start(bf16[4,128,2048]{2,1,0:T(8,128)(2,1)S(1)} %bitcast_dynamic-update-slice_fusion.10), channel_id=1, source_target_pairs={{0,1},{1,0},{2,3},{3,2},{4,5},{5,4},{6,7},{7,6},{8,9},{9,8},{10,11... | collective-permute-start | bytes 6291464 | tf_op jit(solution)/shard_map/ppermute | solution.py:98
  214.2 34.3 %collective-permute-start.34 = (bf16[512,1024]{1,0:T(8,128)(2,1)S(1)}, bf16[512,1024]{1,0:T(8,128)(2,1)S(1)}, u32[]{:S(2)}, u32[]{:S(2)}) collective-permute-start(bf16[512,1024]{1,0:T(8,128)(2,1)S(1)} %bitcast.529), channel_id=1, source_target_pairs={{0,16},{8,24},{16,0},{24,8},{1,17},{9,25},{17,1},{25,9},{2,18},{10... | collective-permute-start | bytes 3145736 | tf_op jit(solution)/shard_map/ppermute | solution.py:60
  218.9 29.5 %collective-permute-start.21 = (bf16[256,768]{1,0:T(8,128)(2,1)S(1)}, bf16[256,768]{1,0:T(8,128)(2,1)S(1)}, u32[]{:S(2)}, u32[]{:S(2)}) collective-permute-start(bf16[256,768]{1,0:T(8,128)(2,1)S(1)} %slice.426), channel_id=1, source_target_pairs={{0,16},{8,24},{16,0},{24,8},{1,17},{9,25},{17,1},{25,9},{2,18},{10... | collective-permute-start | bytes 1179656 | tf_op jit(solution)/shard_map/ppermute | solution.py:62
  228.2 36.8 %collective-permute-start.54 = (bf16[4,128,2048]{2,1,0:T(8,128)(2,1)}, bf16[4,128,2048]{2,1,0:T(8,128)(2,1)S(1)}, u32[]{:S(2)}, u32[]{:S(2)}) collective-permute-start(bf16[4,128,2048]{2,1,0:T(8,128)(2,1)} %bitcast_dynamic-update-slice_fusion.7), channel_id=1, source_target_pairs={{0,1},{1,0},{2,3},{3,2},{4,5},{5,4},{6,7},{7,6},{8,9},{9,8},{10,11... | collective-permute-start | bytes 6291464 | tf_op jit(solution)/shard_map/ppermute | solution.py:98
  378.1 46.6 %collective-permute-start.101 = (bf16[128,2048]{1,0:T(8,128)(2,1)}, bf16[128,2048]{1,0:T(8,128)(2,1)}, u32[]{:S(2)}, u32[]{:S(2)}) collective-permute-start(bf16[128,2048]{1,0:T(8,128)(2,1)} %get-tuple-element.38), channel_id=1, source_target_pairs={{0,16},{8,24},{16,0},{24,8},{1,17},{9,25},{17,1},{25,9},{2,18},{10... | collective-permute-start | bytes 1572872 | tf_op jit(solution)/shard_map/ppermute | solution.py:73
  379.7 45.4 %collective-permute-start.99 = (bf16[128,2048]{1,0:T(8,128)(2,1)}, bf16[128,2048]{1,0:T(8,128)(2,1)}, u32[]{:S(2)}, u32[]{:S(2)}) collective-permute-start(bf16[128,2048]{1,0:T(8,128)(2,1)} %get-tuple-element.37), channel_id=1, source_target_pairs={{0,8},{8,0},{16,24},{24,16},{1,9},{9,1},{17,25},{25,17},{2,10},{10... | collective-permute-start | bytes 1572872 | tf_op jit(solution)/shard_map/ppermute | solution.py:72
  381.4 124.6 %collective-permute-start.98 = (bf16[128,2048]{1,0:T(8,128)(2,1)}, bf16[128,2048]{1,0:T(8,128)(2,1)}, u32[]{:S(2)}, u32[]{:S(2)}) collective-permute-start(bf16[128,2048]{1,0:T(8,128)(2,1)} %get-tuple-element.36), channel_id=1, source_target_pairs={{0,8},{8,0},{16,24},{24,16},{1,9},{9,1},{17,25},{25,17},{2,10},{10... | collective-permute-start | bytes 1572872 | tf_op jit(solution)/shard_map/ppermute | solution.py:74
  384.1 29.4 %collective-permute-start.70 = (bf16[256,768]{1,0:T(8,128)(2,1)}, bf16[256,768]{1,0:T(8,128)(2,1)S(1)}, u32[]{:S(2)}, u32[]{:S(2)}) collective-permute-start(bf16[256,768]{1,0:T(8,128)(2,1)} %get-tuple-element.55), channel_id=1, source_target_pairs={{0,8},{8,0},{16,24},{24,16},{1,9},{9,1},{17,25},{25,17},{2,10},{10... | collective-permute-start | bytes 1179656 | tf_op jit(solution)/shard_map/ppermute | solution.py:72
  424.8 69.9 %collective-permute-start.88 = (bf16[256,1024]{1,0:T(8,128)(2,1)}, bf16[256,1024]{1,0:T(8,128)(2,1)}, u32[]{:S(2)}, u32[]{:S(2)}) collective-permute-start(bf16[256,1024]{1,0:T(8,128)(2,1)} %get-tuple-element.42), channel_id=1, source_target_pairs={{0,8},{8,0},{16,24},{24,16},{1,9},{9,1},{17,25},{25,17},{2,10},{10... | collective-permute-start | bytes 1572872 | tf_op jit(solution)/shard_map/ppermute | solution.py:74
  439.5 61.9 %collective-permute-start.93 = (bf16[256,1024]{1,0:T(8,128)(2,1)}, bf16[256,1024]{1,0:T(8,128)(2,1)}, u32[]{:S(2)}, u32[]{:S(2)}) collective-permute-start(bf16[256,1024]{1,0:T(8,128)(2,1)} %get-tuple-element.45), channel_id=1, source_target_pairs={{0,16},{8,24},{16,0},{24,8},{1,17},{9,25},{17,1},{25,9},{2,18},{10... | collective-permute-start | bytes 1572872 | tf_op jit(solution)/shard_map/ppermute | solution.py:75
  500.2 53.2 %collective-permute-start.41 = (bf16[4,128,2048]{2,1,0:T(8,128)(2,1)S(1)}, bf16[4,128,2048]{2,1,0:T(8,128)(2,1)S(1)}, u32[]{:S(2)}, u32[]{:S(2)}) collective-permute-start(bf16[4,128,2048]{2,1,0:T(8,128)(2,1)S(1)} %copy-done.20), channel_id=1, source_target_pairs={{0,1},{1,0},{2,3},{3,2},{4,5},{5,4},{6,7},{7,6},{8,9},{9,8},{10,11... | collective-permute-start | bytes 6291464 | tf_op jit(solution)/shard_map/ppermute | solution.py:107
  506.9 38.7 %collective-permute-start.55 = (bf16[4,128,2048]{2,1,0:T(8,128)(2,1)S(1)}, bf16[4,128,2048]{2,1,0:T(8,128)(2,1)S(1)}, u32[]{:S(2)}, u32[]{:S(2)}) collective-permute-start(bf16[4,128,2048]{2,1,0:T(8,128)(2,1)S(1)} %copy-done.21), channel_id=1, source_target_pairs={{0,1},{1,0},{2,3},{3,2},{4,5},{5,4},{6,7},{7,6},{8,9},{9,8},{10,11... | collective-permute-start | bytes 6291464 | tf_op jit(solution)/shard_map/ppermute | solution.py:107
  518.2 52.0 %collective-permute-start.94 = (bf16[4,64,1024]{2,1,0:T(8,128)(2,1)S(1)}, bf16[4,64,1024]{2,1,0:T(8,128)(2,1)S(1)}, u32[]{:S(2)}, u32[]{:S(2)}) collective-permute-start(bf16[4,64,1024]{2,1,0:T(8,128)(2,1)S(1)} %dynamic-slice_bitcast_fusion.14), channel_id=1, source_target_pairs={{0,1},{1,0},{2,3},{3,2},{4,5},{5,4},{6,7},{7,6},{8,9},{9,8},{10,11... | collective-permute-start | bytes 1572872 | tf_op jit(solution)/shard_map/ppermute | solution.py:125
  606.2 49.6 %collective-permute-start.95 = (bf16[2,64,1024]{2,1,0:T(8,128)(2,1)S(1)}, bf16[2,64,1024]{2,1,0:T(8,128)(2,1)S(1)}, u32[]{:S(2)}, u32[]{:S(2)}) collective-permute-start(bf16[2,64,1024]{2,1,0:T(8,128)(2,1)S(1)} %get-tuple-element.81), channel_id=1, source_target_pairs={{0,2},{1,3},{2,0},{3,1},{4,6},{5,7},{6,4},{7,5},{8,10},{9,11},{10,... | collective-permute-start | bytes 786440 | tf_op jit(solution)/shard_map/ppermute | solution.py:130
  609.5 51.2 %collective-permute-start.96 = (bf16[2,64,1024]{2,1,0:T(8,128)(2,1)S(1)}, bf16[2,64,1024]{2,1,0:T(8,128)(2,1)S(1)}, u32[]{:S(2)}, u32[]{:S(2)}) collective-permute-start(bf16[2,64,1024]{2,1,0:T(8,128)(2,1)S(1)} %get-tuple-element.82), channel_id=1, source_target_pairs={{0,4},{1,5},{2,6},{3,7},{4,0},{5,1},{6,2},{7,3},{8,12},{9,13},{10,... | collective-permute-start | bytes 786440 | tf_op jit(solution)/shard_map/ppermute | solution.py:130
  611.0 63.8 %collective-permute-start.97 = (bf16[2,64,1024]{2,1,0:T(8,128)(2,1)S(1)}, bf16[2,64,1024]{2,1,0:T(8,128)(2,1)S(1)}, u32[]{:S(2)}, u32[]{:S(2)}) collective-permute-start(bf16[2,64,1024]{2,1,0:T(8,128)(2,1)S(1)} %get-tuple-element.80), channel_id=1, source_target_pairs={{0,6},{1,7},{2,4},{3,5},{4,2},{5,3},{6,0},{7,1},{8,14},{9,15},{10,... | collective-permute-start | bytes 786440 | tf_op jit(solution)/shard_map/ppermute | solution.py:130
  (130 other events, 1867.9 us)

commit v2 on v1

--- a/solution.py
+++ b/solution.py
@@ -1,16 +1,19 @@
+import functools
 import math
 
 import jax
 import jax.numpy as jnp
 from jax import lax
+from jax.experimental import pallas as pl
+from jax.experimental.pallas import tpu as pltpu
 from jax.sharding import PartitionSpec as P
 
 HEADS = 8
 HEAD = 256
 ROT = 64
+TILE = 256
 BF16 = jnp.bfloat16
 F32 = jnp.float32
-
 
 def normalize(values):
     center = values - jnp.mean(values, axis=-1, keepdims=True)
@@ -44,144 +47,6 @@
 
 def swap(extent, mask):
     return [(i, i ^ mask) for i in range(extent)]
-
-
-class LineGrid:
-    def __init__(self):
-        self.dp = lax.axis_index("dp")
-        self.sp = lax.axis_index("sp")
-        self.line = self.sp // 2
-        self.core = self.sp % 2
-        self.part = 0
-
-    def gather_dp(self, block):
-        half = block.shape[0] // 2
-        along_x = lax.ppermute(block, "dp", swap(4, 1))
-        along_y = lax.ppermute(block, "dp", swap(4, 2))
-        far_one = lax.ppermute(along_y[:half], "dp", swap(4, 1))
-        far_two = lax.ppermute(along_x[half:], "dp", swap(4, 2))
-        far = jnp.concatenate([far_one, far_two], axis=0)
-        out = jnp.zeros((4,) + block.shape, block.dtype)
-        for mask, piece in enumerate((block, along_x, along_y, far)):
-            out = put(out, piece, self.dp ^ mask)
-        return out
-
-    def reduce_dp(self, terms):
-        half = terms.shape[1] // 2
-        own, to_x, to_y, to_far = (pick(terms, self.dp ^ mask) for mask in range(4))
-        far_x = lax.ppermute(to_far[:half], "dp", swap(4, 1))
-        far_y = lax.ppermute(to_far[half:], "dp", swap(4, 2))
-        top_x = lax.ppermute(to_x[:half], "dp", swap(4, 1))
-        low_y = lax.ppermute(to_y[half:], "dp", swap(4, 2))
-        top_y = lax.ppermute(
-            (to_y[:half].astype(F32) + far_x.astype(F32)).astype(BF16), "dp", swap(4, 2)
-        )
-        low_x = lax.ppermute(
-            (to_x[half:].astype(F32) + far_y.astype(F32)).astype(BF16), "dp", swap(4, 1)
-        )
-        others = jnp.concatenate(
-            [top_x.astype(F32) + top_y.astype(F32), low_x.astype(F32) + low_y.astype(F32)], axis=0
-        )
-        return own.astype(F32) + others
-
-    def gather_sp(self, block):
-        right = [(i, i + 2) for i in range(6)]
-        left = [(i + 2, i) for i in range(6)]
-        from_left, from_right = [block], [block]
-        for step in range(3):
-            from_left.append(lax.ppermute(from_left[-1], "sp", right[2 * step :]))
-            from_right.append(lax.ppermute(from_right[-1], "sp", left[: 6 - 2 * step]))
-        mine = put(jnp.zeros((4,) + block.shape, block.dtype), block, self.line)
-        for step in range(1, 4):
-            piece = jnp.where(self.line >= step, from_left[step], from_right[4 - step])
-            mine = put(mine, piece, (self.line - step) % 4)
-        other = lax.ppermute(mine, "sp", swap(8, 1))
-        pair = jnp.stack(
-            [jnp.where(self.core == 0, mine, other), jnp.where(self.core == 0, other, mine)], axis=1
-        )
-        return pair.reshape((8 * block.shape[0],) + block.shape[1:])
-
-    def reduce_sp(self, terms):
-        rows = terms.shape[0] // 8
-        pairs = terms.reshape((4, 2, rows) + terms.shape[1:])
-        other = lax.ppermute(pick(pairs, 1 - self.core, 1), "sp", swap(8, 1))
-        mine = (pick(pairs, self.core, 1).astype(F32) + other.astype(F32)).astype(BF16)
-        right = [(i, i + 2) for i in range(6)]
-        left = [(i + 2, i) for i in range(6)]
-        going_right = going_left = None
-        for step in range(1, 4):
-            for_right = pick(mine, jnp.minimum(self.line + 4 - step, 3))
-            for_left = pick(mine, jnp.maximum(self.line - 4 + step, 0))
-            if step > 1:
-                for_right = (for_right.astype(F32) + going_right.astype(F32)).astype(BF16)
-                for_left = (for_left.astype(F32) + going_left.astype(F32)).astype(BF16)
-            going_right = lax.ppermute(for_right, "sp", right[: 2 * step])
-            going_left = lax.ppermute(for_left, "sp", left[6 - 2 * step :])
-        return pick(mine, self.line).astype(F32) + going_right.astype(F32) + going_left.astype(F32)
-
-    def exchange_sp(self, blocks):
-        pairs = blocks.reshape((4, 2) + blocks.shape[1:])
-        keep = pick(pairs, self.core, 1)
-        other = lax.ppermute(pick(pairs, 1 - self.core, 1), "sp", swap(8, 1))
-        out = jnp.stack(
-            [jnp.where(self.core == 0, keep, other), jnp.where(self.core == 0, other, keep)], axis=1
-        )
-        moved = [
-            lax.ppermute(pick(out, self.line ^ step), "sp", swap(8, 2 * step))
-            for step in range(1, 4)
-        ]
-        for step in range(1, 4):
-            out = put(out, moved[step - 1], self.line ^ step)
-        return out.reshape(blocks.shape)
-
-    def exchange_four(self, blocks):
-        place = self.sp % 4
-        moved = [
-            lax.ppermute(pick(blocks, place ^ step), "sp", swap(8, step)) for step in range(1, 4)
-        ]
-        for step in range(1, 4):
-            blocks = put(blocks, moved[step - 1], place ^ step)
-        return blocks
-
-    def gather_small(self, vector):
-        out = jnp.zeros((8, 4) + vector.shape, vector.dtype)
-        other = lax.ppermute(vector, "sp", swap(8, 1))
-        pair = jnp.stack(
-            [jnp.where(self.core == 0, vector, other), jnp.where(self.core == 0, other, vector)]
-        )
-        out = put(jnp.zeros((4,) + pair.shape, pair.dtype), pair, self.line)
-        for step in range(1, 4):
-            out = put(out, lax.ppermute(pair, "sp", swap(8, 2 * step)), self.line ^ step)
-        whole = put(jnp.zeros((4,) + out.shape, out.dtype), out, self.dp)
-        for step in range(1, 4):
-            whole = put(whole, lax.ppermute(out, "dp", swap(4, step)), self.dp ^ step)
-        return whole.reshape((32,) + vector.shape)
-
-    def reduce_small(self, terms):
-        blocks = terms.reshape((4, 8) + terms.shape[1:])
-        total = pick(blocks, self.dp)
-        for step in range(1, 4):
-            total = total + lax.ppermute(pick(blocks, self.dp ^ step), "dp", swap(4, step))
-        pairs = total.reshape((4, 2) + terms.shape[1:])
-        pair = pick(pairs, self.core, 1) + lax.ppermute(
-            pick(pairs, 1 - self.core, 1), "sp", swap(8, 1)
-        )
-        total = pick(pair, self.line)
-        for step in range(1, 4):
-            total = total + lax.ppermute(pick(pair, self.line ^ step), "sp", swap(8, 2 * step))
-        return total
-
-    def gather_out(self, block):
-        return self.exchange_four(self.gather_dp(block)).reshape(HEAD, block.shape[1])
-
-    def reduce_out(self, terms):
-        return self.reduce_dp(self.exchange_four(terms.reshape(4, HEAD // 4, terms.shape[1])))
-
-    def whole_keys(self, block):
-        return block
-
-    def reduce_keys(self, terms):
-        return terms
 
 
 class AnyGrid:
@@ -264,7 +129,7 @@
     )
 
 
-def shards(
+def any_shards(
     block_input,
     segments,
     out_grad,
@@ -283,7 +148,7 @@
 ):
     dps, sps = lax.axis_size("dp"), lax.axis_size("sp")
     devices = dps * sps
-    grid = LineGrid() if (dps, sps) == (4, 8) else AnyGrid()
+    grid = AnyGrid()
     groups = devices // HEADS
     x_own = block_input[0]
     g_own = out_grad[0]
@@ -454,6 +319,467 @@
     )
 
 
+def fill(dp, full, pieces, rows, take=None):
+    own, along_x, along_y, far_one, far_two = pieces
+    take = rows if take is None else take
+    def at(mask, shift=0):
+        return pl.multiple_of((dp ^ mask) * take + shift, 16)
+    full[pl.ds(at(0), take), :] = own[0:take, :]
+    full[pl.ds(at(1), take), :] = along_x[0:take, :]
+    full[pl.ds(at(2), take), :] = along_y[0:take, :]
+    cut = far_one.shape[0]
+    full[pl.ds(at(3), cut), :] = far_one[...]
+    full[pl.ds(at(3, cut), take - cut), :] = far_two[0 : take - cut, :]
+
+def whole(shape):
+    return pl.BlockSpec(shape, lambda *_: (0,) * len(shape), pipeline_mode=pl.Buffered(1))
+
+def tile(cols):
+    return pl.BlockSpec((TILE, cols), lambda i, *_: (i, 0))
+
+def run(body, name, dp, inputs, specs, outs, out_specs, scratch, grid, flops=0, vmem=56):
+    bytes_accessed = sum(a.size * a.dtype.itemsize for a in inputs) + sum(math.prod(o.shape) * o.dtype.itemsize for o in outs)
+    return pl.pallas_call(
+        body, name=name,
+        grid_spec=pltpu.PrefetchScalarGridSpec(num_scalar_prefetch=1, grid=grid, in_specs=specs, out_specs=out_specs, scratch_shapes=scratch),
+        out_shape=outs,
+        compiler_params=pltpu.CompilerParams(vmem_limit_bytes=vmem * 2**20, dimension_semantics=("arbitrary",) * len(grid)),
+        cost_estimate=pl.CostEstimate(flops=flops, bytes_accessed=bytes_accessed, transcendentals=0),
+    )(dp.reshape(1), *inputs)
+
+def shape(dims, kind):
+    return jax.ShapeDtypeStruct(dims, kind)
+
+def norm_tile(x):
+    v = x.astype(F32)
+    center = v - jnp.mean(v, axis=-1, keepdims=True)
+    scale = lax.rsqrt(jnp.mean(center * center, axis=-1, keepdims=True) + 1e-05)
+    return center * scale, scale
+
+def norms_body(dp, x, vec, first, second):
+    normed, _ = norm_tile(x[...])
+    first[...] = (normed * vec[0:1, :] + vec[1:2, :]).astype(BF16)
+    second[...] = (normed * vec[2:3, :] + vec[3:4, :]).astype(BF16)
+
+def norms(dp, x, vec):
+    n, w = x.shape
+    return run(norms_body, "norms", dp, [x, vec], [tile(w), whole(vec.shape)], [shape((n, w), BF16)] * 2, [tile(w)] * 2, [], (n // TILE,))
+
+def turn(v, cos, s1, s2):
+    left = v[:, :128]
+    out = left * cos + pltpu.roll(left, 96, 1) * s1 + pltpu.roll(left, 32, 1) * s2
+    return jnp.concatenate([out, v[:, 128:]], axis=1)
+
+def qkv_body(dp, first, w0, wx, wy, w1, w2, bias, cos, s1, s2, q, k, v, full):
+    @pl.when(pl.program_id(0) == 0)
+    def _():
+        fill(dp[0], full, (w0, wx, wy, w1, w2), w0.shape[0])
+    joined = dot(first[...], full[...], (1, 0)) + bias[...]
+    q[...] = turn(joined[:, :HEAD], cos[...], s1[...], s2[...]).astype(BF16)
+    k[...] = turn(joined[:, HEAD:2 * HEAD], cos[...], s1[...], s2[...]).astype(BF16)
+    v[...] = joined[:, 2 * HEAD:].astype(BF16)
+
+def qkv(dp, first, pieces, bias, tables):
+    n, w = first.shape
+    return run(qkv_body, "qkv", dp, [first, *pieces, bias, *tables],
+        [tile(w)] + [whole(p.shape) for p in pieces] + [whole(bias.shape)] + [tile(128)] * 3,
+        [shape((n, HEAD), BF16)] * 3, [tile(HEAD)] * 3, [pltpu.VMEM((w, 3 * HEAD), BF16)], (n // TILE,), flops=2 * n * w * 3 * HEAD)
+
+def mlp_body(dp, second, g, u0, ux, uy, u1, u2, d0, dx, dy, d1, d2, bias, active, d_hidden, sums, full_up, full_down):
+    step = pl.program_id(0)
+    @pl.when(step == 0)
+    def _():
+        fill(dp[0], full_up, (u0, ux, uy, u1, u2), u0.shape[0])
+        fill(dp[0], full_down, (d0, dx, dy, d1, d2), None, full_down.shape[0] // 4)
+        sums[...] = jnp.zeros_like(sums)
+    hidden = dot(second[...], full_up[...], (1, 0)) + bias[...]
+    d_active = dot(g[...], full_down[...], (1, 1))
+    half_cdf = 0.5 + 0.5 * lax.erf(hidden * (1.0 / math.sqrt(2.0)))
+    active[...] = (hidden * half_cdf).astype(BF16)
+    slope = half_cdf + hidden * (jnp.exp(-0.5 * hidden * hidden) * (1.0 / math.sqrt(2.0 * math.pi)))
+    low = (slope * d_active).astype(BF16)
+    d_hidden[...] = low
+    sums[...] += jnp.sum(low.astype(F32), axis=0, keepdims=True)
+
+def mlp(dp, second, g, up, down, bias):
+    n, w = second.shape
+    h = up[0].shape[1]
+    return run(mlp_body, "mlp", dp, [second, g, *up, *down, bias],
+        [tile(w)] * 2 + [whole(p.shape) for p in (*up, *down, bias)],
+        [shape((n, h), BF16)] * 2 + [shape((1, h), F32)], [tile(h)] * 2 + [whole((1, h))],
+        [pltpu.VMEM((w, h), BF16), pltpu.VMEM((h, w), BF16)], (n // TILE,), flops=4 * n * w * h)
+
+def attend_body(dp, q, k, v, g, w_out, seg_q, seg_k, cos, s1, s2, kcos, ks1, ks2, ctx, dq, dk, dv, sums, dk_acc, dv_acc):
+    step = pl.program_id(0)
+    count = k.shape[0] // TILE
+    scale = 1.0 / math.sqrt(HEAD)
+    @pl.when(step == 0)
+    def _():
+        sums[...] = jnp.zeros_like(sums)
+        dk_acc[...] = jnp.zeros_like(dk_acc)
+        dv_acc[...] = jnp.zeros_like(dv_acc)
+    d_ctx = dot(g[...], w_out[...], (1, 1)).astype(BF16)
+    def block(index):
+        reach = (index + 1) * TILE
+        keys, values = k[0:reach, :], v[0:reach, :]
+        scores = dot(q[...], keys, (1, 1)) * scale
+        row = index * TILE + lax.broadcasted_iota(jnp.int32, (TILE, reach), 0)
+        col = lax.broadcasted_iota(jnp.int32, (TILE, reach), 1)
+        allowed = (seg_q[...] == seg_k[:, 0:reach]) & (col <= row)
+        scores = jnp.where(allowed, scores, -1e30)
+        top = jnp.max(scores, axis=1, keepdims=True)
+        weights = jnp.where(allowed, jnp.exp(scores - top), 0.0)
+        inverse = 1.0 / jnp.sum(weights, axis=1, keepdims=True)
+        context = dot(weights.astype(BF16), values, (1, 0)) * inverse
+        ctx[...] = context.astype(BF16)
+        delta = jnp.sum(d_ctx.astype(F32) * context, axis=1, keepdims=True)
+        probs = weights * inverse
+        d_probs = dot(d_ctx, values, (1, 1))
+        d_scores = (probs * (d_probs - delta)).astype(BF16)
+        d_q = dot(d_scores, keys, (1, 0)) * scale
+        low = turn(d_q, cos[...], -s1[...], -s2[...]).astype(BF16)
+        dq[...] = low
+        sums[:, 0:HEAD] += jnp.sum(low.astype(F32), axis=0, keepdims=True)
+        dk_acc[0:reach, :] += dot(d_scores, q[...], (0, 0))
+        dv_acc[0:reach, :] += dot(probs.astype(BF16), d_ctx, (0, 0))
+    for index in range(count):
+        @pl.when(step == index)
+        def _(index=index):
+            block(index)
+    @pl.when(step == count - 1)
+    def _():
+        low_k = turn(dk_acc[...] * scale, kcos[...], -ks1[...], -ks2[...]).astype(BF16)
+        low_v = dv_acc[...].astype(BF16)
+        dk[...] = low_k
+        dv[...] = low_v
+        sums[:, HEAD:2 * HEAD] = jnp.sum(low_k.astype(F32), axis=0, keepdims=True)
+        sums[:, 2 * HEAD:] = jnp.sum(low_v.astype(F32), axis=0, keepdims=True)
+
+def attend(dp, q, k, v, g, w_out, seg_col, seg_row, tables):
+    n = q.shape[0]; w = g.shape[1]
+    return run(attend_body, "attend", dp, [q, k, v, g, w_out, seg_col, seg_row, *tables, *tables],
+        [tile(HEAD), whole(k.shape), whole(v.shape), tile(w), whole(w_out.shape), tile(1), whole(seg_row.shape)] + [tile(128)] * 3 + [whole((n, 128))] * 3,
+        [shape((n, HEAD), BF16)] * 4 + [shape((1, 3 * HEAD), F32)],
+        [tile(HEAD)] * 2 + [whole((n, HEAD))] * 2 + [whole((1, 3 * HEAD))],
+        [pltpu.VMEM((n, HEAD), F32)] * 2, (n // TILE,), flops=2 * n * w * HEAD + 7 * n * n * HEAD)
+
+def output_body(dp, ctx, active, w_out, d0, dx, dy, d1, d2, out, full):
+    @pl.when(pl.program_id(0) == 0)
+    def _():
+        fill(dp[0], full, (d0, dx, dy, d1, d2), None, full.shape[0] // 4)
+    out[...] = (dot(ctx[...], w_out[...], (1, 0)) + dot(active[...], full[...], (1, 0))).astype(BF16)
+
+def output(dp, ctx, active, w_out, down):
+    n, h = active.shape; w = w_out.shape[1]
+    return run(output_body, "output", dp, [ctx, active, w_out, *down],
+        [tile(HEAD), tile(h), whole(w_out.shape)] + [whole(p.shape) for p in down],
+        [shape((n, w), BF16)], [tile(w)], [pltpu.VMEM((h, w), BF16)], (n // TILE,), flops=2 * n * w * (h + HEAD))[0]
+
+def inward_body(dp, x, dq, dk, dv, d_hidden, w0, wx, wy, w1, w2, u0, ux, uy, u1, u2, vec, u, sums, full_qkv, full_up):
+    @pl.when(pl.program_id(0) == 0)
+    def _():
+        fill(dp[0], full_qkv, (w0, wx, wy, w1, w2), w0.shape[0])
+        fill(dp[0], full_up, (u0, ux, uy, u1, u2), u0.shape[0])
+        sums[...] = jnp.zeros_like(sums)
+    normed, _ = norm_tile(x[...])
+    d_joined = jnp.concatenate([dq[...], dk[...], dv[...]], axis=1)
+    d_first = dot(d_joined, full_qkv[...], (1, 1))
+    d_second = dot(d_hidden[...], full_up[...], (1, 1))
+    u[...] = (d_first * vec[0:1, :] + d_second * vec[2:3, :]).astype(BF16)
+    sums[0:1, :] += jnp.sum(d_first * normed, axis=0, keepdims=True)
+    sums[1:2, :] += jnp.sum(d_first, axis=0, keepdims=True)
+    sums[2:3, :] += jnp.sum(d_second * normed, axis=0, keepdims=True)
+    sums[3:4, :] += jnp.sum(d_second, axis=0, keepdims=True)
+
+def inward(dp, x, dq, dk, dv, d_hidden, wq, up, vec):
+    n, w = x.shape; h = d_hidden.shape[1]
+    return run(inward_body, "inward", dp, [x, dq, dk, dv, d_hidden, *wq, *up, vec],
+        [tile(w)] + [tile(HEAD)] * 3 + [tile(h)] + [whole(p.shape) for p in (*wq, *up, vec)],
+        [shape((n, w), BF16), shape((4, w), F32)], [tile(w), whole((4, w))],
+        [pltpu.VMEM((w, 3 * HEAD), BF16), pltpu.VMEM((w, h), BF16)], (n // TILE,), flops=2 * n * w * (h + 3 * HEAD))
+
+ORDER = (3, 1, 2, 0)
+def terms_body(count, dp, left, *refs):
+    rights, outs = refs[:count], refs[count:]
+    step = pl.program_id(0)
+    right = rights[0][...] if count == 1 else jnp.concatenate([r[...] for r in rights], axis=1)
+    for place in range(4):
+        @pl.when(step == place)
+        def _(place=place):
+            term = dot(left[...], right, (0, 0)).astype(BF16)
+            if place == 3:
+                outs[6][...] = term
+            else:
+                half = term.shape[0] // 2
+                outs[2 * place][...] = term[:half]
+                outs[2 * place + 1][...] = term[half:]
+
+def order_mask(step):
+    return jnp.where(step == 0, 3, jnp.where(step == 3, 0, step))
+
+def terms(dp, left, rights, name):
+    n, w = left.shape; rows = w // 4; cols = sum(r.shape[1] for r in rights)
+    outs = [shape((rows // 2, cols), BF16)] * 6 + [shape((rows, cols), BF16)]
+    return run(functools.partial(terms_body, len(rights)), name, dp, [left, *rights],
+        [pl.BlockSpec((n, rows), lambda i, d: (0, d[0] ^ order_mask(i)))] + [whole(r.shape) for r in rights],
+        outs, [whole(o.shape) for o in outs], [], (4,), flops=2 * n * w * cols)
+
+
+def up_blocks_body(source, out):
+    for rank in range(HEADS):
+        for group in range(4):
+            at = (group * HEADS + rank) * 256
+            out[rank, :, group * 256 : group * 256 + 256] = source[:, at : at + 256]
+
+
+def qkv_blocks_body(source, out):
+    for rank in range(HEADS):
+        for part in range(3):
+            at = (part * HEADS + HEAD_ORDER[rank]) * HEAD
+            out[rank, :, part * HEAD : part * HEAD + HEAD] = source[:, at : at + HEAD]
+
+
+def up_rows_body(source, out):
+    for rank in range(HEADS):
+        for group in range(4):
+            at = (group * HEADS + rank) * 256
+            out[:, at : at + 256] = source[rank, :, group * 256 : group * 256 + 256].astype(F32)
+
+
+def qkv_rows_body(source, out):
+    for rank in range(HEADS):
+        for part in range(3):
+            at = (part * HEADS + HEAD_ORDER[rank]) * HEAD
+            out[:, at : at + HEAD] = source[rank, :, part * HEAD : part * HEAD + HEAD].astype(F32)
+
+
+def repack(body, name, source, out):
+    return pl.pallas_call(
+        body,
+        name=name,
+        out_shape=out,
+        compiler_params=pltpu.CompilerParams(vmem_limit_bytes=16 * 2**20),
+        cost_estimate=pl.CostEstimate(
+            flops=0,
+            bytes_accessed=source.size * source.dtype.itemsize * 3,
+            transcendentals=0,
+        ),
+    )(source)
+
+
+def over_x(block):
+    return lax.ppermute(block, "dp", swap(4, 1))
+
+
+def over_y(block):
+    return lax.ppermute(block, "dp", swap(4, 2))
+
+
+def gather_pieces(block, cut):
+    along_x = over_x(block)
+    along_y = over_y(block)
+    return (block, along_x, along_y, over_x(along_y[:cut]), over_y(along_x[cut:]))
+
+
+def reduce_pieces(pieces):
+    far_top, far_low, x_top, x_low, y_top, y_low, own = pieces
+    half = far_top.shape[0]
+    far_x = over_x(far_top)
+    far_y = over_y(far_low)
+    got_x_top = over_x(x_top)
+    got_y_low = over_y(y_low)
+    got_y_top = over_y((y_top.astype(F32) + far_x.astype(F32)).astype(BF16))
+    got_x_low = over_x((x_low.astype(F32) + far_y.astype(F32)).astype(BF16))
+    top = own[:half].astype(F32) + got_x_top.astype(F32) + got_y_top.astype(F32)
+    low = own[half:].astype(F32) + got_x_low.astype(F32) + got_y_low.astype(F32)
+    return top, low
+
+
+def rotary_lanes(length):
+    position = jnp.arange(length, dtype=jnp.int32).astype(F32)
+    cosine, sine = rotary_tables(position)
+    blank = jnp.zeros((length, 32), F32)
+    rest = jnp.zeros((length, 64), F32)
+    cos = jnp.concatenate([cosine, jnp.ones((length, 64), F32)], axis=1)
+    first = jnp.concatenate([-sine[:, :32], blank, rest], axis=1)
+    second = jnp.concatenate([blank, sine[:, 32:], rest], axis=1)
+    return cos, first, second
+
+
+def line_shards(
+    block_input,
+    segments,
+    out_grad,
+    ln1_gain,
+    ln1_bias,
+    w_qkv,
+    b_qkv,
+    w_attn_out,
+    b_attn_out,
+    ln2_gain,
+    ln2_bias,
+    w_up,
+    b_up,
+    w_down,
+    b_down,
+):
+    dp, sp = lax.axis_index("dp"), lax.axis_index("sp")
+    dp = dp.astype(jnp.int32)
+    x_own = block_input[0]
+    g_own = out_grad[0]
+    tokens, width = x_own.shape
+    length = tokens * HEADS
+    rows = w_qkv.shape[0]
+    everywhere = ("dp", "sp")
+    head = head_of(sp)
+
+    x_all = lax.all_gather(x_own, "sp", axis=0, tiled=True)
+    down = gather_pieces(jnp.concatenate([w_down, w_attn_out], axis=0), w_down.shape[0] // 2)
+    up_blocks = repack(
+        up_blocks_body, "up_blocks", w_up, jax.ShapeDtypeStruct((HEADS, rows, 1024), BF16)
+    )
+    up_rows = lax.all_to_all(up_blocks, "sp", 0, 0, tiled=True).reshape(HEADS * rows, 1024)
+    packed = jnp.concatenate(
+        [
+            jnp.stack([ln1_gain, ln1_bias, ln2_gain, ln2_bias, b_attn_out, b_down]),
+            b_qkv.reshape(3, 64),
+            b_up.reshape(4, 64),
+            segments[0].astype(BF16).reshape(2, 64),
+        ]
+    )
+    small = lax.all_to_all(
+        jnp.broadcast_to(packed[None], (32,) + packed.shape), everywhere, 0, 0, tiled=True
+    )
+    up = gather_pieces(up_rows, HEADS * rows // 2)
+    qkv_blocks = repack(
+        qkv_blocks_body, "qkv_blocks", w_qkv, jax.ShapeDtypeStruct((HEADS, rows, 768), BF16)
+    )
+    qkv_rows = lax.all_to_all(qkv_blocks, "sp", 0, 0, tiled=True).reshape(HEADS * rows, 768)
+    w_in = gather_pieces(qkv_rows, HEADS * rows // 2)
+    g_all = lax.all_gather(g_own, "sp", axis=0, tiled=True)
+    cut = w_down.shape[0] // 2
+    out_parts = [piece[2 * cut :] for piece in down[:3]] + [down[4][cut:]]
+    out_rows = jnp.zeros((4, rows, width), BF16)
+    for mask, piece in enumerate(out_parts):
+        out_rows = put(out_rows, piece, dp ^ mask)
+    fours = [[0, 1, 2, 3], [4, 5, 6, 7]]
+    w_out = lax.all_to_all(
+        out_rows, "sp", 0, 0, tiled=True, axis_index_groups=fours
+    ).reshape(HEAD, width)
+
+    vectors = small[:, :6].transpose(1, 0, 2).reshape(6, width).astype(F32)
+    norm_vec = vectors[:4]
+    bias_qkv = pick(small[:, 6:9].reshape(3, HEADS, HEAD), head, 1).astype(F32).reshape(1, 768)
+    bias_up = pick(small[:, 9:13].reshape(4, HEADS, 256), sp, 1).astype(F32).reshape(1, 1024)
+    seg = pick(small[:, 13:].reshape(4, length), dp).astype(F32)
+    tables = rotary_lanes(length)
+
+    first_in, second_in = norms(dp, x_all, norm_vec)
+    active, d_hidden, up_sums = mlp(dp, second_in, g_all, up, down, bias_up)
+    down_terms = terms(dp, active, [g_all], "down_terms")
+    up_terms = terms(dp, second_in, [d_hidden], "up_terms")
+    queries, key_rows, value_rows = qkv(dp, first_in, w_in, bias_qkv, tables)
+    context, d_q, d_k, d_v, qkv_sums = attend(
+        dp,
+        queries,
+        key_rows,
+        value_rows,
+        g_all,
+        w_out,
+        seg.reshape(length, 1),
+        seg.reshape(1, length),
+        tables,
+    )
+    out_terms = output(dp, context, active, w_out, down)
+    out_sum = lax.psum_scatter(out_terms, "sp", scatter_dimension=0, tiled=True)
+    u_terms, norm_sums = inward(dp, x_all, d_q, d_k, d_v, d_hidden, w_in, up, norm_vec)
+    u_sum = lax.psum_scatter(u_terms, "sp", scatter_dimension=0, tiled=True)
+    qkv_terms = terms(dp, first_in, [d_q, d_k, d_v], "qkv_terms")
+    attn_terms = dot(context, g_all, (0, 0)).astype(BF16).reshape(4, HEAD // 4, width)
+    attn_terms = lax.all_to_all(
+        attn_terms, "sp", 0, 0, tiled=True, axis_index_groups=fours
+    )
+
+    grad_down = jnp.concatenate(reduce_pieces(down_terms), axis=0)
+    up_sum = jnp.concatenate([half.astype(BF16) for half in reduce_pieces(up_terms)], axis=0)
+    up_back = lax.all_to_all(up_sum.reshape(HEADS, rows, 1024), "sp", 0, 0, tiled=True)
+    grad_up = repack(
+        up_rows_body, "up_rows", up_back, jax.ShapeDtypeStruct((rows, HEADS * 1024), F32)
+    )
+    own, to_x, to_y, to_far = (pick(attn_terms, dp ^ mask) for mask in range(4))
+    part = rows // 2
+    grad_out = jnp.concatenate(
+        reduce_pieces(
+            (
+                to_far[:part],
+                to_far[part:],
+                to_x[:part],
+                to_x[part:],
+                to_y[:part],
+                to_y[part:],
+                own,
+            )
+        ),
+        axis=0,
+    )
+    qkv_sum = jnp.concatenate([half.astype(BF16) for half in reduce_pieces(qkv_terms)], axis=0)
+    qkv_back = lax.all_to_all(qkv_sum.reshape(HEADS, rows, 768), "sp", 0, 0, tiled=True)
+    grad_qkv = repack(
+        qkv_rows_body, "qkv_rows", qkv_back, jax.ShapeDtypeStruct((rows, HEADS * 768), F32)
+    )
+
+    x_wide = x_own.astype(F32)
+    block_output = (x_wide + out_sum.astype(F32) + (vectors[4] + vectors[5]))[None]
+    u_wide = u_sum.astype(F32)
+    normed, scale = normalize(x_wide)
+    u_mean = jnp.mean(u_wide, axis=-1, keepdims=True)
+    u_along = jnp.mean(u_wide * normed, axis=-1, keepdims=True)
+    input_grad = (g_own.astype(F32) + (u_wide - u_mean - normed * u_along) * scale)[None]
+
+    sum_qkv = lax.dynamic_update_slice(
+        jnp.zeros((3, HEADS, HEAD), F32), qkv_sums.reshape(3, 1, HEAD), (0, head, 0)
+    )
+    sum_up = lax.dynamic_update_slice(
+        jnp.zeros((4, HEADS, 256), F32), up_sums.reshape(4, 1, 256), (0, sp, 0)
+    )
+    sum_out = jnp.sum(g_own.astype(F32), axis=0)
+    totals = jnp.concatenate(
+        [
+            norm_sums.reshape(4, 32, 64).transpose(1, 0, 2).reshape(32, 256),
+            sum_out.reshape(32, 64),
+            sum_qkv.reshape(32, 192),
+            sum_up.reshape(32, 256),
+        ],
+        axis=1,
+    )
+    owned = jnp.sum(lax.all_to_all(totals, everywhere, 0, 0, tiled=True), axis=0)
+    grad_g1, grad_s1, grad_g2, grad_s2, grad_bout = (
+        owned[k * rows : (k + 1) * rows] for k in range(5)
+    )
+    return (
+        block_output,
+        input_grad,
+        grad_g1,
+        grad_s1,
+        grad_qkv,
+        owned[320:512],
+        grad_out,
+        grad_bout,
+        grad_g2,
+        grad_s2,
+        grad_up,
+        owned[512:],
+        grad_down,
+        grad_bout,
+    )
+
+
+def shards(*arrays):
+    if (lax.axis_size("dp"), lax.axis_size("sp")) == (4, 8):
+        return line_shards(*arrays)
+    return any_shards(*arrays)
+
+
 def solution(mesh):
     tokens = P("dp", "sp", None)
     split = P(("dp", "sp"))

time: 696 us -> 413 us (0.59)
  waiting for transfers between devices: 285 us -> 145 us
  Pallas kernels: 0 us -> 103 us
  matrix products: 94.6 us -> 2.24 us
  starting transfers between devices: 154 us -> 79.1 us
  local copies, waits for them, and re-layouts: 93.9 us -> 32.1 us
  other arithmetic: 55 us -> 32.5 us
  between operations: 2.84 us -> 14.6 us
    ppermute x104 -> x36, waiting for transfers between devices: 285 us -> 74.8 us  [the longest x18 45.1 us: over_y(): return lax.ppermute(block, 'dp', swap(4, 2))]
    ppermute x104 -> x36, starting transfers between devices: 154 us -> 41.9 us  [the longest x18 21.8 us: over_y(): return lax.ppermute(block, 'dp', swap(4, 2))]
    pallas_call x0 -> x13, Pallas kernels: none -> 103 us  [the longest x9 98.3 us: run(): pl.pallas_call(body, name=name, grid_spec=pltpu.PrefetchScalarGridSpec(nu...]
    dot_general x18 -> x1, matrix products: 94.6 us -> 2.24 us  [dot(): lax.dot_general(left, right, (((contract[0],), (contract[1],)), ((), ()))...]
    all_to_all x0 -> x8, waiting for transfers between devices: none -> 68.7 us  [the longest x1 36 us: line_shards(): lax.all_to_all(qkv_blocks, 'sp', 0, 0, tiled=True)]
    all_to_all x0 -> x8, starting transfers between devices: none -> 36.5 us  [the longest x1 7.3 us: line_shards(): lax.all_to_all(jnp.broadcast_to(packed[None], (32,) + packed.shape), ever...]
    concatenate x9 -> x4, local copies, waits for them, and re-layouts: 15.7 us -> 2.49 us  [the longest x1 0.87 us: line_shards(): jnp.concatenate([jnp.stack([ln1_gain, ln1_bias, ln2_gain, ln2_bias, b_att...]
    squeeze x12 -> x0, local copies, waits for them, and re-layouts: 11.2 us -> none  [pick(): return lax.dynamic_index_in_dim(array, index, axis, keepdims=False)]
  transfers between devices with their start and end apart: 104 -> 48, of which waited for: 51 -> 18; matrix products, arithmetic and copies ran while one was open for 18% -> 14% of each run, Pallas kernels for 0% -> 18%
where the time goes in v2:
time: 413 us; the launch traced here: 409 us
  waiting for transfers between devices  145 us (35%)
  Pallas kernels  103 us (25%)
  starting transfers between devices  79.1 us (19%)
  other arithmetic  32.5 us (8%)
  local copies, waits for them, and re-layouts  32.1 us (8%)
  between operations  14.6 us (4%)
    pallas_call x9, Pallas kernels, run(): pl.pallas_call(body, name=name, grid_spec=pltpu.PrefetchScalarGridSpec(nu...  98.3 us
    ppermute x18, waiting for transfers between devices, over_y(): return lax.ppermute(block, 'dp', swap(4, 2))  45.1 us
    all_to_all x1, waiting for transfers between devices, line_shards(): lax.all_to_all(qkv_blocks, 'sp', 0, 0, tiled=True)  36 us
    ppermute x18, waiting for transfers between devices, over_x(): return lax.ppermute(block, 'dp', swap(4, 1))  29.7 us
    ppermute x18, starting transfers between devices, over_y(): return lax.ppermute(block, 'dp', swap(4, 2))  21.8 us
    ppermute x18, starting transfers between devices, over_x(): return lax.ppermute(block, 'dp', swap(4, 1))  20.1 us
    all_to_all x1, waiting for transfers between devices, line_shards(): lax.all_to_all(up_blocks, 'sp', 0, 0, tiled=True)  19 us
    unnamed x60, local copies, waits for them, and re-layouts  8.92 us
  transfers between devices with their start and end apart: 48, of which 18 were waited for; matrix products, arithmetic and copies ran while one was open for 14% of the time, Pallas kernels for 18%

profile of v2, /device:TPU:0, one launch (start us, length us, event | category | flops | bytes accessed | tf_op | source)
XLA Modules:
  0.0 408.6 jit_solution(2598611950551953127)
XLA Ops:
  12.6 7.3 %all-to-all-start = ((bf16[32,2,480]{2,1,0:T(2,128)(2,1)}), bf16[32,2,480]{2,1,0:T(2,128)(2,1)S(1)}, u32[]{:S(2)}, u32[]{:S(2)}) async-start(bf16[32,2,480]{2,1,0:T(2,128)(2,1)} %reshape.238), calls=%async_computation | async-start | bytes 131072 | tf_op jit(solution)/shard_map/all_to_all | solution.py:650
  22.0 5.6 %all-to-all-done = bf16[32,2,480]{2,1,0:T(2,128)(2,1)S(1)} async-done(((bf16[32,2,480]{2,1,0:T(2,128)(2,1)}), bf16[32,2,480]{2,1,0:T(2,128)(2,1)S(1)}, u32[]{:S(2)}, u32[]{:S(2)}) %all-to-all-start) | async-done | bytes 61472 | tf_op jit(solution)/shard_map/all_to_all | solution.py:650
  36.1 36.0 %all-to-all-done.1 = bf16[8,64,768]{2,1,0:T(8,128)(2,1)S(1)} async-done(((bf16[8,64,768]{2,1,0:T(8,128)(2,1)}), bf16[8,64,768]{2,1,0:T(8,128)(2,1)S(1)}, u32[]{:S(2)}, u32[]{:S(2)}) %all-to-all-start.1) | async-done | bytes 786464 | tf_op jit(solution)/shard_map/all_to_all | solution.py:657
  85.7 13.5 %collective-permute-done.6.d2 = bf16[192,2048]{1,0:T(8,128)(2,1)S(1)} collective-permute-done((bf16[192,2048]{1,0:T(8,128)(2,1)S(1)}, bf16[192,2048]{1,0:T(8,128)(2,1)S(1)}, u32[]{:S(2)}, u32[]{:S(2)}) %collective-permute-start.6) | collective-permute-done | bytes 786464 | tf_op jit(solution)/shard_map/ppermute | solution.py:575
  100.8 19.0 %all-to-all-done.3 = bf16[8,64,1024]{2,1,0:T(8,128)(2,1)S(1)} async-done(((bf16[8,64,1024]{2,1,0:T(8,128)(2,1)}), bf16[8,64,1024]{2,1,0:T(8,128)(2,1)S(1)}, u32[]{:S(2)}, u32[]{:S(2)}) %all-to-all-start.3) | async-done | bytes 1048608 | tf_op jit(solution)/shard_map/all_to_all | solution.py:641
  119.8 4.3 %all-to-all-start.2 = ((bf16[4,64,2048]{2,1,0:T(8,128)(2,1)}), bf16[4,64,2048]{2,1,0:T(8,128)(2,1)}, u32[]{:S(2)}, u32[]{:S(2)}) async-start(bf16[4,64,2048]{2,1,0:T(8,128)(2,1)} %fusion.15), calls=%async_computation.2 | async-start | bytes 2097152 | tf_op jit(solution)/shard_map/all_to_all | solution.py:666
  143.0 9.9 %collective-permute-done.8.uy = bf16[512,1024]{1,0:T(8,128)(2,1)} collective-permute-done((bf16[512,1024]{1,0:T(8,128)(2,1)S(1)}, bf16[512,1024]{1,0:T(8,128)(2,1)}, u32[]{:S(2)}, u32[]{:S(2)}) %collective-permute-start.8) | collective-permute-done | bytes 1048608 | tf_op jit(solution)/shard_map/ppermute | solution.py:575
  158.1 7.7 %norms.1 = (bf16[1024,2048]{1,0:T(8,128)(2,1)}, bf16[1024,2048]{1,0:T(8,128)(2,1)}) custom-call(s32[1]{0:T(128)} %bitcast.1.dp, bf16[1024,2048]{1,0:T(8,128)(2,1)} %bitcast.114, f32[4,2048]{1,0:T(4,128)} %slice.140.vec), custom_call_target="tpu_custom_call" | custom-call | bytes 12615680 | tf_op jit(solution)/shard_map/norms/pallas_call | solution.py:342
  166.5 8.0 %qkv.1 = (bf16[1024,256]{1,0:T(8,128)(2,1)}, bf16[1024,256]{1,0:T(8,128)(2,1)}, bf16[1024,256]{1,0:T(8,128)(2,1)}) custom-call(s32[1]{0:T(128)} %bitcast.1.dp, bf16[1024,2048]{1,0:T(8,128)(2,1)} %get-tuple-element.50.first.left, bf16[512,768]{1,0:T(8,128)(2,1)} %bitcast.124, bf16[512,768]{1,0:T(8,128)(2,1)} %collective-permute-done.wx, ...), custom_call_target="tpu_custom_call" | custom-call | flops 3221225472 | bytes 10488832 | tf_op jit(solution)/shard_map/qkv/pallas_call | solution.py:342
  174.5 11.7 %attend.1 = (bf16[1024,256]{1,0:T(8,128)(2,1)}, bf16[1024,256]{1,0:T(8,128)(2,1)}, bf16[1024,256]{1,0:T(8,128)(2,1)}, bf16[1024,256]{1,0:T(8,128)(2,1)}, f32[1,768]{1,0:T(1,128)}) custom-call(s32[1]{0:T(128)} %bitcast.1.dp, bf16[1024,256]{1,0:T(8,128)(2,1)} %get-tuple-element.51.q, bf16[1024,256]{1,0:T(8,128)(2,1)} %get-tuple-element.52.k, ...), custom_call_target="tpu_custom_call" | custom-call | flops 2952790016 | bytes 12069888 | tf_op jit(solution)/shard_map/attend/pallas_call | solution.py:342
  187.1 15.4 %mlp.1 = (bf16[1024,1024]{1,0:T(8,128)(2,1)}, bf16[1024,1024]{1,0:T(8,128)(2,1)}, f32[1,1024]{1,0:T(1,128)}) custom-call(s32[1]{0:T(128)} %bitcast.1.dp, bf16[1024,2048]{1,0:T(8,128)(2,1)} %get-tuple-element.55.second.left, bf16[1024,2048]{1,0:T(8,128)(2,1)} %bitcast.139, bf16[512,1024]{1,0:T(8,128)(2,1)} %bitcast.120, ...), custom_call_target="tpu_custom_call" | custom-call | flops 8589934592 | bytes 22028288 | tf_op jit(solution)/shard_map/mlp/pallas_call | solution.py:342
  202.5 16.0 %inward.1 = (bf16[1024,2048]{1,0:T(8,128)(2,1)}, f32[4,2048]{1,0:T(4,128)}) custom-call(s32[1]{0:T(128)} %bitcast.1.dp, bf16[1024,2048]{1,0:T(8,128)(2,1)} %bitcast.115, bf16[1024,256]{1,0:T(8,128)(2,1)} %get-tuple-element.57.dq.refs_0_, bf16[1024,256]{1,0:T(8,128)(2,1)} %get-tuple-element.58.dk.refs_1_, bf16[1024,256]{1,0:T(8,128)(2,1)} %get-tuple-element.59.dv.refs_2_, ...), custom_call_target="tpu_custom_call" | custom-call | flops 7516192768 | bytes 19464192 | tf_op jit(solution)/shard_map/inward/pallas_call | solution.py:342
  219.7 10.5 %output.1 = bf16[1024,2048]{1,0:T(8,128)(2,1)} custom-call(s32[1]{0:T(128)} %bitcast.1.dp, bf16[1024,256]{1,0:T(8,128)(2,1)} %get-tuple-element.54.ctx, bf16[1024,1024]{1,0:T(8,128)(2,1)} %get-tuple-element.56.active.left, bf16[256,2048]{1,0:T(8,128)(2,1)} %bitcast.17.w_out, bf16[320,2048]{1,0:T(8,128)(2,1)} %constant_dynamic-update-slice_fusion.d0, ...), custom_call_target="tpu_custom_call" | custom-call | flops 5368709120 | bytes 13107200 | tf_op jit(solution)/shard_map/output/pallas_call | solution.py:342
  232.0 8.2 %qkv_terms.1 = (bf16[256,768]{1,0:T(8,128)(2,1)}, bf16[256,768]{1,0:T(8,128)(2,1)}, bf16[256,768]{1,0:T(8,128)(2,1)}, bf16[256,768]{1,0:T(8,128)(2,1)}, bf16[256...) custom-call(s32[1]{0:T(128)} %bitcast.1.dp, ...), custom_call_target="tpu_custom_call" | custom-call | flops 3221225472 | bytes 8912896 | tf_op jit(solution)/shard_map/qkv_terms/pallas_call | solution.py:342
  242.0 4.4 %all-to-all-start.4 = ((f32[32,1,768]{2,1,0:T(1,128)}), f32[32,1,768]{2,1,0:T(1,128)S(1)}, u32[]{:S(2)}, u32[]{:S(2)}) async-start(f32[32,1,768]{2,1,0:T(1,128)} %copy.40), calls=%async_computation.6 | async-start | bytes 196608 | tf_op jit(solution)/shard_map/all_to_all | solution.py:755
  246.4 11.0 %down_terms.1 = (bf16[128,2048]{1,0:T(8,128)(2,1)}, bf16[128,2048]{1,0:T(8,128)(2,1)}, bf16[128,2048]{1,0:T(8,128)(2,1)}, bf16[128,2048]{1,0:T(8,128)(2,1)}, bf1...) custom-call(s32[1]{0:T(128)} %bitcast.1.dp, ...), custom_call_target="tpu_custom_call" | custom-call | flops 4294967296 | bytes 10485760 | tf_op jit(solution)/shard_map/down_terms/pallas_call | solution.py:342
  259.6 9.8 %up_terms.1 = (bf16[256,1024]{1,0:T(8,128)(2,1)}, bf16[256,1024]{1,0:T(8,128)(2,1)}, bf16[256,1024]{1,0:T(8,128)(2,1)}, bf16[256,1024]{1,0:T(8,128)(2,1)}, bf16[...) custom-call(s32[1]{0:T(128)} %bitcast.1.dp, ...), custom_call_target="tpu_custom_call" | custom-call | flops 4294967296 | bytes 10485760 | tf_op jit(solution)/shard_map/up_terms/pallas_call | solution.py:342
  286.2 6.5 %collective-permute-done.31 = bf16[128,2048]{1,0:T(8,128)(2,1)S(1)} collective-permute-done((bf16[128,2048]{1,0:T(8,128)(2,1)}, bf16[128,2048]{1,0:T(8,128)(2,1)S(1)}, u32[]{:S(2)}, u32[]{:S(2)}) %collective-permute-start.31) | collective-permute-done | bytes 524320 | tf_op jit(solution)/shard_map/ppermute | solution.py:571
  296.1 7.3 %collective-permute-done.25 = bf16[256,1024]{1,0:T(8,128)(2,1)S(1)} collective-permute-done((bf16[256,1024]{1,0:T(8,128)(2,1)}, bf16[256,1024]{1,0:T(8,128)(2,1)S(1)}, u32[]{:S(2)}, u32[]{:S(2)}) %collective-permute-start.25) | collective-permute-done | bytes 524320 | tf_op jit(solution)/shard_map/ppermute | solution.py:571
  323.8 5.3 %all-to-all-start.5 = ((bf16[8,64,768]{2,1,0:T(8,128)(2,1)}), bf16[8,64,768]{2,1,0:T(8,128)(2,1)S(1)}, u32[]{:S(2)}, u32[]{:S(2)}) async-start(bf16[8,64,768]{2,1,0:T(8,128)(2,1)} %bitcast.117), calls=%async_computation.7 | async-start | bytes 1572864 | tf_op jit(solution)/shard_map/all_to_all | solution.py:726
  335.6 9.8 %collective-permute-done.26 = bf16[256,1024]{1,0:T(8,128)(2,1)} collective-permute-done((bf16[256,1024]{1,0:T(8,128)(2,1)}, bf16[256,1024]{1,0:T(8,128)(2,1)}, u32[]{:S(2)}, u32[]{:S(2)}) %collective-permute-start.26) | collective-permute-done | bytes 524320 | tf_op jit(solution)/shard_map/ppermute | solution.py:575
  351.4 10.4 %collective-permute-done.19 = bf16[32,2048]{1,0:T(8,128)(2,1)S(1)} collective-permute-done((bf16[32,2048]{1,0:T(8,128)(2,1)S(1)}, bf16[32,2048]{1,0:T(8,128)(2,1)S(1)}, u32[]{:S(2)}, u32[]{:S(2)}) %collective-permute-start.19) | collective-permute-done | bytes 131104 | tf_op jit(solution)/shard_map/ppermute | solution.py:571
  363.9 4.7 %all-to-all-start.7 = ((bf16[8,64,1024]{2,1,0:T(8,128)(2,1)}), bf16[8,64,1024]{2,1,0:T(8,128)(2,1)S(1)}, u32[]{:S(2)}, u32[]{:S(2)}) async-start(bf16[8,64,1024]{2,1,0:T(8,128)(2,1)} %bitcast.116), calls=%async_computation.9 | async-start | bytes 2097152 | tf_op jit(solution)/shard_map/all_to_all | solution.py:705
  387.1 8.1 %all-to-all-done.7.source = bf16[8,64,1024]{2,1,0:T(8,128)(2,1)S(1)} async-done(((bf16[8,64,1024]{2,1,0:T(8,128)(2,1)}), bf16[8,64,1024]{2,1,0:T(8,128)(2,1)S(1)}, u32[]{:S(2)}, u32[]{:S(2)}) %all-to-all-start.7) | async-done | bytes 1048608 | tf_op jit(solution)/shard_map/all_to_all | solution.py:705
  (237 shorter events, 143.6 us)
Async XLA Ops:
  7.2 150.9 %all-gather.5.cloned.1.call-start = ((), (), s32[]{:S(2)}) async-start(), calls=%async_computation.12 | async-start | bytes 4718592 | tf_op jit(solution)/shard_map/all_gather | solution.py:636
  7.9 166.6 %all-gather.7.cloned.1.call-start = ((), (), s32[]{:S(2)}) async-start(), calls=%async_computation.13 | async-start | bytes 4718592 | tf_op jit(solution)/shard_map/all_gather | solution.py:659
  27.6 44.6 %all-to-all-start.1 = ((bf16[8,64,768]{2,1,0:T(8,128)(2,1)}), bf16[8,64,768]{2,1,0:T(8,128)(2,1)S(1)}, u32[]{:S(2)}, u32[]{:S(2)}) async-start(bf16[8,64,768]{2,1,0:T(8,128)(2,1)} %qkv_blocks.1), calls=%async_computation.1 | async-start | bytes 1572864 | tf_op jit(solution)/shard_map/all_to_all | solution.py:657
  32.9 44.6 %collective-permute-start.4 = (bf16[320,2048]{1,0:T(8,128)(2,1)}, bf16[320,2048]{1,0:T(8,128)(2,1)}, u32[]{:S(2)}, u32[]{:S(2)}) collective-permute-start(bf16[320,2048]{1,0:T(8,128)(2,1)} %constant_dynamic-update-slice_fusion.d0), channel_id=1, source_target_pairs={{0,8},{8,0},{16,24},{24,16},{1,9},{9,1},{17,25},{25,17},{2,10},{10... | collective-permute-start | bytes 3932168 | tf_op jit(solution)/shard_map/ppermute | solution.py:571
  34.0 48.0 %collective-permute-start.5 = (bf16[320,2048]{1,0:T(8,128)(2,1)}, bf16[320,2048]{1,0:T(8,128)(2,1)}, u32[]{:S(2)}, u32[]{:S(2)}) collective-permute-start(bf16[320,2048]{1,0:T(8,128)(2,1)} %constant_dynamic-update-slice_fusion.d0), channel_id=1, source_target_pairs={{0,16},{8,24},{16,0},{24,8},{1,17},{9,25},{17,1},{25,9},{2,18},{10... | collective-permute-start | bytes 3932168 | tf_op jit(solution)/shard_map/ppermute | solution.py:575
  72.2 47.6 %all-to-all-start.3 = ((bf16[8,64,1024]{2,1,0:T(8,128)(2,1)}), bf16[8,64,1024]{2,1,0:T(8,128)(2,1)S(1)}, u32[]{:S(2)}, u32[]{:S(2)}) async-start(bf16[8,64,1024]{2,1,0:T(8,128)(2,1)} %up_blocks.1), calls=%async_computation.3 | async-start | bytes 2097152 | tf_op jit(solution)/shard_map/all_to_all | solution.py:641
  83.6 50.3 %collective-permute-start.1 = (bf16[512,768]{1,0:T(8,128)(2,1)S(1)}, bf16[512,768]{1,0:T(8,128)(2,1)}, u32[]{:S(2)}, u32[]{:S(2)}) collective-permute-start(bf16[512,768]{1,0:T(8,128)(2,1)S(1)} %bitcast.122), channel_id=1, source_target_pairs={{0,16},{8,24},{16,0},{24,8},{1,17},{9,25},{17,1},{25,9},{2,18},{10... | collective-permute-start | bytes 2359304 | tf_op jit(solution)/shard_map/ppermute | solution.py:575
  84.2 52.2 %collective-permute-start = (bf16[512,768]{1,0:T(8,128)(2,1)S(1)}, bf16[512,768]{1,0:T(8,128)(2,1)}, u32[]{:S(2)}, u32[]{:S(2)}) collective-permute-start(bf16[512,768]{1,0:T(8,128)(2,1)S(1)} %bitcast.123), channel_id=1, source_target_pairs={{0,8},{8,0},{16,24},{24,16},{1,9},{9,1},{17,25},{25,17},{2,10},{10... | collective-permute-start | bytes 2359304 | tf_op jit(solution)/shard_map/ppermute | solution.py:571
  119.8 54.7 %all-to-all-start.2 = ((bf16[4,64,2048]{2,1,0:T(8,128)(2,1)}), bf16[4,64,2048]{2,1,0:T(8,128)(2,1)}, u32[]{:S(2)}, u32[]{:S(2)}) async-start(bf16[4,64,2048]{2,1,0:T(8,128)(2,1)} %fusion.15), calls=%async_computation.2 | async-start | bytes 2097152 | tf_op jit(solution)/shard_map/all_to_all | solution.py:666
  124.0 272.6 %reduce-scatter.5.cloned.1.call-start = ((), (), s32[]{:S(2)}) async-start(), calls=%async_computation.11 | async-start | bytes 4718592 | tf_op jit(solution)/shard_map/reduce_scatter | solution.py:696
  141.6 44.7 %collective-permute-start.11 = (bf16[128,2048]{1,0:T(8,128)(2,1)S(1)}, bf16[128,2048]{1,0:T(8,128)(2,1)}, u32[]{:S(2)}, u32[]{:S(2)}) collective-permute-start(bf16[128,2048]{1,0:T(8,128)(2,1)S(1)} %slice.196), channel_id=1, source_target_pairs={{0,8},{8,0},{16,24},{24,16},{1,9},{9,1},{17,25},{25,17},{2,10},{10... | collective-permute-start | bytes 1572872 | tf_op jit(solution)/shard_map/ppermute | solution.py:571
  154.1 32.2 %collective-permute-start.9 = (bf16[256,1024]{1,0:T(8,128)(2,1)S(1)}, bf16[256,1024]{1,0:T(8,128)(2,1)}, u32[]{:S(2)}, u32[]{:S(2)}) collective-permute-start(bf16[256,1024]{1,0:T(8,128)(2,1)S(1)} %slice.194), channel_id=1, source_target_pairs={{0,8},{8,0},{16,24},{24,16},{1,9},{9,1},{17,25},{25,17},{2,10},{10... | collective-permute-start | bytes 1572872 | tf_op jit(solution)/shard_map/ppermute | solution.py:571
  218.5 179.6 %reduce-scatter.3.cloned.1.call-start = ((), (), s32[]{:S(2)}) async-start(), calls=%async_computation.10 | async-start | bytes 4718592 | tf_op jit(solution)/shard_map/reduce_scatter | solution.py:694
  240.2 38.6 %collective-permute-start.13 = (bf16[256,768]{1,0:T(8,128)(2,1)}, bf16[256,768]{1,0:T(8,128)(2,1)}, u32[]{:S(2)}, u32[]{:S(2)}) collective-permute-start(bf16[256,768]{1,0:T(8,128)(2,1)} %get-tuple-element.68), channel_id=1, source_target_pairs={{0,8},{8,0},{16,24},{24,16},{1,9},{9,1},{17,25},{25,17},{2,10},{10... | collective-permute-start | bytes 1179656 | tf_op jit(solution)/shard_map/ppermute | solution.py:571
  242.0 31.5 %all-to-all-start.4 = ((f32[32,1,768]{2,1,0:T(1,128)}), f32[32,1,768]{2,1,0:T(1,128)S(1)}, u32[]{:S(2)}, u32[]{:S(2)}) async-start(f32[32,1,768]{2,1,0:T(1,128)} %copy.40), calls=%async_computation.6 | async-start | bytes 196608 | tf_op jit(solution)/shard_map/all_to_all | solution.py:755
  269.4 39.1 %collective-permute-start.12 = (bf16[256,768]{1,0:T(8,128)(2,1)}, bf16[256,768]{1,0:T(8,128)(2,1)}, u32[]{:S(2)}, u32[]{:S(2)}) collective-permute-start(bf16[256,768]{1,0:T(8,128)(2,1)} %get-tuple-element.66), channel_id=1, source_target_pairs={{0,8},{8,0},{16,24},{24,16},{1,9},{9,1},{17,25},{25,17},{2,10},{10... | collective-permute-start | bytes 1179656 | tf_op jit(solution)/shard_map/ppermute | solution.py:571
  272.7 36.4 %collective-permute-start.17 = (bf16[256,768]{1,0:T(8,128)(2,1)}, bf16[256,768]{1,0:T(8,128)(2,1)}, u32[]{:S(2)}, u32[]{:S(2)}) collective-permute-start(bf16[256,768]{1,0:T(8,128)(2,1)} %get-tuple-element.71), channel_id=1, source_target_pairs={{0,16},{8,24},{16,0},{24,8},{1,17},{9,25},{17,1},{25,9},{2,18},{10... | collective-permute-start | bytes 1179656 | tf_op jit(solution)/shard_map/ppermute | solution.py:575
  273.5 50.3 %all-to-all-start.6 = ((bf16[4,64,2048]{2,1,0:T(8,128)(2,1)}), bf16[4,64,2048]{2,1,0:T(8,128)(2,1)S(1)}, u32[]{:S(2)}, u32[]{:S(2)}) async-start(bf16[4,64,2048]{2,1,0:T(8,128)(2,1)} %bitcast.30), calls=%async_computation.8 | async-start | bytes 2097152 | tf_op jit(solution)/shard_map/all_to_all | solution.py:699
  311.6 33.8 %collective-permute-start.26 = (bf16[256,1024]{1,0:T(8,128)(2,1)}, bf16[256,1024]{1,0:T(8,128)(2,1)}, u32[]{:S(2)}, u32[]{:S(2)}) collective-permute-start(bf16[256,1024]{1,0:T(8,128)(2,1)} %add_convert_fusion.5), channel_id=1, source_target_pairs={{0,16},{8,24},{16,0},{24,8},{1,17},{9,25},{17,1},{25,9},{2,18},{10... | collective-permute-start | bytes 1572872 | tf_op jit(solution)/shard_map/ppermute | solution.py:575
  323.6 45.0 %collective-permute-start.30 = (bf16[128,2048]{1,0:T(8,128)(2,1)}, bf16[128,2048]{1,0:T(8,128)(2,1)}, u32[]{:S(2)}, u32[]{:S(2)}) collective-permute-start(bf16[128,2048]{1,0:T(8,128)(2,1)} %get-tuple-element.80), channel_id=1, source_target_pairs={{0,8},{8,0},{16,24},{24,16},{1,9},{9,1},{17,25},{25,17},{2,10},{10... | collective-permute-start | bytes 1572872 | tf_op jit(solution)/shard_map/ppermute | solution.py:571
  323.8 40.2 %all-to-all-start.5 = ((bf16[8,64,768]{2,1,0:T(8,128)(2,1)}), bf16[8,64,768]{2,1,0:T(8,128)(2,1)S(1)}, u32[]{:S(2)}, u32[]{:S(2)}) async-start(bf16[8,64,768]{2,1,0:T(8,128)(2,1)} %bitcast.117), calls=%async_computation.7 | async-start | bytes 1572864 | tf_op jit(solution)/shard_map/all_to_all | solution.py:726
  331.3 38.8 %collective-permute-start.35 = (bf16[128,2048]{1,0:T(8,128)(2,1)}, bf16[128,2048]{1,0:T(8,128)(2,1)}, u32[]{:S(2)}, u32[]{:S(2)}) collective-permute-start(bf16[128,2048]{1,0:T(8,128)(2,1)} %get-tuple-element.85), channel_id=1, source_target_pairs={{0,16},{8,24},{16,0},{24,8},{1,17},{9,25},{17,1},{25,9},{2,18},{10... | collective-permute-start | bytes 1572872 | tf_op jit(solution)/shard_map/ppermute | solution.py:575
  334.2 36.5 %collective-permute-start.32 = (bf16[128,2048]{1,0:T(8,128)(2,1)S(1)}, bf16[128,2048]{1,0:T(8,128)(2,1)}, u32[]{:S(2)}, u32[]{:S(2)}) collective-permute-start(bf16[128,2048]{1,0:T(8,128)(2,1)S(1)} %add_convert_fusion.1), channel_id=1, source_target_pairs={{0,16},{8,24},{16,0},{24,8},{1,17},{9,25},{17,1},{25,9},{2,18},{10... | collective-permute-start | bytes 1572872 | tf_op jit(solution)/shard_map/ppermute | solution.py:575
  363.9 31.3 %all-to-all-start.7 = ((bf16[8,64,1024]{2,1,0:T(8,128)(2,1)}), bf16[8,64,1024]{2,1,0:T(8,128)(2,1)S(1)}, u32[]{:S(2)}, u32[]{:S(2)}) async-start(bf16[8,64,1024]{2,1,0:T(8,128)(2,1)} %bitcast.116), calls=%async_computation.9 | async-start | bytes 2097152 | tf_op jit(solution)/shard_map/all_to_all | solution.py:705
  (52 other events, 761.7 us)
Sparse Core Ops, SparseCore 0:
  9.6 67.5 all-gather.4
  78.8 62.1 all-gather.6
  218.7 50.3 reduce-scatter.4
  271.3 59.3 reduce-scatter.2

commit v3 on v2

--- a/solution.py
+++ b/solution.py
@@ -319,17 +319,16 @@
     )
 
 
-def fill(dp, full, pieces, rows, take=None):
+def fill(dp, full, pieces):
     own, along_x, along_y, far_one, far_two = pieces
-    take = rows if take is None else take
-    def at(mask, shift=0):
-        return pl.multiple_of((dp ^ mask) * take + shift, 16)
-    full[pl.ds(at(0), take), :] = own[0:take, :]
-    full[pl.ds(at(1), take), :] = along_x[0:take, :]
-    full[pl.ds(at(2), take), :] = along_y[0:take, :]
+    take, cols = full.shape[0] // 4, full.shape[1]
     cut = far_one.shape[0]
-    full[pl.ds(at(3), cut), :] = far_one[...]
-    full[pl.ds(at(3, cut), take - cut), :] = far_two[0 : take - cut, :]
+    for mask, piece in enumerate((own, along_x, along_y)):
+        full[pl.ds(pl.multiple_of((dp ^ mask) * take, 16), take), :] = piece[0:take, 0:cols]
+    far = (dp ^ 3) * take
+    full[pl.ds(pl.multiple_of(far, 16), cut), :] = far_one[:, 0:cols]
+    full[pl.ds(pl.multiple_of(far + cut, 16), take - cut), :] = far_two[0 : take - cut, 0:cols]
+
 
 def whole(shape):
     return pl.BlockSpec(shape, lambda *_: (0,) * len(shape), pipeline_mode=pl.Buffered(1))
@@ -338,7 +337,7 @@
     return pl.BlockSpec((TILE, cols), lambda i, *_: (i, 0))
 
 def run(body, name, dp, inputs, specs, outs, out_specs, scratch, grid, flops=0, vmem=56):
-    bytes_accessed = sum(a.size * a.dtype.itemsize for a in inputs) + sum(math.prod(o.shape) * o.dtype.itemsize for o in outs)
+    bytes_accessed = sum(math.prod(a.shape) * a.dtype.itemsize for a in [*inputs, *jax.tree.leaves(outs)])
     return pl.pallas_call(
         body, name=name,
         grid_spec=pltpu.PrefetchScalarGridSpec(num_scalar_prefetch=1, grid=grid, in_specs=specs, out_specs=out_specs, scratch_shapes=scratch),
@@ -373,7 +372,7 @@
 def qkv_body(dp, first, w0, wx, wy, w1, w2, bias, cos, s1, s2, q, k, v, full):
     @pl.when(pl.program_id(0) == 0)
     def _():
-        fill(dp[0], full, (w0, wx, wy, w1, w2), w0.shape[0])
+        fill(dp[0], full, (w0, wx, wy, w1, w2))
     joined = dot(first[...], full[...], (1, 0)) + bias[...]
     q[...] = turn(joined[:, :HEAD], cos[...], s1[...], s2[...]).astype(BF16)
     k[...] = turn(joined[:, HEAD:2 * HEAD], cos[...], s1[...], s2[...]).astype(BF16)
@@ -385,31 +384,74 @@
         [tile(w)] + [whole(p.shape) for p in pieces] + [whole(bias.shape)] + [tile(128)] * 3,
         [shape((n, HEAD), BF16)] * 3, [tile(HEAD)] * 3, [pltpu.VMEM((w, 3 * HEAD), BF16)], (n // TILE,), flops=2 * n * w * 3 * HEAD)
 
-def mlp_body(dp, second, g, u0, ux, uy, u1, u2, d0, dx, dy, d1, d2, bias, active, d_hidden, sums, full_up, full_down):
-    step = pl.program_id(0)
-    @pl.when(step == 0)
+def mlp_forward_body(dp, second, u0, ux, uy, u1, u2, bias, active, slope, full):
+    @pl.when(pl.program_id(0) == 0)
     def _():
-        fill(dp[0], full_up, (u0, ux, uy, u1, u2), u0.shape[0])
-        fill(dp[0], full_down, (d0, dx, dy, d1, d2), None, full_down.shape[0] // 4)
-        sums[...] = jnp.zeros_like(sums)
-    hidden = dot(second[...], full_up[...], (1, 0)) + bias[...]
-    d_active = dot(g[...], full_down[...], (1, 1))
+        fill(dp[0], full, (u0, ux, uy, u1, u2))
+    hidden = dot(second[...], full[...], (1, 0)) + bias[...]
     half_cdf = 0.5 + 0.5 * lax.erf(hidden * (1.0 / math.sqrt(2.0)))
     active[...] = (hidden * half_cdf).astype(BF16)
-    slope = half_cdf + hidden * (jnp.exp(-0.5 * hidden * hidden) * (1.0 / math.sqrt(2.0 * math.pi)))
-    low = (slope * d_active).astype(BF16)
+    slope[...] = half_cdf + hidden * (jnp.exp(-0.5 * hidden * hidden) * (1.0 / math.sqrt(2.0 * math.pi)))
+
+def mlp_forward(dp, second, up, bias):
+    n, w = second.shape
+    h = up[0].shape[1]
+    return run(mlp_forward_body, "mlp_forward", dp, [second, *up, bias],
+        [tile(w)] + [whole(p.shape) for p in (*up, bias)],
+        [shape((n, h), BF16), shape((n, h), F32)], [tile(h)] * 2,
+        [pltpu.VMEM((w, h), BF16)], (n // TILE,), flops=2 * n * w * h)
+
+def mlp_backward_body(dp, g, d0, dx, dy, d1, d2, slope, d_hidden, sums, full):
+    @pl.when(pl.program_id(0) == 0)
+    def _():
+        fill(dp[0], full, (d0, dx, dy, d1, d2))
+        sums[...] = jnp.zeros_like(sums)
+    low = (slope[...] * dot(g[...], full[...], (1, 1))).astype(BF16)
     d_hidden[...] = low
     sums[...] += jnp.sum(low.astype(F32), axis=0, keepdims=True)
 
-def mlp(dp, second, g, up, down, bias):
-    n, w = second.shape
-    h = up[0].shape[1]
-    return run(mlp_body, "mlp", dp, [second, g, *up, *down, bias],
-        [tile(w)] * 2 + [whole(p.shape) for p in (*up, *down, bias)],
-        [shape((n, h), BF16)] * 2 + [shape((1, h), F32)], [tile(h)] * 2 + [whole((1, h))],
-        [pltpu.VMEM((w, h), BF16), pltpu.VMEM((h, w), BF16)], (n // TILE,), flops=4 * n * w * h)
-
-def attend_body(dp, q, k, v, g, w_out, seg_q, seg_k, cos, s1, s2, kcos, ks1, ks2, ctx, dq, dk, dv, sums, dk_acc, dv_acc):
+def mlp_backward(dp, g, down, slope):
+    n, w = g.shape
+    h = slope.shape[1]
+    return run(mlp_backward_body, "mlp_backward", dp, [g, *down, slope],
+        [tile(w)] + [whole(p.shape) for p in down] + [tile(h)],
+        [shape((n, h), BF16), shape((1, h), F32)], [tile(h), whole((1, h))],
+        [pltpu.VMEM((h, w), BF16)], (n // TILE,), flops=2 * n * w * h)
+
+def masked_scores(index, q, keys, seg_q, seg_k):
+    reach = keys.shape[0]
+    scores = dot(q, keys, (1, 1)) * (1.0 / math.sqrt(HEAD))
+    row = index * TILE + lax.broadcasted_iota(jnp.int32, (TILE, reach), 0)
+    col = lax.broadcasted_iota(jnp.int32, (TILE, reach), 1)
+    allowed = (seg_q[...] == seg_k[:, 0:reach]) & (col <= row)
+    return jnp.where(allowed, scores, -1e30), allowed
+
+def each_tile(count, block):
+    for index in range(count):
+        @pl.when(pl.program_id(0) == index)
+        def _(index=index):
+            block(index, (index + 1) * TILE)
+
+def attend_forward_body(dp, q, k, v, seg_q, seg_k, context, low, log_sum):
+    def block(index, reach):
+        scores, allowed = masked_scores(index, q[...], k[0:reach, :], seg_q, seg_k)
+        top = jnp.max(scores, axis=1, keepdims=True)
+        weights = jnp.where(allowed, jnp.exp(scores - top), 0.0)
+        weight_sum = jnp.sum(weights, axis=1, keepdims=True)
+        mixed = dot(weights.astype(BF16), v[0:reach, :], (1, 0)) / weight_sum
+        context[...] = mixed
+        low[...] = mixed.astype(BF16)
+        log_sum[...] = top + jnp.log(weight_sum)
+    each_tile(k.shape[0] // TILE, block)
+
+def attend_forward(dp, q, k, v, seg_col, seg_row):
+    n = q.shape[0]
+    return run(attend_forward_body, "attend_forward", dp, [q, k, v, seg_col, seg_row],
+        [tile(HEAD), whole(k.shape), whole(v.shape), tile(1), whole(seg_row.shape)],
+        [shape((n, HEAD), F32), shape((n, HEAD), BF16), shape((n, 1), F32)],
+        [tile(HEAD)] * 2 + [tile(1)], [], (n // TILE,), flops=3 * n * n * HEAD)
+
+def attend_backward_body(dp, q, k, v, g, w_out, context, log_sum, seg_q, seg_k, cos, s1, s2, kcos, ks1, ks2, dq, dk, dv, sums, dk_acc, dv_acc):
     step = pl.program_id(0)
     count = k.shape[0] // TILE
     scale = 1.0 / math.sqrt(HEAD)
@@ -419,33 +461,19 @@
         dk_acc[...] = jnp.zeros_like(dk_acc)
         dv_acc[...] = jnp.zeros_like(dv_acc)
     d_ctx = dot(g[...], w_out[...], (1, 1)).astype(BF16)
-    def block(index):
-        reach = (index + 1) * TILE
+    def block(index, reach):
         keys, values = k[0:reach, :], v[0:reach, :]
-        scores = dot(q[...], keys, (1, 1)) * scale
-        row = index * TILE + lax.broadcasted_iota(jnp.int32, (TILE, reach), 0)
-        col = lax.broadcasted_iota(jnp.int32, (TILE, reach), 1)
-        allowed = (seg_q[...] == seg_k[:, 0:reach]) & (col <= row)
-        scores = jnp.where(allowed, scores, -1e30)
-        top = jnp.max(scores, axis=1, keepdims=True)
-        weights = jnp.where(allowed, jnp.exp(scores - top), 0.0)
-        inverse = 1.0 / jnp.sum(weights, axis=1, keepdims=True)
-        context = dot(weights.astype(BF16), values, (1, 0)) * inverse
-        ctx[...] = context.astype(BF16)
-        delta = jnp.sum(d_ctx.astype(F32) * context, axis=1, keepdims=True)
-        probs = weights * inverse
-        d_probs = dot(d_ctx, values, (1, 1))
-        d_scores = (probs * (d_probs - delta)).astype(BF16)
+        scores, allowed = masked_scores(index, q[...], keys, seg_q, seg_k)
+        probs = jnp.where(allowed, jnp.exp(scores - log_sum[...]), 0.0)
+        delta = jnp.sum(d_ctx.astype(F32) * context[...], axis=1, keepdims=True)
+        d_scores = (probs * (dot(d_ctx, values, (1, 1)) - delta)).astype(BF16)
         d_q = dot(d_scores, keys, (1, 0)) * scale
         low = turn(d_q, cos[...], -s1[...], -s2[...]).astype(BF16)
         dq[...] = low
         sums[:, 0:HEAD] += jnp.sum(low.astype(F32), axis=0, keepdims=True)
         dk_acc[0:reach, :] += dot(d_scores, q[...], (0, 0))
         dv_acc[0:reach, :] += dot(probs.astype(BF16), d_ctx, (0, 0))
-    for index in range(count):
-        @pl.when(step == index)
-        def _(index=index):
-            block(index)
+    each_tile(count, block)
     @pl.when(step == count - 1)
     def _():
         low_k = turn(dk_acc[...] * scale, kcos[...], -ks1[...], -ks2[...]).astype(BF16)
@@ -455,18 +483,18 @@
         sums[:, HEAD:2 * HEAD] = jnp.sum(low_k.astype(F32), axis=0, keepdims=True)
         sums[:, 2 * HEAD:] = jnp.sum(low_v.astype(F32), axis=0, keepdims=True)
 
-def attend(dp, q, k, v, g, w_out, seg_col, seg_row, tables):
+def attend_backward(dp, q, k, v, g, w_out, context, log_sum, seg_col, seg_row, tables):
     n = q.shape[0]; w = g.shape[1]
-    return run(attend_body, "attend", dp, [q, k, v, g, w_out, seg_col, seg_row, *tables, *tables],
-        [tile(HEAD), whole(k.shape), whole(v.shape), tile(w), whole(w_out.shape), tile(1), whole(seg_row.shape)] + [tile(128)] * 3 + [whole((n, 128))] * 3,
-        [shape((n, HEAD), BF16)] * 4 + [shape((1, 3 * HEAD), F32)],
-        [tile(HEAD)] * 2 + [whole((n, HEAD))] * 2 + [whole((1, 3 * HEAD))],
-        [pltpu.VMEM((n, HEAD), F32)] * 2, (n // TILE,), flops=2 * n * w * HEAD + 7 * n * n * HEAD)
+    return run(attend_backward_body, "attend_backward", dp, [q, k, v, g, w_out, context, log_sum, seg_col, seg_row, *tables, *tables],
+        [tile(HEAD), whole(k.shape), whole(v.shape), tile(w), whole(w_out.shape), tile(HEAD), tile(1), tile(1), whole(seg_row.shape)] + [tile(128)] * 3 + [whole((n, 128))] * 3,
+        [shape((n, HEAD), BF16)] * 3 + [shape((1, 3 * HEAD), F32)],
+        [tile(HEAD)] + [whole((n, HEAD))] * 2 + [whole((1, 3 * HEAD))],
+        [pltpu.VMEM((n, HEAD), F32)] * 2, (n // TILE,), flops=2 * n * w * HEAD + 6 * n * n * HEAD)
 
 def output_body(dp, ctx, active, w_out, d0, dx, dy, d1, d2, out, full):
     @pl.when(pl.program_id(0) == 0)
     def _():
-        fill(dp[0], full, (d0, dx, dy, d1, d2), None, full.shape[0] // 4)
+        fill(dp[0], full, (d0, dx, dy, d1, d2))
     out[...] = (dot(ctx[...], w_out[...], (1, 0)) + dot(active[...], full[...], (1, 0))).astype(BF16)
 
 def output(dp, ctx, active, w_out, down):
@@ -478,8 +506,8 @@
 def inward_body(dp, x, dq, dk, dv, d_hidden, w0, wx, wy, w1, w2, u0, ux, uy, u1, u2, vec, u, sums, full_qkv, full_up):
     @pl.when(pl.program_id(0) == 0)
     def _():
-        fill(dp[0], full_qkv, (w0, wx, wy, w1, w2), w0.shape[0])
-        fill(dp[0], full_up, (u0, ux, uy, u1, u2), u0.shape[0])
+        fill(dp[0], full_qkv, (w0, wx, wy, w1, w2))
+        fill(dp[0], full_up, (u0, ux, uy, u1, u2))
         sums[...] = jnp.zeros_like(sums)
     normed, _ = norm_tile(x[...])
     d_joined = jnp.concatenate([dq[...], dk[...], dv[...]], axis=1)
@@ -498,30 +526,31 @@
         [shape((n, w), BF16), shape((4, w), F32)], [tile(w), whole((4, w))],
         [pltpu.VMEM((w, 3 * HEAD), BF16), pltpu.VMEM((w, h), BF16)], (n // TILE,), flops=2 * n * w * (h + 3 * HEAD))
 
-ORDER = (3, 1, 2, 0)
-def terms_body(count, dp, left, *refs):
-    rights, outs = refs[:count], refs[count:]
-    step = pl.program_id(0)
+def terms_body(count, extra, dp, left, *refs):
+    rights, outs = refs[:count], refs[count + extra :]
     right = rights[0][...] if count == 1 else jnp.concatenate([r[...] for r in rights], axis=1)
+    cols = right.shape[1]
     for place in range(4):
-        @pl.when(step == place)
+        @pl.when(pl.program_id(0) == place)
         def _(place=place):
             term = dot(left[...], right, (0, 0)).astype(BF16)
-            if place == 3:
-                outs[6][...] = term
-            else:
-                half = term.shape[0] // 2
-                outs[2 * place][...] = term[:half]
-                outs[2 * place + 1][...] = term[half:]
+            half = term.shape[0] // 2
+            parts = [outs[6]] if place == 3 else [outs[2 * place], outs[2 * place + 1]]
+            for part, out in enumerate(parts):
+                rows = out.shape[0]
+                out[:, 0:cols] = term[part * half : part * half + rows]
+                if extra:
+                    out[:, cols:] = refs[count][part * half : part * half + rows, :]
 
 def order_mask(step):
     return jnp.where(step == 0, 3, jnp.where(step == 3, 0, step))
 
-def terms(dp, left, rights, name):
-    n, w = left.shape; rows = w // 4; cols = sum(r.shape[1] for r in rights)
+def terms(dp, left, rights, name, extra=()):
+    n, w = left.shape; rows = w // 4; cols = sum(r.shape[1] for r in (*rights, *extra))
     outs = [shape((rows // 2, cols), BF16)] * 6 + [shape((rows, cols), BF16)]
-    return run(functools.partial(terms_body, len(rights)), name, dp, [left, *rights],
-        [pl.BlockSpec((n, rows), lambda i, d: (0, d[0] ^ order_mask(i)))] + [whole(r.shape) for r in rights],
+    return run(functools.partial(terms_body, len(rights), len(extra)), name, dp, [left, *rights, *extra],
+        [pl.BlockSpec((n, rows), lambda i, d: (0, d[0] ^ order_mask(i)))] + [whole(r.shape) for r in rights]
+        + [pl.BlockSpec((rows, e.shape[1]), lambda i, d: (d[0] ^ order_mask(i), 0)) for e in extra],
         outs, [whole(o.shape) for o in outs], [], (4,), flops=2 * n * w * cols)
 
 
@@ -532,11 +561,18 @@
             out[rank, :, group * 256 : group * 256 + 256] = source[:, at : at + 256]
 
 
-def qkv_blocks_body(source, out):
+def qkv_blocks_body(source, packed, out):
     for rank in range(HEADS):
         for part in range(3):
             at = (part * HEADS + HEAD_ORDER[rank]) * HEAD
             out[rank, :, part * HEAD : part * HEAD + HEAD] = source[:, at : at + HEAD]
+        out[rank, :, 3 * HEAD :] = packed[...]
+
+
+def out_rows_body(dp, own, along_x, along_y, far, out):
+    for mask, piece in enumerate((own, along_x, along_y)):
+        out[dp[0] ^ mask] = piece[256:, :]
+    out[dp[0] ^ 3] = far[128:, :]
 
 
 def up_rows_body(source, out):
@@ -553,7 +589,7 @@
             out[:, at : at + HEAD] = source[rank, :, part * HEAD : part * HEAD + HEAD].astype(F32)
 
 
-def repack(body, name, source, out):
+def repack(body, name, out, *sources):
     return pl.pallas_call(
         body,
         name=name,
@@ -561,10 +597,18 @@
         compiler_params=pltpu.CompilerParams(vmem_limit_bytes=16 * 2**20),
         cost_estimate=pl.CostEstimate(
             flops=0,
-            bytes_accessed=source.size * source.dtype.itemsize * 3,
+            bytes_accessed=sources[0].size * 6,
             transcendentals=0,
         ),
-    )(source)
+    )(*sources)
+
+
+def tie(value, *others):
+    return lax.optimization_barrier((value, others))[0]
+
+
+def stage(values, done):
+    return lax.optimization_barrier((tuple(values), tuple(done)))[0]
 
 
 def over_x(block):
@@ -575,24 +619,21 @@
     return lax.ppermute(block, "dp", swap(4, 2))
 
 
-def gather_pieces(block, cut):
-    along_x = over_x(block)
-    along_y = over_y(block)
-    return (block, along_x, along_y, over_x(along_y[:cut]), over_y(along_x[cut:]))
-
-
-def reduce_pieces(pieces):
-    far_top, far_low, x_top, x_low, y_top, y_low, own = pieces
-    half = far_top.shape[0]
-    far_x = over_x(far_top)
-    far_y = over_y(far_low)
-    got_x_top = over_x(x_top)
-    got_y_low = over_y(y_low)
+def pass_on(near, far):
+    _, x_low, y_top, _ = near
+    far_x, far_y = far
     got_y_top = over_y((y_top.astype(F32) + far_x.astype(F32)).astype(BF16))
     got_x_low = over_x((x_low.astype(F32) + far_y.astype(F32)).astype(BF16))
+    return got_y_top, got_x_low
+
+
+def reduce_last(own, near, then, kind):
+    half = own.shape[0] // 2
+    got_x_top, got_y_low = near
+    got_y_top, got_x_low = then
     top = own[:half].astype(F32) + got_x_top.astype(F32) + got_y_top.astype(F32)
     low = own[half:].astype(F32) + got_x_low.astype(F32) + got_y_low.astype(F32)
-    return top, low
+    return jnp.concatenate([top.astype(kind), low.astype(kind)], axis=0)
 
 
 def rotary_lanes(length):
@@ -633,12 +674,10 @@
     everywhere = ("dp", "sp")
     head = head_of(sp)
 
+    fours = [[0, 1, 2, 3], [4, 5, 6, 7]]
     x_all = lax.all_gather(x_own, "sp", axis=0, tiled=True)
-    down = gather_pieces(jnp.concatenate([w_down, w_attn_out], axis=0), w_down.shape[0] // 2)
-    up_blocks = repack(
-        up_blocks_body, "up_blocks", w_up, jax.ShapeDtypeStruct((HEADS, rows, 1024), BF16)
-    )
-    up_rows = lax.all_to_all(up_blocks, "sp", 0, 0, tiled=True).reshape(HEADS * rows, 1024)
+    down_own = jnp.concatenate([w_down, w_attn_out], axis=0)
+    down_x, down_y = over_x(down_own), over_y(down_own)
     packed = jnp.concatenate(
         [
             jnp.stack([ln1_gain, ln1_bias, ln2_gain, ln2_bias, b_attn_out, b_down]),
@@ -647,86 +686,147 @@
             segments[0].astype(BF16).reshape(2, 64),
         ]
     )
-    small = lax.all_to_all(
-        jnp.broadcast_to(packed[None], (32,) + packed.shape), everywhere, 0, 0, tiled=True
-    )
-    up = gather_pieces(up_rows, HEADS * rows // 2)
+    packed = jnp.pad(packed, ((0, rows - 15), (0, 64)))
     qkv_blocks = repack(
-        qkv_blocks_body, "qkv_blocks", w_qkv, jax.ShapeDtypeStruct((HEADS, rows, 768), BF16)
-    )
-    qkv_rows = lax.all_to_all(qkv_blocks, "sp", 0, 0, tiled=True).reshape(HEADS * rows, 768)
-    w_in = gather_pieces(qkv_rows, HEADS * rows // 2)
-    g_all = lax.all_gather(g_own, "sp", axis=0, tiled=True)
+        qkv_blocks_body, "qkv_blocks", jax.ShapeDtypeStruct((HEADS, rows, 896), BF16), w_qkv, packed
+    )
+    up_blocks = repack(
+        up_blocks_body, "up_blocks", jax.ShapeDtypeStruct((HEADS, rows, 1024), BF16), w_up
+    )
+    cos, sin_one, sin_two = rotary_lanes(length)
+    qkv_rows = lax.all_to_all(qkv_blocks, "sp", 0, 0, tiled=True).reshape(HEADS * rows, 896)
+
     cut = w_down.shape[0] // 2
-    out_parts = [piece[2 * cut :] for piece in down[:3]] + [down[4][cut:]]
-    out_rows = jnp.zeros((4, rows, width), BF16)
-    for mask, piece in enumerate(out_parts):
-        out_rows = put(out_rows, piece, dp ^ mask)
-    fours = [[0, 1, 2, 3], [4, 5, 6, 7]]
+    half = HEADS * rows // 2
+    down_far = over_x(down_y[:cut]), over_y(down_x[cut:])
+    sum_out = jnp.sum(g_own.astype(F32), axis=0)
+    up_blocks, qkv_rows, down_far, cos, sin_one, sin_two, sum_out = stage(
+        (up_blocks, qkv_rows, down_far, cos, sin_one, sin_two, sum_out), ()
+    )
+    tables = (cos, sin_one, sin_two)
+    down = (down_own, down_x, down_y, *down_far)
+    up_rows = lax.all_to_all(up_blocks, "sp", 0, 0, tiled=True).reshape(HEADS * rows, 1024)
+    qkv_x, qkv_y = over_x(qkv_rows), over_y(qkv_rows)
+    out_rows = run(
+        out_rows_body, "out_rows", dp, [*down[:3], down[4]], [whole(d.shape) for d in (*down[:3], down[4])],
+        shape((4, rows, width), BF16), whole((4, rows, width)), [], (1,),
+    )
+
+    qkv_x, qkv_y, out_rows = stage((qkv_x, qkv_y, out_rows), ())
+    qkv_far = over_x(qkv_y[:half]), over_y(qkv_x[half:])
+
+    up_rows, qkv_far, g_late, out_rows = stage((up_rows, qkv_far, g_own, out_rows), ())
+    w_in = (qkv_rows, qkv_x, qkv_y, *qkv_far)
+    g_all = lax.all_gather(g_late, "sp", axis=0, tiled=True)
+    up_x, up_y = over_x(up_rows), over_y(up_rows)
     w_out = lax.all_to_all(
         out_rows, "sp", 0, 0, tiled=True, axis_index_groups=fours
     ).reshape(HEAD, width)
 
+    small = jnp.zeros((4, HEADS, 15, 64), BF16)
+    far = jnp.concatenate([piece[:, 768:832] for piece in qkv_far], axis=0)
+    for mask, piece in enumerate([piece[:, 768:832] for piece in w_in[:3]] + [far]):
+        small = put(small, piece.reshape(HEADS, rows, 64)[:, :15], dp ^ mask)
+    small = small.reshape(32, 15, 64)
     vectors = small[:, :6].transpose(1, 0, 2).reshape(6, width).astype(F32)
     norm_vec = vectors[:4]
     bias_qkv = pick(small[:, 6:9].reshape(3, HEADS, HEAD), head, 1).astype(F32).reshape(1, 768)
     bias_up = pick(small[:, 9:13].reshape(4, HEADS, 256), sp, 1).astype(F32).reshape(1, 1024)
     seg = pick(small[:, 13:].reshape(4, length), dp).astype(F32)
-    tables = rotary_lanes(length)
-
+    seg_col, seg_row = seg.reshape(length, 1), seg.reshape(1, length)
     first_in, second_in = norms(dp, x_all, norm_vec)
-    active, d_hidden, up_sums = mlp(dp, second_in, g_all, up, down, bias_up)
-    down_terms = terms(dp, active, [g_all], "down_terms")
+    queries, key_rows, value_rows = qkv(dp, first_in, w_in, bias_qkv, tables)
+
+    up_x, up_y, queries, w_out = stage((up_x, up_y, queries, w_out), (bias_up, seg_col, seg_row))
+    up = (up_rows, up_x, up_y, over_x(up_y[:half]), over_y(up_x[half:]))
+
+    wide_context, context, log_sum = attend_forward(
+        dp, queries, key_rows, value_rows, seg_col, seg_row
+    )
+    up, context = stage((up, context), ())
+    active, slope = mlp_forward(dp, second_in, up, bias_up)
+    out_terms = output(dp, context, active, w_out, down)
+    out_sum = lax.psum_scatter(out_terms, "sp", scatter_dimension=0, tiled=True)
+
+    attn_terms = dot(tie(context, out_terms), g_all, (0, 0)).astype(BF16)
+    attn_sent = lax.all_to_all(
+        attn_terms.reshape(4, HEAD // 4, width), "sp", 0, 0, tiled=True, axis_index_groups=fours
+    )
+    d_hidden, up_sums = mlp_backward(dp, tie(g_all, attn_terms), down, slope)
     up_terms = terms(dp, second_in, [d_hidden], "up_terms")
-    queries, key_rows, value_rows = qkv(dp, first_in, w_in, bias_qkv, tables)
-    context, d_q, d_k, d_v, qkv_sums = attend(
+    up_far = over_x(up_terms[0]), over_y(up_terms[1])
+    d_q, d_k, d_v, qkv_sums = attend_backward(
         dp,
-        queries,
+        tie(queries, up_terms),
         key_rows,
         value_rows,
         g_all,
         w_out,
-        seg.reshape(length, 1),
-        seg.reshape(1, length),
+        wide_context,
+        log_sum,
+        seg_col,
+        seg_row,
         tables,
     )
-    out_terms = output(dp, context, active, w_out, down)
-    out_sum = lax.psum_scatter(out_terms, "sp", scatter_dimension=0, tiled=True)
-    u_terms, norm_sums = inward(dp, x_all, d_q, d_k, d_v, d_hidden, w_in, up, norm_vec)
+    own, to_x, to_y, to_far = (pick(attn_sent, dp ^ mask) for mask in range(4))
+    part = rows // 2
+    attn_near = (to_x[:part], to_x[part:], to_y[:part], to_y[part:])
+    up_near, to_far = stage((up_terms[2:6], to_far), (d_q,))
+    up_near_got = over_x(up_near[0]), over_y(up_near[3])
+    attn_far = over_x(to_far[:part]), over_y(to_far[part:])
+    sum_qkv = lax.dynamic_update_slice(
+        jnp.zeros((3, HEADS, HEAD), F32), qkv_sums.reshape(3, 1, HEAD), (0, head, 0)
+    )
+    sum_up = lax.dynamic_update_slice(
+        jnp.zeros((4, HEADS, 256), F32), up_sums.reshape(4, 1, 256), (0, sp, 0)
+    )
+    early = jnp.concatenate(
+        [sum_out.reshape(32, 64), sum_qkv.reshape(32, 192), sum_up.reshape(32, 256)], axis=1
+    )
+    u_terms, norm_sums = inward(
+        dp, tie(x_all, up_far), d_q, d_k, d_v, d_hidden, w_in, up, norm_vec
+    )
+    up_near, attn_near = stage((up_near, attn_near), (up_near_got, attn_far))
+    up_then = pass_on(up_near, up_far)
+    attn_near_got = over_x(attn_near[0]), over_y(attn_near[3])
+    u_terms, early, norm_sums = stage((u_terms, early, norm_sums), (out_sum, up_near_got))
     u_sum = lax.psum_scatter(u_terms, "sp", scatter_dimension=0, tiled=True)
-    qkv_terms = terms(dp, first_in, [d_q, d_k, d_v], "qkv_terms")
-    attn_terms = dot(context, g_all, (0, 0)).astype(BF16).reshape(4, HEAD // 4, width)
-    attn_terms = lax.all_to_all(
-        attn_terms, "sp", 0, 0, tiled=True, axis_index_groups=fours
-    )
-
-    grad_down = jnp.concatenate(reduce_pieces(down_terms), axis=0)
-    up_sum = jnp.concatenate([half.astype(BF16) for half in reduce_pieces(up_terms)], axis=0)
+    totals = jnp.concatenate(
+        [norm_sums.reshape(4, 32, 64).transpose(1, 0, 2).reshape(32, 256), early], axis=1
+    )
+    totals = jnp.pad(totals.astype(BF16).reshape(32, 6, 128), ((0, 0), (0, rows - 6), (0, 0)))
+    totals = totals.reshape(32 * rows, 128)
+    qkv_terms = terms(dp, tie(first_in, u_terms), [d_q, d_k, d_v], "qkv_terms", (totals,))
+
+    qkv_terms, up_then = stage((qkv_terms, up_then), (attn_near_got,))
+    up_sum = reduce_last(up_terms[6], up_near_got, up_then, BF16)
     up_back = lax.all_to_all(up_sum.reshape(HEADS, rows, 1024), "sp", 0, 0, tiled=True)
+    qkv_far = over_x(qkv_terms[0]), over_y(qkv_terms[1])
+    qkv_near_got = over_x(qkv_terms[2]), over_y(qkv_terms[5])
+    down_terms = terms(dp, tie(active, up_sum), [g_all], "down_terms")
+
+    qkv_far, qkv_near_got, down_terms = stage((qkv_far, qkv_near_got, down_terms), ())
+    qkv_then = pass_on(qkv_terms[2:6], qkv_far)
+    attn_then = pass_on(attn_near, attn_far)
+
+    qkv_then, down_terms = stage((qkv_then, down_terms), (attn_then, up_back))
+    qkv_sum = reduce_last(qkv_terms[6], qkv_near_got, qkv_then, BF16)
+    qkv_back = lax.all_to_all(qkv_sum.reshape(HEADS, rows, 896), "sp", 0, 0, tiled=True)
+    down_far = over_x(down_terms[0]), over_y(down_terms[1])
+    down_near_got = over_x(down_terms[2]), over_y(down_terms[5])
+
+    down_far, down_terms = stage((down_far, down_terms), (down_near_got, qkv_sum))
+    grad_out = reduce_last(own, attn_near_got, attn_then, F32)
     grad_up = repack(
-        up_rows_body, "up_rows", up_back, jax.ShapeDtypeStruct((rows, HEADS * 1024), F32)
-    )
-    own, to_x, to_y, to_far = (pick(attn_terms, dp ^ mask) for mask in range(4))
-    part = rows // 2
-    grad_out = jnp.concatenate(
-        reduce_pieces(
-            (
-                to_far[:part],
-                to_far[part:],
-                to_x[:part],
-                to_x[part:],
-                to_y[:part],
-                to_y[part:],
-                own,
-            )
-        ),
-        axis=0,
-    )
-    qkv_sum = jnp.concatenate([half.astype(BF16) for half in reduce_pieces(qkv_terms)], axis=0)
-    qkv_back = lax.all_to_all(qkv_sum.reshape(HEADS, rows, 768), "sp", 0, 0, tiled=True)
+        up_rows_body, "up_rows", jax.ShapeDtypeStruct((rows, HEADS * 1024), F32), up_back
+    )
+    down_then = pass_on(down_terms[2:6], down_far)
+    down_then = stage(down_then, (qkv_back, grad_up, grad_out))
+    grad_down = reduce_last(down_terms[6], down_near_got, down_then, F32)
     grad_qkv = repack(
-        qkv_rows_body, "qkv_rows", qkv_back, jax.ShapeDtypeStruct((rows, HEADS * 768), F32)
-    )
+        qkv_rows_body, "qkv_rows", jax.ShapeDtypeStruct((rows, HEADS * 768), F32), qkv_back
+    )
+    owned = jnp.sum(qkv_back[:, :6, 768:].astype(F32), axis=0).reshape(768)
 
     x_wide = x_own.astype(F32)
     block_output = (x_wide + out_sum.astype(F32) + (vectors[4] + vectors[5]))[None]
@@ -736,23 +836,6 @@
     u_along = jnp.mean(u_wide * normed, axis=-1, keepdims=True)
     input_grad = (g_own.astype(F32) + (u_wide - u_mean - normed * u_along) * scale)[None]
 
-    sum_qkv = lax.dynamic_update_slice(
-        jnp.zeros((3, HEADS, HEAD), F32), qkv_sums.reshape(3, 1, HEAD), (0, head, 0)
-    )
-    sum_up = lax.dynamic_update_slice(
-        jnp.zeros((4, HEADS, 256), F32), up_sums.reshape(4, 1, 256), (0, sp, 0)
-    )
-    sum_out = jnp.sum(g_own.astype(F32), axis=0)
-    totals = jnp.concatenate(
-        [
-            norm_sums.reshape(4, 32, 64).transpose(1, 0, 2).reshape(32, 256),
-            sum_out.reshape(32, 64),
-            sum_qkv.reshape(32, 192),
-            sum_up.reshape(32, 256),
-        ],
-        axis=1,
-    )
-    owned = jnp.sum(lax.all_to_all(totals, everywhere, 0, 0, tiled=True), axis=0)
     grad_g1, grad_s1, grad_g2, grad_s2, grad_bout = (
         owned[k * rows : (k + 1) * rows] for k in range(5)
     )

time: 413 us -> 388 us (0.939)
  waiting for transfers between devices: 145 us -> 128 us
  starting transfers between devices: 79.1 us -> 62.6 us
  Pallas kernels: 103 us -> 117 us
  local copies, waits for them, and re-layouts: 32.1 us -> 23.2 us
    ppermute x18, waiting for transfers between devices: 29.7 us -> 49.7 us  [over_x(): return lax.ppermute(block, 'dp', swap(4, 1))]
    all_to_all x1, waiting for transfers between devices: 36 us -> 16.8 us  [line_shards(): lax.all_to_all(qkv_blocks, 'sp', 0, 0, tiled=True)]
    all_to_all x1, waiting for transfers between devices: 19 us -> 0.01 us  [line_shards(): lax.all_to_all(up_blocks, 'sp', 0, 0, tiled=True)]
    pallas_call x9 -> x12, Pallas kernels: 98.3 us -> 112 us  [run(): pl.pallas_call(body, name=name, grid_spec=pltpu.PrefetchScalarGridSpec(nu...]
    all_to_all x4 -> x2, starting transfers between devices: 20.5 us -> 7.88 us  [the longest x1 4.34 us: line_shards(): lax.all_to_all(qkv_sum.reshape(HEADS, rows, 896), 'sp', 0, 0, tiled=True)]
    all_to_all x1, waiting for transfers between devices: 0.01 us -> 9.67 us  [line_shards(): lax.all_to_all(out_rows, 'sp', 0, 0, tiled=True, axis_index_groups=fours)]
    all_to_all x1, waiting for transfers between devices: 8.09 us -> 0.01 us  [line_shards(): lax.all_to_all(up_sum.reshape(HEADS, rows, 1024), 'sp', 0, 0, tiled=True)]
    dynamic_update_slice x4, local copies, waits for them, and re-layouts: 4.78 us -> 0.07 us  [put(): return lax.dynamic_update_slice_in_dim(array, piece[None], index, 0)]
  transfers between devices with their start and end apart: 48 -> 46, of which waited for: 18 -> 26; matrix products, arithmetic and copies ran while one was open for 14% -> 13% of each run, Pallas kernels for 18% -> 30%
where the time goes in v3:
time: 388 us; the launch traced here: 383 us
  waiting for transfers between devices  128 us (33%)
  Pallas kernels  117 us (30%)
  starting transfers between devices  62.6 us (16%)
  other arithmetic  33.4 us (9%)
  local copies, waits for them, and re-layouts  23.2 us (6%)
  between operations  15 us (4%)
  matrix products  4.44 us (1%)
    pallas_call x12, Pallas kernels, run(): pl.pallas_call(body, name=name, grid_spec=pltpu.PrefetchScalarGridSpec(nu...  112 us
    ppermute x18, waiting for transfers between devices, over_x(): return lax.ppermute(block, 'dp', swap(4, 1))  49.7 us
    ppermute x18, waiting for transfers between devices, over_y(): return lax.ppermute(block, 'dp', swap(4, 2))  49.4 us
    ppermute x18, starting transfers between devices, over_y(): return lax.ppermute(block, 'dp', swap(4, 2))  18.4 us
    ppermute x18, starting transfers between devices, over_x(): return lax.ppermute(block, 'dp', swap(4, 1))  18.1 us
    all_to_all x1, waiting for transfers between devices, line_shards(): lax.all_to_all(qkv_blocks, 'sp', 0, 0, tiled=True)  16.8 us
    all_to_all x1, waiting for transfers between devices, line_shards(): lax.all_to_all(out_rows, 'sp', 0, 0, tiled=True, axis_index_groups=fours)  9.67 us
  transfers between devices with their start and end apart: 46, of which 26 were waited for; matrix products, arithmetic and copies ran while one was open for 13% of the time, Pallas kernels for 30%

profile of v3, /device:TPU:0, one launch (start us, length us, event | category | flops | bytes accessed | tf_op | source)
XLA Modules:
  0.0 383.3 jit_solution(3937553199286815657)
XLA Ops:
  15.4 4.9 %all-to-all-start = ((bf16[8,64,896]{2,1,0:T(8,128)(2,1)}), bf16[8,64,896]{2,1,0:T(8,128)(2,1)S(1)}, u32[]{:S(2)}, u32[]{:S(2)}) async-start(bf16[8,64,896]{2,1,0:T(8,128)(2,1)} %qkv_blocks.1), calls=%async_computation | async-start | bytes 1835008 | tf_op jit(solution)/shard_map/all_to_all | solution.py:697
  20.5 20.6 %collective-permute-done.2.along_x.dx = bf16[320,2048]{1,0:T(8,128)(2,1)S(1)} collective-permute-done((bf16[320,2048]{1,0:T(8,128)(2,1)S(1)}, bf16[320,2048]{1,0:T(8,128)(2,1)S(1)}, u32[]{:S(2)}, u32[]{:S(2)}) %collective-permute-start.2) | collective-permute-done | bytes 1310752 | tf_op jit(solution)/shard_map/ppermute | solution.py:615
  52.4 16.8 %all-to-all-done = bf16[8,64,896]{2,1,0:T(8,128)(2,1)S(1)} async-done(((bf16[8,64,896]{2,1,0:T(8,128)(2,1)}), bf16[8,64,896]{2,1,0:T(8,128)(2,1)S(1)}, u32[]{:S(2)}, u32[]{:S(2)}) %all-to-all-start) | async-done | bytes 917536 | tf_op jit(solution)/shard_map/all_to_all | solution.py:697
  77.2 19.1 %collective-permute-done.5.wy = bf16[512,896]{1,0:T(8,128)(2,1)S(1)} collective-permute-done((bf16[512,896]{1,0:T(8,128)(2,1)S(1)}, bf16[512,896]{1,0:T(8,128)(2,1)S(1)}, u32[]{:S(2)}, u32[]{:S(2)}) %collective-permute-start.5) | collective-permute-done | bytes 917536 | tf_op jit(solution)/shard_map/ppermute | solution.py:619
  99.6 10.2 %collective-permute-done.7.w2 = bf16[256,896]{1,0:T(8,128)(2,1)S(1)} collective-permute-done((bf16[256,896]{1,0:T(8,128)(2,1)S(1)}, bf16[256,896]{1,0:T(8,128)(2,1)S(1)}, u32[]{:S(2)}, u32[]{:S(2)}) %collective-permute-start.7) | collective-permute-done | bytes 458784 | tf_op jit(solution)/shard_map/ppermute | solution.py:619
  123.3 7.7 %norms.1 = (bf16[1024,2048]{1,0:T(8,128)(2,1)}, bf16[1024,2048]{1,0:T(8,128)(2,1)}) custom-call(s32[1]{0:T(128)} %bitcast.1.dp, bf16[1024,2048]{1,0:T(8,128)(2,1)} %bitcast.113, f32[4,2048]{1,0:T(4,128)} %slice.177.vec), custom_call_target="tpu_custom_call" | custom-call | bytes 12615680 | tf_op jit(solution)/shard_map/norms/pallas_call | solution.py:341
  131.0 8.2 %qkv.1 = (bf16[1024,256]{1,0:T(8,128)(2,1)}, bf16[1024,256]{1,0:T(8,128)(2,1)}, bf16[1024,256]{1,0:T(8,128)(2,1)}) custom-call(s32[1]{0:T(128)} %bitcast.1.dp, bf16[1024,2048]{1,0:T(8,128)(2,1)} %get-tuple-element.193.first.left, bf16[512,896]{1,0:T(8,128)(2,1)} %bitcast.122, bf16[512,896]{1,0:T(8,128)(2,1)} %collective-permute-done.4.wx, ...), custom_call_target="tpu_custom_call" | custom-call | flops 3221225472 | bytes 11013120 | tf_op jit(solution)/shard_map/qkv/pallas_call | solution.py:341
  143.5 9.7 %all-to-all-done.2 = bf16[4,64,2048]{2,1,0:T(8,128)(2,1)S(1)} async-done(((bf16[4,64,2048]{2,1,0:T(8,128)(2,1)}), bf16[4,64,2048]{2,1,0:T(8,128)(2,1)S(1)}, u32[]{:S(2)}, u32[]{:S(2)}) %all-to-all-start.2) | async-done | bytes 1048608 | tf_op jit(solution)/shard_map/all_to_all | solution.py:722
  156.3 5.7 %attend_forward.1 = (f32[1024,256]{1,0:T(8,128)}, bf16[1024,256]{1,0:T(8,128)(2,1)}, f32[1024,1]{1,0:T(8,128)}) custom-call(s32[1]{0:T(128)} %bitcast.1.dp, bf16[1024,256]{1,0:T(8,128)(2,1)} %get-tuple-element.179.q, bf16[1024,256]{1,0:T(8,128)(2,1)} %get-tuple-element.153.k, bf16[1024,256]{1,0:T(8,128)(2,1)} %get-tuple-element.154.v, ...), custom_call_target="tpu_custom_call" | custom-call | flops 805306368 | bytes 3158016 | tf_op jit(solution)/shard_map/attend_forward/pallas_call | solution.py:341
  166.1 10.7 %mlp_forward.1 = (bf16[1024,1024]{1,0:T(8,128)(2,1)}, f32[1024,1024]{1,0:T(8,128)}) custom-call(s32[1]{0:T(128)} %bitcast.1.dp, bf16[1024,2048]{1,0:T(8,128)(2,1)} %get-tuple-element.157.second.left, bf16[512,1024]{1,0:T(8,128)(2,1)} %bitcast.126, bf16[512,1024]{1,0:T(8,128)(2,1)} %collective-permute-done.8.ux, bf16[512,1024]{1,0:T(8,128)(2,1)} %copy-done.30, ...), custom_call_target="tpu_custom_call" | custom-call | flops 4294967296 | bytes 14684160 | tf_op jit(solution)/shard_map/mlp_forward/pallas_call | solution.py:341
  176.8 10.5 %output.1 = bf16[1024,2048]{1,0:T(8,128)(2,1)} custom-call(s32[1]{0:T(128)} %bitcast.1.dp, bf16[1024,256]{1,0:T(8,128)(2,1)} %get-tuple-element.167.ctx, bf16[1024,1024]{1,0:T(8,128)(2,1)} %get-tuple-element.217.active.left, bf16[256,2048]{1,0:T(8,128)(2,1)} %bitcast.116, bf16[320,2048]{1,0:T(8,128)(2,1)} %copy-done.5, bf16[320,2048]{1,0:T(8,128)(2,1)} %copy-done.7, ...), custom_call_target="tpu_custom_call" | custom-call | flops 5368709120 | bytes 13107200 | tf_op jit(solution)/shard_map/output/pallas_call | solution.py:341
  188.3 4.4 %convolution_convert_fusion = bf16[256,2048]{1,0:T(8,128)(2,1)} fusion(bf16[1024,256]{1,0:T(8,128)(2,1)S(1)} %copy-done.56, bf16[1024,2048]{1,0:T(8,128)(2,1)} %all-gather.4.cloned.1.call-done.g.refs_0_), kind=kOutput, calls=%fused_computation | convolution fusion | flops 1074266112 | bytes 5767168 | tf_op jit(solution)/shard_map/dot_general | solution.py:127
  196.5 9.9 %mlp_backward.1 = (bf16[1024,1024]{1,0:T(8,128)(2,1)}, f32[1,1024]{1,0:T(1,128)}) custom-call(s32[1]{0:T(128)} %bitcast.1.dp, bf16[1024,2048]{1,0:T(8,128)(2,1)} %all-gather.4.cloned.1.call-done.g.refs_0_, bf16[320,2048]{1,0:T(8,128)(2,1)} %copy-done.5, bf16[320,2048]{1,0:T(8,128)(2,1)} %copy-done.7, bf16[320,2048]{1,0:T(8,128)(2,1)} %collective-permute-done.along_y.dy, ...), custom_call_target="tpu_custom_call" | custom-call | flops 4294967296 | bytes 15732736 | tf_op jit(solution)/shard_map/mlp_backward/pallas_call | solution.py:341
  206.5 9.8 %up_terms.1 = (bf16[256,1024]{1,0:T(8,128)(2,1)}, bf16[256,1024]{1,0:T(8,128)(2,1)}, bf16[256,1024]{1,0:T(8,128)(2,1)}, bf16[256,1024]{1,0:T(8,128)(2,1)}, bf16[...) custom-call(s32[1]{0:T(128)} %bitcast.1.dp, ...), custom_call_target="tpu_custom_call" | custom-call | flops 4294967296 | bytes 10485760 | tf_op jit(solution)/shard_map/up_terms/pallas_call | solution.py:341
  218.5 10.3 %attend_backward.1 = (bf16[1024,256]{1,0:T(8,128)(2,1)}, bf16[1024,256]{1,0:T(8,128)(2,1)}, bf16[1024,256]{1,0:T(8,128)(2,1)}, f32[1,768]{1,0:T(1,128)}) custom-call(s32[1]{0:T(128)} %bitcast.1.dp, bf16[1024,256]{1,0:T(8,128)(2,1)} %get-tuple-element.179.q, bf16[1024,256]{1,0:T(8,128)(2,1)} %get-tuple-element.153.k, bf16[1024,256]{1,0:T(8,128)(2,1)} %get-tuple-element.154.v, ...), custom_call_target="tpu_custom_call" | custom-call | flops 2684354560 | bytes 12598272 | tf_op jit(solution)/shard_map/attend_backward/pallas_call | solution.py:341
  233.0 16.3 %inward.1 = (bf16[1024,2048]{1,0:T(8,128)(2,1)}, f32[4,2048]{1,0:T(4,128)}) custom-call(s32[1]{0:T(128)} %bitcast.1.dp, bf16[1024,2048]{1,0:T(8,128)(2,1)} %bitcast.114, bf16[1024,256]{1,0:T(8,128)(2,1)} %get-tuple-element.182.dq.refs_0_, bf16[1024,256]{1,0:T(8,128)(2,1)} %get-tuple-element.183.dk.refs_1_, bf16[1024,256]{1,0:T(8,128)(2,1)} %get-tuple-element.184.dv.refs_2_, ...), custom_call_target="tpu_custom_call" | custom-call | flops 7516192768 | bytes 19988480 | tf_op jit(solution)/shard_map/inward/pallas_call | solution.py:341
  265.7 8.5 %qkv_terms.1 = (bf16[256,896]{1,0:T(8,128)(2,1)}, bf16[256,896]{1,0:T(8,128)(2,1)}, bf16[256,896]{1,0:T(8,128)(2,1)}, bf16[256,896]{1,0:T(8,128)(2,1)}, bf16[256...) custom-call(s32[1]{0:T(128)} %bitcast.1.dp, ...), custom_call_target="tpu_custom_call" | custom-call | flops 3758096384 | bytes 9961472 | tf_op jit(solution)/shard_map/qkv_terms/pallas_call | solution.py:341
  277.2 5.3 %all-to-all-start.4 = ((bf16[8,64,1024]{2,1,0:T(8,128)(2,1)}), bf16[8,64,1024]{2,1,0:T(8,128)(2,1)S(1)}, u32[]{:S(2)}, u32[]{:S(2)}) async-start(bf16[8,64,1024]{2,1,0:T(8,128)(2,1)} %bitcast.115), calls=%async_computation.6 | async-start | bytes 2097152 | tf_op jit(solution)/shard_map/all_to_all | solution.py:803
  289.0 10.8 %down_terms.1 = (bf16[128,2048]{1,0:T(8,128)(2,1)}, bf16[128,2048]{1,0:T(8,128)(2,1)}, bf16[128,2048]{1,0:T(8,128)(2,1)}, bf16[128,2048]{1,0:T(8,128)(2,1)}, bf1...) custom-call(s32[1]{0:T(128)} %bitcast.1.dp, ...), custom_call_target="tpu_custom_call" | custom-call | flops 4294967296 | bytes 10485760 | tf_op jit(solution)/shard_map/down_terms/pallas_call | solution.py:341
  299.8 6.1 %collective-permute-done.24 = bf16[256,896]{1,0:T(8,128)(2,1)S(1)} collective-permute-done((bf16[256,896]{1,0:T(8,128)(2,1)}, bf16[256,896]{1,0:T(8,128)(2,1)S(1)}, u32[]{:S(2)}, u32[]{:S(2)}) %collective-permute-start.24) | collective-permute-done | bytes 458784 | tf_op jit(solution)/shard_map/ppermute | solution.py:615
  314.5 8.5 %collective-permute-done.28 = bf16[32,2048]{1,0:T(8,128)(2,1)} collective-permute-done((bf16[32,2048]{1,0:T(8,128)(2,1)}, bf16[32,2048]{1,0:T(8,128)(2,1)}, u32[]{:S(2)}, u32[]{:S(2)}) %collective-permute-start.28) | collective-permute-done | bytes 131104 | tf_op jit(solution)/shard_map/ppermute | solution.py:619
  329.9 4.3 %all-to-all-start.5 = ((bf16[8,64,896]{2,1,0:T(8,128)(2,1)}), bf16[8,64,896]{2,1,0:T(8,128)(2,1)S(1)}, u32[]{:S(2)}, u32[]{:S(2)}) async-start(bf16[8,64,896]{2,1,0:T(8,128)(2,1)} %bitcast.118), calls=%async_computation.7 | async-start | bytes 1835008 | tf_op jit(solution)/shard_map/all_to_all | solution.py:814
  339.0 8.6 %collective-permute-done.32 = bf16[128,2048]{1,0:T(8,128)(2,1)} collective-permute-done((bf16[128,2048]{1,0:T(8,128)(2,1)}, bf16[128,2048]{1,0:T(8,128)(2,1)}, u32[]{:S(2)}, u32[]{:S(2)}) %collective-permute-start.32) | collective-permute-done | bytes 524320 | tf_op jit(solution)/shard_map/ppermute | solution.py:615
  359.2 4.7 %collective-permute-done.35 = bf16[128,2048]{1,0:T(8,128)(2,1)} collective-permute-done((bf16[128,2048]{1,0:T(8,128)(2,1)}, bf16[128,2048]{1,0:T(8,128)(2,1)}, u32[]{:S(2)}, u32[]{:S(2)}) %collective-permute-start.35) | collective-permute-done | bytes 524320 | tf_op jit(solution)/shard_map/ppermute | solution.py:615
  (304 shorter events, 136.7 us)
Async XLA Ops:
  7.3 116.0 %all-gather.6.cloned.1.call-start = ((), (), s32[]{:S(2)}) async-start(), calls=%async_computation.11 | async-start | bytes 4718592 | tf_op jit(solution)/shard_map/all_gather | solution.py:678
  9.4 31.8 %collective-permute-start.2 = (bf16[320,2048]{1,0:T(8,128)(2,1)S(1)}, bf16[320,2048]{1,0:T(8,128)(2,1)S(1)}, u32[]{:S(2)}, u32[]{:S(2)}) collective-permute-start(bf16[320,2048]{1,0:T(8,128)(2,1)S(1)} %constant_dynamic-update-slice_fusion.own.d0), channel_id=1, source_target_pairs={{0,8},{8,0},{16,24},{24,16},{1,9},{9,1},{17,25},{25,17},{2,10},{10... | collective-permute-start | bytes 3932168 | tf_op jit(solution)/shard_map/ppermute | solution.py:615
  12.4 33.7 %collective-permute-start = (bf16[320,2048]{1,0:T(8,128)(2,1)S(1)}, bf16[320,2048]{1,0:T(8,128)(2,1)}, u32[]{:S(2)}, u32[]{:S(2)}) collective-permute-start(bf16[320,2048]{1,0:T(8,128)(2,1)S(1)} %constant_dynamic-update-slice_fusion.own.d0), channel_id=1, source_target_pairs={{0,16},{8,24},{16,0},{24,8},{1,17},{9,25},{17,1},{25,9},{2,18},{10... | collective-permute-start | bytes 3932168 | tf_op jit(solution)/shard_map/ppermute | solution.py:619
  15.4 53.8 %all-to-all-start = ((bf16[8,64,896]{2,1,0:T(8,128)(2,1)}), bf16[8,64,896]{2,1,0:T(8,128)(2,1)S(1)}, u32[]{:S(2)}, u32[]{:S(2)}) async-start(bf16[8,64,896]{2,1,0:T(8,128)(2,1)} %qkv_blocks.1), calls=%async_computation | async-start | bytes 1835008 | tf_op jit(solution)/shard_map/all_to_all | solution.py:697
  42.1 27.1 %collective-permute-start.3 = (bf16[192,2048]{1,0:T(8,128)(2,1)}, bf16[192,2048]{1,0:T(8,128)(2,1)}, u32[]{:S(2)}, u32[]{:S(2)}) collective-permute-start(bf16[192,2048]{1,0:T(8,128)(2,1)} %slice.213), channel_id=1, source_target_pairs={{0,16},{8,24},{16,0},{24,8},{1,17},{9,25},{17,1},{25,9},{2,18},{10... | collective-permute-start | bytes 2359304 | tf_op jit(solution)/shard_map/ppermute | solution.py:619
  47.2 22.0 %collective-permute-start.1 = (bf16[128,2048]{1,0:T(8,128)(2,1)S(1)}, bf16[128,2048]{1,0:T(8,128)(2,1)S(1)}, u32[]{:S(2)}, u32[]{:S(2)}) collective-permute-start(bf16[128,2048]{1,0:T(8,128)(2,1)S(1)} %slice.212), channel_id=1, source_target_pairs={{0,8},{8,0},{16,24},{24,16},{1,9},{9,1},{17,25},{25,17},{2,10},{10... | collective-permute-start | bytes 1572872 | tf_op jit(solution)/shard_map/ppermute | solution.py:615
  70.0 40.7 %all-to-all-start.1 = ((bf16[8,64,1024]{2,1,0:T(8,128)(2,1)}), bf16[8,64,1024]{2,1,0:T(8,128)(2,1)S(1)}, u32[]{:S(2)}, u32[]{:S(2)}) async-start(bf16[8,64,1024]{2,1,0:T(8,128)(2,1)} %up_blocks.1), calls=%async_computation.1 | async-start | bytes 2097152 | tf_op jit(solution)/shard_map/all_to_all | solution.py:708
  73.6 113.7 %all-gather.4.cloned.1.call-start = ((), (), s32[]{:S(2)}) async-start(), calls=%async_computation.9 | async-start | bytes 4718592 | tf_op jit(solution)/shard_map/all_gather | solution.py:720
  73.7 22.6 %collective-permute-start.5 = (bf16[512,896]{1,0:T(8,128)(2,1)S(1)}, bf16[512,896]{1,0:T(8,128)(2,1)S(1)}, u32[]{:S(2)}, u32[]{:S(2)}) collective-permute-start(bf16[512,896]{1,0:T(8,128)(2,1)S(1)} %bitcast.119), channel_id=1, source_target_pairs={{0,16},{8,24},{16,0},{24,8},{1,17},{9,25},{17,1},{25,9},{2,18},{10... | collective-permute-start | bytes 2752520 | tf_op jit(solution)/shard_map/ppermute | solution.py:619
  73.7 22.7 %collective-permute-start.4 = (bf16[512,896]{1,0:T(8,128)(2,1)S(1)}, bf16[512,896]{1,0:T(8,128)(2,1)}, u32[]{:S(2)}, u32[]{:S(2)}) collective-permute-start(bf16[512,896]{1,0:T(8,128)(2,1)S(1)} %bitcast.120), channel_id=1, source_target_pairs={{0,8},{8,0},{16,24},{24,16},{1,9},{9,1},{17,25},{25,17},{2,10},{10... | collective-permute-start | bytes 2752520 | tf_op jit(solution)/shard_map/ppermute | solution.py:615
  112.0 41.1 %all-to-all-start.2 = ((bf16[4,64,2048]{2,1,0:T(8,128)(2,1)}), bf16[4,64,2048]{2,1,0:T(8,128)(2,1)S(1)}, u32[]{:S(2)}, u32[]{:S(2)}) async-start(bf16[4,64,2048]{2,1,0:T(8,128)(2,1)} %out_rows.1), calls=%async_computation.2 | async-start | bytes 2097152 | tf_op jit(solution)/shard_map/all_to_all | solution.py:722
  115.6 134.6 %reduce-scatter.3.cloned.1.call-start = ((), (), s32[]{:S(2)}) async-start(), calls=%async_computation.8 | async-start | bytes 4718592 | tf_op jit(solution)/shard_map/reduce_scatter | solution.py:749
  117.1 25.6 %collective-permute-start.9 = (bf16[512,1024]{1,0:T(8,128)(2,1)S(1)}, bf16[512,1024]{1,0:T(8,128)(2,1)S(1)}, u32[]{:S(2)}, u32[]{:S(2)}) collective-permute-start(bf16[512,1024]{1,0:T(8,128)(2,1)S(1)} %bitcast.124), channel_id=1, source_target_pairs={{0,16},{8,24},{16,0},{24,8},{1,17},{9,25},{17,1},{25,9},{2,18},{10... | collective-permute-start | bytes 3145736 | tf_op jit(solution)/shard_map/ppermute | solution.py:619
  118.1 25.3 %collective-permute-start.8 = (bf16[512,1024]{1,0:T(8,128)(2,1)S(1)}, bf16[512,1024]{1,0:T(8,128)(2,1)}, u32[]{:S(2)}, u32[]{:S(2)}) collective-permute-start(bf16[512,1024]{1,0:T(8,128)(2,1)S(1)} %bitcast.125), channel_id=1, source_target_pairs={{0,8},{8,0},{16,24},{24,16},{1,9},{9,1},{17,25},{25,17},{2,10},{10... | collective-permute-start | bytes 3145736 | tf_op jit(solution)/shard_map/ppermute | solution.py:615
  192.7 39.4 %all-to-all-start.3 = ((bf16[4,64,2048]{2,1,0:T(8,128)(2,1)}), bf16[4,64,2048]{2,1,0:T(8,128)(2,1)S(1)}, u32[]{:S(2)}, u32[]{:S(2)}) async-start(bf16[4,64,2048]{2,1,0:T(8,128)(2,1)} %bitcast.31), calls=%async_computation.4 | async-start | bytes 2097152 | tf_op jit(solution)/shard_map/all_to_all | solution.py:752
  196.3 175.3 %reduce-scatter.5.cloned.1.call-start = ((), (), s32[]{:S(2)}) async-start(), calls=%async_computation.10 | async-start | bytes 4718592 | tf_op jit(solution)/shard_map/reduce_scatter | solution.py:793
  277.2 45.7 %all-to-all-start.4 = ((bf16[8,64,1024]{2,1,0:T(8,128)(2,1)}), bf16[8,64,1024]{2,1,0:T(8,128)(2,1)S(1)}, u32[]{:S(2)}, u32[]{:S(2)}) async-start(bf16[8,64,1024]{2,1,0:T(8,128)(2,1)} %bitcast.115), calls=%async_computation.6 | async-start | bytes 2097152 | tf_op jit(solution)/shard_map/all_to_all | solution.py:803
  282.5 17.3 %collective-permute-start.22 = (bf16[256,896]{1,0:T(8,128)(2,1)}, bf16[256,896]{1,0:T(8,128)(2,1)S(1)}, u32[]{:S(2)}, u32[]{:S(2)}) collective-permute-start(bf16[256,896]{1,0:T(8,128)(2,1)} %get-tuple-element.211), channel_id=1, source_target_pairs={{0,8},{8,0},{16,24},{24,16},{1,9},{9,1},{17,25},{25,17},{2,10},{10... | collective-permute-start | bytes 1376264 | tf_op jit(solution)/shard_map/ppermute | solution.py:615
  284.8 21.1 %collective-permute-start.24 = (bf16[256,896]{1,0:T(8,128)(2,1)}, bf16[256,896]{1,0:T(8,128)(2,1)S(1)}, u32[]{:S(2)}, u32[]{:S(2)}) collective-permute-start(bf16[256,896]{1,0:T(8,128)(2,1)} %get-tuple-element.213), channel_id=1, source_target_pairs={{0,8},{8,0},{16,24},{24,16},{1,9},{9,1},{17,25},{25,17},{2,10},{10... | collective-permute-start | bytes 1376264 | tf_op jit(solution)/shard_map/ppermute | solution.py:615
  285.5 21.5 %collective-permute-start.25 = (bf16[256,896]{1,0:T(8,128)(2,1)}, bf16[256,896]{1,0:T(8,128)(2,1)S(1)}, u32[]{:S(2)}, u32[]{:S(2)}) collective-permute-start(bf16[256,896]{1,0:T(8,128)(2,1)} %get-tuple-element.214), channel_id=1, source_target_pairs={{0,16},{8,24},{16,0},{24,8},{1,17},{9,25},{17,1},{25,9},{2,18},{10... | collective-permute-start | bytes 1376264 | tf_op jit(solution)/shard_map/ppermute | solution.py:619
  287.4 27.1 %collective-permute-start.29 = (bf16[32,2048]{1,0:T(8,128)(2,1)}, bf16[32,2048]{1,0:T(8,128)(2,1)}, u32[]{:S(2)}, u32[]{:S(2)}) collective-permute-start(bf16[32,2048]{1,0:T(8,128)(2,1)} %add_convert_fusion.10), channel_id=1, source_target_pairs={{0,8},{8,0},{16,24},{24,16},{1,9},{9,1},{17,25},{25,17},{2,10},{10... | collective-permute-start | bytes 393224 | tf_op jit(solution)/shard_map/ppermute | solution.py:615
  324.9 22.7 %collective-permute-start.32 = (bf16[128,2048]{1,0:T(8,128)(2,1)}, bf16[128,2048]{1,0:T(8,128)(2,1)}, u32[]{:S(2)}, u32[]{:S(2)}) collective-permute-start(bf16[128,2048]{1,0:T(8,128)(2,1)} %get-tuple-element.244), channel_id=1, source_target_pairs={{0,8},{8,0},{16,24},{24,16},{1,9},{9,1},{17,25},{25,17},{2,10},{10... | collective-permute-start | bytes 1572872 | tf_op jit(solution)/shard_map/ppermute | solution.py:615
  325.6 23.3 %collective-permute-start.33 = (bf16[128,2048]{1,0:T(8,128)(2,1)}, bf16[128,2048]{1,0:T(8,128)(2,1)}, u32[]{:S(2)}, u32[]{:S(2)}) collective-permute-start(bf16[128,2048]{1,0:T(8,128)(2,1)} %get-tuple-element.247), channel_id=1, source_target_pairs={{0,16},{8,24},{16,0},{24,8},{1,17},{9,25},{17,1},{25,9},{2,18},{10... | collective-permute-start | bytes 1572872 | tf_op jit(solution)/shard_map/ppermute | solution.py:619
  329.9 28.1 %all-to-all-start.5 = ((bf16[8,64,896]{2,1,0:T(8,128)(2,1)}), bf16[8,64,896]{2,1,0:T(8,128)(2,1)S(1)}, u32[]{:S(2)}, u32[]{:S(2)}) async-start(bf16[8,64,896]{2,1,0:T(8,128)(2,1)} %bitcast.118), calls=%async_computation.7 | async-start | bytes 1835008 | tf_op jit(solution)/shard_map/all_to_all | solution.py:814
  (80 other events, 847.9 us)
Sparse Core Ops, SparseCore 0:
  9.7 69.4 all-gather.5
  110.9 54.4 all-gather.3
  187.4 62.7 reduce-scatter.2
  252.3 63.6 reduce-scatter.4

commit v4 on v3

--- a/solution.py
+++ b/solution.py
@@ -401,23 +401,6 @@
         [shape((n, h), BF16), shape((n, h), F32)], [tile(h)] * 2,
         [pltpu.VMEM((w, h), BF16)], (n // TILE,), flops=2 * n * w * h)
 
-def mlp_backward_body(dp, g, d0, dx, dy, d1, d2, slope, d_hidden, sums, full):
-    @pl.when(pl.program_id(0) == 0)
-    def _():
-        fill(dp[0], full, (d0, dx, dy, d1, d2))
-        sums[...] = jnp.zeros_like(sums)
-    low = (slope[...] * dot(g[...], full[...], (1, 1))).astype(BF16)
-    d_hidden[...] = low
-    sums[...] += jnp.sum(low.astype(F32), axis=0, keepdims=True)
-
-def mlp_backward(dp, g, down, slope):
-    n, w = g.shape
-    h = slope.shape[1]
-    return run(mlp_backward_body, "mlp_backward", dp, [g, *down, slope],
-        [tile(w)] + [whole(p.shape) for p in down] + [tile(h)],
-        [shape((n, h), BF16), shape((1, h), F32)], [tile(h), whole((1, h))],
-        [pltpu.VMEM((h, w), BF16)], (n // TILE,), flops=2 * n * w * h)
-
 def masked_scores(index, q, keys, seg_q, seg_k):
     reach = keys.shape[0]
     scores = dot(q, keys, (1, 1)) * (1.0 / math.sqrt(HEAD))
@@ -451,46 +434,6 @@
         [shape((n, HEAD), F32), shape((n, HEAD), BF16), shape((n, 1), F32)],
         [tile(HEAD)] * 2 + [tile(1)], [], (n // TILE,), flops=3 * n * n * HEAD)
 
-def attend_backward_body(dp, q, k, v, g, w_out, context, log_sum, seg_q, seg_k, cos, s1, s2, kcos, ks1, ks2, dq, dk, dv, sums, dk_acc, dv_acc):
-    step = pl.program_id(0)
-    count = k.shape[0] // TILE
-    scale = 1.0 / math.sqrt(HEAD)
-    @pl.when(step == 0)
-    def _():
-        sums[...] = jnp.zeros_like(sums)
-        dk_acc[...] = jnp.zeros_like(dk_acc)
-        dv_acc[...] = jnp.zeros_like(dv_acc)
-    d_ctx = dot(g[...], w_out[...], (1, 1)).astype(BF16)
-    def block(index, reach):
-        keys, values = k[0:reach, :], v[0:reach, :]
-        scores, allowed = masked_scores(index, q[...], keys, seg_q, seg_k)
-        probs = jnp.where(allowed, jnp.exp(scores - log_sum[...]), 0.0)
-        delta = jnp.sum(d_ctx.astype(F32) * context[...], axis=1, keepdims=True)
-        d_scores = (probs * (dot(d_ctx, values, (1, 1)) - delta)).astype(BF16)
-        d_q = dot(d_scores, keys, (1, 0)) * scale
-        low = turn(d_q, cos[...], -s1[...], -s2[...]).astype(BF16)
-        dq[...] = low
-        sums[:, 0:HEAD] += jnp.sum(low.astype(F32), axis=0, keepdims=True)
-        dk_acc[0:reach, :] += dot(d_scores, q[...], (0, 0))
-        dv_acc[0:reach, :] += dot(probs.astype(BF16), d_ctx, (0, 0))
-    each_tile(count, block)
-    @pl.when(step == count - 1)
-    def _():
-        low_k = turn(dk_acc[...] * scale, kcos[...], -ks1[...], -ks2[...]).astype(BF16)
-        low_v = dv_acc[...].astype(BF16)
-        dk[...] = low_k
-        dv[...] = low_v
-        sums[:, HEAD:2 * HEAD] = jnp.sum(low_k.astype(F32), axis=0, keepdims=True)
-        sums[:, 2 * HEAD:] = jnp.sum(low_v.astype(F32), axis=0, keepdims=True)
-
-def attend_backward(dp, q, k, v, g, w_out, context, log_sum, seg_col, seg_row, tables):
-    n = q.shape[0]; w = g.shape[1]
-    return run(attend_backward_body, "attend_backward", dp, [q, k, v, g, w_out, context, log_sum, seg_col, seg_row, *tables, *tables],
-        [tile(HEAD), whole(k.shape), whole(v.shape), tile(w), whole(w_out.shape), tile(HEAD), tile(1), tile(1), whole(seg_row.shape)] + [tile(128)] * 3 + [whole((n, 128))] * 3,
-        [shape((n, HEAD), BF16)] * 3 + [shape((1, 3 * HEAD), F32)],
-        [tile(HEAD)] + [whole((n, HEAD))] * 2 + [whole((1, 3 * HEAD))],
-        [pltpu.VMEM((n, HEAD), F32)] * 2, (n // TILE,), flops=2 * n * w * HEAD + 6 * n * n * HEAD)
-
 def output_body(dp, ctx, active, w_out, d0, dx, dy, d1, d2, out, full):
     @pl.when(pl.program_id(0) == 0)
     def _():
@@ -503,55 +446,249 @@
         [tile(HEAD), tile(h), whole(w_out.shape)] + [whole(p.shape) for p in down],
         [shape((n, w), BF16)], [tile(w)], [pltpu.VMEM((h, w), BF16)], (n // TILE,), flops=2 * n * w * (h + HEAD))[0]
 
-def inward_body(dp, x, dq, dk, dv, d_hidden, w0, wx, wy, w1, w2, u0, ux, uy, u1, u2, vec, u, sums, full_qkv, full_up):
-    @pl.when(pl.program_id(0) == 0)
-    def _():
-        fill(dp[0], full_qkv, (w0, wx, wy, w1, w2))
-        fill(dp[0], full_up, (u0, ux, uy, u1, u2))
-        sums[...] = jnp.zeros_like(sums)
-    normed, _ = norm_tile(x[...])
-    d_joined = jnp.concatenate([dq[...], dk[...], dv[...]], axis=1)
-    d_first = dot(d_joined, full_qkv[...], (1, 1))
-    d_second = dot(d_hidden[...], full_up[...], (1, 1))
-    u[...] = (d_first * vec[0:1, :] + d_second * vec[2:3, :]).astype(BF16)
-    sums[0:1, :] += jnp.sum(d_first * normed, axis=0, keepdims=True)
-    sums[1:2, :] += jnp.sum(d_first, axis=0, keepdims=True)
-    sums[2:3, :] += jnp.sum(d_second * normed, axis=0, keepdims=True)
-    sums[3:4, :] += jnp.sum(d_second, axis=0, keepdims=True)
-
-def inward(dp, x, dq, dk, dv, d_hidden, wq, up, vec):
-    n, w = x.shape; h = d_hidden.shape[1]
-    return run(inward_body, "inward", dp, [x, dq, dk, dv, d_hidden, *wq, *up, vec],
-        [tile(w)] + [tile(HEAD)] * 3 + [tile(h)] + [whole(p.shape) for p in (*wq, *up, vec)],
-        [shape((n, w), BF16), shape((4, w), F32)], [tile(w), whole((4, w))],
-        [pltpu.VMEM((w, 3 * HEAD), BF16), pltpu.VMEM((w, h), BF16)], (n // TILE,), flops=2 * n * w * (h + 3 * HEAD))
-
-def terms_body(count, extra, dp, left, *refs):
-    rights, outs = refs[:count], refs[count + extra :]
-    right = rights[0][...] if count == 1 else jnp.concatenate([r[...] for r in rights], axis=1)
-    cols = right.shape[1]
-    for place in range(4):
-        @pl.when(pl.program_id(0) == place)
-        def _(place=place):
-            term = dot(left[...], right, (0, 0)).astype(BF16)
-            half = term.shape[0] // 2
-            parts = [outs[6]] if place == 3 else [outs[2 * place], outs[2 * place + 1]]
-            for part, out in enumerate(parts):
-                rows = out.shape[0]
-                out[:, 0:cols] = term[part * half : part * half + rows]
-                if extra:
-                    out[:, cols:] = refs[count][part * half : part * half + rows, :]
-
-def order_mask(step):
-    return jnp.where(step == 0, 3, jnp.where(step == 3, 0, step))
-
-def terms(dp, left, rights, name, extra=()):
-    n, w = left.shape; rows = w // 4; cols = sum(r.shape[1] for r in (*rights, *extra))
-    outs = [shape((rows // 2, cols), BF16)] * 6 + [shape((rows, cols), BF16)]
-    return run(functools.partial(terms_body, len(rights), len(extra)), name, dp, [left, *rights, *extra],
-        [pl.BlockSpec((n, rows), lambda i, d: (0, d[0] ^ order_mask(i)))] + [whole(r.shape) for r in rights]
-        + [pl.BlockSpec((rows, e.shape[1]), lambda i, d: (d[0] ^ order_mask(i), 0)) for e in extra],
-        outs, [whole(o.shape) for o in outs], [], (4,), flops=2 * n * w * cols)
+SLAB = 512
+
+def sections(half):
+    return (
+        (0, 0, 3, 0, half),
+        (1, half, 3, half, half),
+        (0, half, 1, 0, half),
+        (1, 0, 2, half, half),
+        (2, 0, 1, half, half),
+        (3, 0, 2, 0, half),
+        (4, 0, 0, 0, half),
+        (4, half, 0, half, half),
+    )
+
+def term_shapes(rows, cols):
+    counts = (rows, rows, rows // 2, rows // 2, rows)
+    return [shape((count, cols), BF16) for count in counts]
+
+class Copies:
+    def __init__(self, sems):
+        self.sems, self.count = sems, 0
+
+    def start(self, source, target):
+        copy = pltpu.make_async_copy(source, target, self.sems.at[self.count])
+        self.count += 1
+        copy.start()
+        return copy
+
+    def lay(self, dp, full, pieces):
+        take, cols = full.shape[0] // 4, full.shape[1]
+        cut = pieces[3].shape[0]
+        copies = []
+        for mask in range(3):
+            at = pl.multiple_of((dp ^ mask) * take, 16)
+            copies.append(
+                self.start(pieces[mask].at[pl.ds(0, take), pl.ds(0, cols)], full.at[pl.ds(at, take), :])
+            )
+        far = (dp ^ 3) * take
+        copies.append(
+            self.start(pieces[3].at[:, pl.ds(0, cols)], full.at[pl.ds(pl.multiple_of(far, 16), cut), :])
+        )
+        copies.append(
+            self.start(
+                pieces[4].at[pl.ds(0, take - cut), pl.ds(0, cols)],
+                full.at[pl.ds(pl.multiple_of(far + cut, 16), take - cut), :],
+            )
+        )
+        return copies
+
+    def slabs(self, source, target):
+        return [
+            self.start(source.at[pl.ds(at, SLAB), :], target.at[pl.ds(at, SLAB), :])
+            for at in range(0, source.shape[0], SLAB)
+        ]
+
+    def send_terms(self, dp, staged, outs):
+        rows = staged.shape[0] // 4
+        sent = []
+        for out, at, mask, low, count in sections(rows // 2):
+            source = pl.multiple_of((dp ^ mask) * rows + low, rows // 2)
+            sent.append(self.start(staged.at[pl.ds(source, count), :], outs[out].at[pl.ds(at, count), :]))
+        return sent
+
+def wait_all(copies):
+    for copy in copies:
+        copy.wait()
+
+def anywhere(count):
+    return [pl.BlockSpec(memory_space=pl.ANY)] * count
+
+def middle_body(dp, *refs):
+    slope, g, d0, dx, dy, d1, d2, second, context = refs[:9]
+    d_hidden, sums, attn_terms = refs[9:12]
+    up_outs = refs[12:17]
+    s_slope, s_g, full, s_second, s_context, s_hidden, staged, s_attn, sems = refs[17:]
+    me = dp[0]
+    copies = Copies(sems)
+    got_full = copies.lay(me, full, (d0, dx, dy, d1, d2))
+    got_g, got_slope = [], []
+    n = g.shape[0]
+    spans = [pl.ds(at, SLAB) for at in range(0, n, SLAB)]
+    for span in spans:
+        got_g.append(copies.start(g.at[span, :], s_g.at[span, :]))
+        got_slope.append(copies.start(slope.at[span, :], s_slope.at[span, :]))
+    got_second = copies.slabs(second, s_second)
+    got_context = copies.start(context, s_context)
+    wait_all(got_full)
+    sent = []
+    total = jnp.zeros(sums.shape, F32)
+    for index, span in enumerate(spans):
+        got_g[index].wait()
+        got_slope[index].wait()
+        low = (s_slope[span, :] * dot(s_g[span, :], full[...], (1, 1))).astype(BF16)
+        s_hidden[span, :] = low
+        total += jnp.sum(low.astype(F32), axis=0, keepdims=True)
+        sent.append(copies.start(s_hidden.at[span, :], d_hidden.at[span, :]))
+    sums[...] = total
+    wait_all(got_second)
+    for at in range(0, staged.shape[0], 1024):
+        staged[at : at + 1024, :] = dot(s_second[:, at : at + 1024], s_hidden[...], (0, 0)).astype(BF16)
+    sent += copies.send_terms(me, staged, up_outs)
+    got_context.wait()
+    s_attn[...] = dot(s_context[...], s_g[...], (0, 0)).astype(BF16)
+    sent.append(copies.start(s_attn, attn_terms))
+    wait_all(sent)
+
+def middle(dp, slope, g, down, second, context):
+    n, w = second.shape
+    h = slope.shape[1]
+    rows = w // 4
+    outs = [shape((n, h), BF16), shape((1, h), F32), shape((HEAD, w), BF16)]
+    outs += term_shapes(rows, h)
+    result = run(middle_body, "middle", dp, [slope, g, *down, second, context],
+        anywhere(9), outs, anywhere(1) + [whole((1, h))] + anywhere(6),
+        [pltpu.VMEM((n, h), F32), pltpu.VMEM((n, w), BF16), pltpu.VMEM((h, w), BF16), pltpu.VMEM((n, w), BF16),
+         pltpu.VMEM((n, HEAD), BF16), pltpu.VMEM((n, h), BF16),
+         pltpu.VMEM((w, h), BF16), pltpu.VMEM((HEAD, w), BF16), pltpu.SemaphoreType.DMA((40,))],
+        (1,), flops=4 * n * w * h)
+    return result[0], result[1], result[2], result[3:]
+
+def last_body(dp, *refs):
+    q, k, v, wide, log_sum, seg_q, seg_k, cos, s1, s2, vec = refs[:11]
+    g, w_out, first, x, hidden = refs[11:16]
+    w_pieces, u_pieces = refs[16:21], refs[21:26]
+    sums_joined, sums_norm, u_terms = refs[26:29]
+    qkv_outs = refs[29:34]
+    (s_g, s_w_out, s_first, s_x, s_hidden, full_qkv, full_up,
+     s_dj, dk_acc, dv_acc, staged, s_u, sems) = refs[34:]
+    me = dp[0]
+    copies = Copies(sems)
+    got_w_out = copies.start(w_out, s_w_out)
+    n = q.shape[0]
+    got_g = copies.slabs(g, s_g)
+    got_first = copies.slabs(first, s_first)
+    got_full = copies.lay(me, full_qkv, w_pieces) + copies.lay(me, full_up, u_pieces)
+    got_x = copies.slabs(x, s_x)
+    got_hidden = copies.slabs(hidden, s_hidden)
+    scale = 1.0 / math.sqrt(HEAD)
+    dk_acc[...] = jnp.zeros_like(dk_acc)
+    dv_acc[...] = jnp.zeros_like(dv_acc)
+    got_w_out.wait()
+    total_q = jnp.zeros((1, HEAD), F32)
+    for index in range(n // TILE):
+        span = pl.ds(index * TILE, TILE)
+        reach = (index + 1) * TILE
+        if index * TILE % SLAB == 0:
+            got_g[index * TILE // SLAB].wait()
+        d_ctx = dot(s_g[span, :], s_w_out[...], (1, 1)).astype(BF16)
+        keys, values, queries = k[0:reach, :], v[0:reach, :], q[span, :]
+        scores, allowed = masked_scores(index, queries, keys, seg_q.at[span, :], seg_k)
+        probs = jnp.where(allowed, jnp.exp(scores - log_sum[span, :]), 0.0)
+        delta = jnp.sum(d_ctx.astype(F32) * wide[span, :], axis=1, keepdims=True)
+        d_scores = (probs * (dot(d_ctx, values, (1, 1)) - delta)).astype(BF16)
+        d_q = dot(d_scores, keys, (1, 0)) * scale
+        low_q = turn(d_q, cos[span, :], -s1[span, :], -s2[span, :]).astype(BF16)
+        s_dj[span, 0:HEAD] = low_q
+        total_q += jnp.sum(low_q.astype(F32), axis=0, keepdims=True)
+        dk_acc[0:reach, :] += dot(d_scores, queries, (0, 0))
+        dv_acc[0:reach, :] += dot(probs.astype(BF16), d_ctx, (0, 0))
+    low_k = turn(dk_acc[...] * scale, cos[...], -s1[...], -s2[...]).astype(BF16)
+    low_v = dv_acc[...].astype(BF16)
+    s_dj[:, HEAD : 2 * HEAD] = low_k
+    s_dj[:, 2 * HEAD :] = low_v
+    sums_joined[:, 0:HEAD] = total_q
+    sums_joined[:, HEAD : 2 * HEAD] = jnp.sum(low_k.astype(F32), axis=0, keepdims=True)
+    sums_joined[:, 2 * HEAD :] = jnp.sum(low_v.astype(F32), axis=0, keepdims=True)
+    wait_all(got_first)
+    for at in range(0, staged.shape[0], 1024):
+        staged[at : at + 1024, :] = dot(s_first[:, at : at + 1024], s_dj[...], (0, 0)).astype(BF16)
+    sent = copies.send_terms(me, staged, qkv_outs)
+    wait_all(got_full)
+    sums_norm[...] = jnp.zeros_like(sums_norm)
+    for index in range(n // TILE):
+        span = pl.ds(index * TILE, TILE)
+        if index * TILE % SLAB == 0:
+            got_x[index * TILE // SLAB].wait()
+            got_hidden[index * TILE // SLAB].wait()
+        d_first = dot(s_dj[span, :], full_qkv[...], (1, 1))
+        d_second = dot(s_hidden[span, :], full_up[...], (1, 1))
+        s_u[span, :] = (d_first * vec[0:1, :] + d_second * vec[2:3, :]).astype(BF16)
+        sent.append(copies.start(s_u.at[span, :], u_terms.at[span, :]))
+        normed, _ = norm_tile(s_x[span, :])
+        sums_norm[0:1, :] += jnp.sum(d_first * normed, axis=0, keepdims=True)
+        sums_norm[1:2, :] += jnp.sum(d_first, axis=0, keepdims=True)
+        sums_norm[2:3, :] += jnp.sum(d_second * normed, axis=0, keepdims=True)
+        sums_norm[3:4, :] += jnp.sum(d_second, axis=0, keepdims=True)
+    wait_all(sent)
+
+def last(dp, q, k, v, wide, log_sum, seg_col, seg_row, tables, vec, g, w_out, first, x, hidden, w_in, up):
+    n, w = x.shape
+    h = hidden.shape[1]
+    rows = w // 4
+    near = [q, k, v, wide, log_sum, seg_col, seg_row, *tables, vec]
+    outs = [shape((1, 3 * HEAD), F32), shape((4, w), F32), shape((n, w), BF16)]
+    outs += term_shapes(rows, 3 * HEAD)
+    result = run(last_body, "last", dp, [*near, g, w_out, first, x, hidden, *w_in, *up],
+        [whole(a.shape) for a in near] + anywhere(15), outs,
+        [whole((1, 3 * HEAD)), whole((4, w))] + anywhere(6),
+        [pltpu.VMEM((n, w), BF16), pltpu.VMEM((HEAD, w), BF16), pltpu.VMEM((n, w), BF16),
+         pltpu.VMEM((n, w), BF16), pltpu.VMEM((n, h), BF16), pltpu.VMEM((w, 3 * HEAD), BF16), pltpu.VMEM((w, h), BF16),
+         pltpu.VMEM((n, 3 * HEAD), BF16), pltpu.VMEM((n, HEAD), F32), pltpu.VMEM((n, HEAD), F32),
+         pltpu.VMEM((w, 3 * HEAD), BF16), pltpu.VMEM((n, w), BF16),
+         pltpu.SemaphoreType.DMA((48,))],
+        (1,), flops=2 * n * w * (4 * HEAD + 3 * HEAD + h) + 6 * n * n * HEAD)
+    return result[0], result[1], result[2], result[3:]
+
+def outward_body(dp, *refs):
+    left, right, attn = refs[:3]
+    outs = refs[3:8]
+    s_left, s_right, s_attn, staged, sems = refs[8:]
+    me = dp[0]
+    copies = Copies(sems)
+    got_right = copies.slabs(right, s_right)
+    got_left = copies.start(left, s_left)
+    got_attn = copies.start(attn, s_attn)
+    rows, extra = staged.shape[0] // 4, attn.shape[1]
+    half, part = rows // 2, extra // 2
+    one = half + part
+    wait_all(got_right)
+    got_left.wait()
+    staged[...] = dot(s_left[...], s_right[...], (0, 0)).astype(BF16)
+    got_attn.wait()
+    sent = []
+    for out, at, mask, low, _ in sections(half):
+        source = pl.multiple_of((me ^ mask) * rows + low, half)
+        at = one if at else 0
+        target = outs[out]
+        sent.append(copies.start(staged.at[pl.ds(source, half), :], target.at[pl.ds(at, half), :]))
+        source = part if low else 0
+        sent.append(
+            copies.start(
+                s_attn.at[me ^ mask, pl.ds(source, part), :], target.at[pl.ds(at + half, part), :]
+            )
+        )
+    wait_all(sent)
+
+def outward(dp, left, right, attn):
+    n, h = left.shape; w = right.shape[1]
+    outs = term_shapes(h // 4 + attn.shape[1], w)
+    return run(outward_body, "outward", dp, [left, right, attn], anywhere(3), outs, anywhere(5),
+        [pltpu.VMEM((n, h), BF16), pltpu.VMEM((n, w), BF16), pltpu.VMEM(attn.shape, BF16),
+         pltpu.VMEM((h, w), BF16), pltpu.SemaphoreType.DMA((24,))],
+        (1,), flops=2 * n * h * w)
 
 
 def up_blocks_body(source, out):
@@ -619,21 +756,59 @@
     return lax.ppermute(block, "dp", swap(4, 2))
 
 
-def pass_on(near, far):
-    _, x_low, y_top, _ = near
-    far_x, far_y = far
-    got_y_top = over_y((y_top.astype(F32) + far_x.astype(F32)).astype(BF16))
-    got_x_low = over_x((x_low.astype(F32) + far_y.astype(F32)).astype(BF16))
-    return got_y_top, got_x_low
-
-
-def reduce_last(own, near, then, kind):
-    half = own.shape[0] // 2
-    got_x_top, got_y_low = near
-    got_y_top, got_x_low = then
-    top = own[:half].astype(F32) + got_x_top.astype(F32) + got_y_top.astype(F32)
-    low = own[half:].astype(F32) + got_x_low.astype(F32) + got_y_low.astype(F32)
-    return jnp.concatenate([top.astype(kind), low.astype(kind)], axis=0)
+def small_call(body, name, outs, *sources):
+    return pl.pallas_call(
+        body,
+        name=name,
+        out_shape=outs,
+        compiler_params=pltpu.CompilerParams(vmem_limit_bytes=56 * 2**20),
+        cost_estimate=pl.CostEstimate(flops=0, bytes_accessed=sources[0].size * 8, transcendentals=0),
+    )(*sources)
+
+
+def send_both(terms):
+    return over_x(terms[0]), over_y(terms[1])
+
+
+def pass_on_body(x_low, y_top, got_x, got_y, to_x, to_y):
+    half = x_low.shape[0]
+    to_y[...] = (y_top[...].astype(F32) + got_x[:half].astype(F32)).astype(BF16)
+    to_x[...] = (x_low[...].astype(F32) + got_y[half:].astype(F32)).astype(BF16)
+
+
+def pass_on(terms, got):
+    out = jax.ShapeDtypeStruct(terms[2].shape, BF16)
+    to_x, to_y = small_call(pass_on_body, "pass_on", (out, out), terms[2], terms[3], *got)
+    return over_x(to_x), over_y(to_y)
+
+
+def reduce_last_body(own, got_x, got_y, x_low, y_top, out):
+    half = x_low.shape[0]
+    top = got_x[half:].astype(F32) + y_top[...].astype(F32)
+    low = got_y[:half].astype(F32) + x_low[...].astype(F32)
+    out[:half] = (own[:half].astype(F32) + top).astype(out.dtype)
+    out[half:] = (own[half:].astype(F32) + low).astype(out.dtype)
+
+
+def reduce_last(terms, got, then):
+    out = jax.ShapeDtypeStruct(terms[4].shape, BF16)
+    return small_call(reduce_last_body, "reduce_last", out, terms[4], *got, *then)
+
+
+def reduce_both_body(own, got_x, got_y, x_low, y_top, first, second):
+    one = x_low.shape[0]
+    half, part = first.shape[0] // 2, second.shape[0] // 2
+    top = got_x[one:].astype(F32) + y_top[...].astype(F32)
+    low = got_y[:one].astype(F32) + x_low[...].astype(F32)
+    for index, others in enumerate((top, low)):
+        total = own[index * one : (index + 1) * one].astype(F32) + others
+        first[index * half : (index + 1) * half] = total[:half]
+        second[index * part : (index + 1) * part] = total[half:]
+
+
+def reduce_both(terms, got, then, rows, part):
+    outs = [jax.ShapeDtypeStruct((count, terms[4].shape[1]), F32) for count in (rows, part)]
+    return small_call(reduce_both_body, "reduce_both", outs, terms[4], *got, *then)
 
 
 def rotary_lanes(length):
@@ -737,7 +912,7 @@
     first_in, second_in = norms(dp, x_all, norm_vec)
     queries, key_rows, value_rows = qkv(dp, first_in, w_in, bias_qkv, tables)
 
-    up_x, up_y, queries, w_out = stage((up_x, up_y, queries, w_out), (bias_up, seg_col, seg_row))
+    up_x, up_y, queries = stage((up_x, up_y, queries), (bias_up, seg_col, seg_row))
     up = (up_rows, up_x, up_y, over_x(up_y[:half]), over_y(up_x[half:]))
 
     wide_context, context, log_sum = attend_forward(
@@ -745,88 +920,81 @@
     )
     up, context = stage((up, context), ())
     active, slope = mlp_forward(dp, second_in, up, bias_up)
+
     out_terms = output(dp, context, active, w_out, down)
     out_sum = lax.psum_scatter(out_terms, "sp", scatter_dimension=0, tiled=True)
-
-    attn_terms = dot(tie(context, out_terms), g_all, (0, 0)).astype(BF16)
+    d_hidden, up_sums, attn_terms, up_terms = middle(
+        dp, slope, tie(g_all, out_terms), down, second_in, context
+    )
     attn_sent = lax.all_to_all(
         attn_terms.reshape(4, HEAD // 4, width), "sp", 0, 0, tiled=True, axis_index_groups=fours
     )
-    d_hidden, up_sums = mlp_backward(dp, tie(g_all, attn_terms), down, slope)
-    up_terms = terms(dp, second_in, [d_hidden], "up_terms")
-    up_far = over_x(up_terms[0]), over_y(up_terms[1])
-    d_q, d_k, d_v, qkv_sums = attend_backward(
+    up_got = send_both(up_terms)
+    sum_up = lax.dynamic_update_slice(
+        jnp.zeros((4, HEADS, 256), F32), up_sums.reshape(4, 1, 256), (0, sp, 0)
+    )
+    qkv_sums, norm_sums, u_terms, qkv_terms = last(
         dp,
-        tie(queries, up_terms),
+        tie(queries, attn_terms),
         key_rows,
         value_rows,
-        g_all,
-        w_out,
         wide_context,
         log_sum,
         seg_col,
         seg_row,
         tables,
-    )
-    own, to_x, to_y, to_far = (pick(attn_sent, dp ^ mask) for mask in range(4))
-    part = rows // 2
-    attn_near = (to_x[:part], to_x[part:], to_y[:part], to_y[part:])
-    up_near, to_far = stage((up_terms[2:6], to_far), (d_q,))
-    up_near_got = over_x(up_near[0]), over_y(up_near[3])
-    attn_far = over_x(to_far[:part]), over_y(to_far[part:])
+        norm_vec,
+        g_all,
+        w_out,
+        first_in,
+        x_all,
+        d_hidden,
+        w_in,
+        up,
+    )
+    u_terms, up_got, qkv_terms, down_left, norm_sums, attn_sent = stage(
+        (u_terms, up_got, qkv_terms, active, norm_sums, attn_sent), ()
+    )
+    up_then = pass_on(up_terms, up_got)
+    qkv_got = send_both(qkv_terms)
+    u_sum = lax.psum_scatter(u_terms, "sp", scatter_dimension=0, tiled=True)
     sum_qkv = lax.dynamic_update_slice(
         jnp.zeros((3, HEADS, HEAD), F32), qkv_sums.reshape(3, 1, HEAD), (0, head, 0)
     )
-    sum_up = lax.dynamic_update_slice(
-        jnp.zeros((4, HEADS, 256), F32), up_sums.reshape(4, 1, 256), (0, sp, 0)
-    )
-    early = jnp.concatenate(
-        [sum_out.reshape(32, 64), sum_qkv.reshape(32, 192), sum_up.reshape(32, 256)], axis=1
-    )
-    u_terms, norm_sums = inward(
-        dp, tie(x_all, up_far), d_q, d_k, d_v, d_hidden, w_in, up, norm_vec
-    )
-    up_near, attn_near = stage((up_near, attn_near), (up_near_got, attn_far))
-    up_then = pass_on(up_near, up_far)
-    attn_near_got = over_x(attn_near[0]), over_y(attn_near[3])
-    u_terms, early, norm_sums = stage((u_terms, early, norm_sums), (out_sum, up_near_got))
-    u_sum = lax.psum_scatter(u_terms, "sp", scatter_dimension=0, tiled=True)
     totals = jnp.concatenate(
-        [norm_sums.reshape(4, 32, 64).transpose(1, 0, 2).reshape(32, 256), early], axis=1
-    )
-    totals = jnp.pad(totals.astype(BF16).reshape(32, 6, 128), ((0, 0), (0, rows - 6), (0, 0)))
-    totals = totals.reshape(32 * rows, 128)
-    qkv_terms = terms(dp, tie(first_in, u_terms), [d_q, d_k, d_v], "qkv_terms", (totals,))
-
-    qkv_terms, up_then = stage((qkv_terms, up_then), (attn_near_got,))
-    up_sum = reduce_last(up_terms[6], up_near_got, up_then, BF16)
+        [
+            norm_sums.reshape(4, 32, 64).transpose(1, 0, 2).reshape(32, 256),
+            sum_out.reshape(32, 64),
+            sum_qkv.reshape(32, 192),
+            sum_up.reshape(32, 256),
+        ],
+        axis=1,
+    )
+    down_terms = outward(dp, down_left, g_all, attn_sent)
+
+    up_then, qkv_got, down_terms, totals = stage((up_then, qkv_got, down_terms, totals), ())
+    qkv_then = pass_on(qkv_terms, qkv_got)
+    down_got = send_both(down_terms)
+    up_sum = reduce_last(up_terms, up_got, up_then)
     up_back = lax.all_to_all(up_sum.reshape(HEADS, rows, 1024), "sp", 0, 0, tiled=True)
-    qkv_far = over_x(qkv_terms[0]), over_y(qkv_terms[1])
-    qkv_near_got = over_x(qkv_terms[2]), over_y(qkv_terms[5])
-    down_terms = terms(dp, tie(active, up_sum), [g_all], "down_terms")
-
-    qkv_far, qkv_near_got, down_terms = stage((qkv_far, qkv_near_got, down_terms), ())
-    qkv_then = pass_on(qkv_terms[2:6], qkv_far)
-    attn_then = pass_on(attn_near, attn_far)
-
-    qkv_then, down_terms = stage((qkv_then, down_terms), (attn_then, up_back))
-    qkv_sum = reduce_last(qkv_terms[6], qkv_near_got, qkv_then, BF16)
-    qkv_back = lax.all_to_all(qkv_sum.reshape(HEADS, rows, 896), "sp", 0, 0, tiled=True)
-    down_far = over_x(down_terms[0]), over_y(down_terms[1])
-    down_near_got = over_x(down_terms[2]), over_y(down_terms[5])
-
-    down_far, down_terms = stage((down_far, down_terms), (down_near_got, qkv_sum))
-    grad_out = reduce_last(own, attn_near_got, attn_then, F32)
+    qkv_sum = reduce_last(qkv_terms, qkv_got, qkv_then)
+    qkv_sum, out_sum = stage((qkv_sum, out_sum), (up_back,))
+    qkv_back = lax.all_to_all(qkv_sum.reshape(HEADS, rows, 768), "sp", 0, 0, tiled=True)
+
+    down_got = stage(down_got, (qkv_sum,))
+    down_then = pass_on(down_terms, down_got)
     grad_up = repack(
         up_rows_body, "up_rows", jax.ShapeDtypeStruct((rows, HEADS * 1024), F32), up_back
     )
-    down_then = pass_on(down_terms[2:6], down_far)
-    down_then = stage(down_then, (qkv_back, grad_up, grad_out))
-    grad_down = reduce_last(down_terms[6], down_near_got, down_then, F32)
+    owned = lax.all_to_all(tie(totals, qkv_back), everywhere, 0, 0, tiled=True)
+    down_then = stage(down_then, (owned, grad_up))
+    grad_down, grad_out = reduce_both(
+        down_terms, down_got, down_then, w_down.shape[0], w_attn_out.shape[0]
+    )
     grad_qkv = repack(
         qkv_rows_body, "qkv_rows", jax.ShapeDtypeStruct((rows, HEADS * 768), F32), qkv_back
     )
-    owned = jnp.sum(qkv_back[:, :6, 768:].astype(F32), axis=0).reshape(768)
+    owned = jnp.sum(owned, axis=0)
 
     x_wide = x_own.astype(F32)
     block_output = (x_wide + out_sum.astype(F32) + (vectors[4] + vectors[5]))[None]

time: 388 us -> 362 us (0.933)
  other arithmetic: 33.4 us -> 9.92 us
  starting transfers between devices: 62.6 us -> 54.4 us
  Pallas kernels: 117 us -> 122 us
  waiting for transfers between devices: 128 us -> 133 us
  matrix products: 4.44 us -> 0 us
    all_to_all x1, waiting for transfers between devices: 0.01 us -> 21.4 us  [line_shards(): lax.all_to_all(up_sum.reshape(HEADS, rows, 1024), 'sp', 0, 0, tiled=True)]
    pallas_call x0 -> x6, Pallas kernels: none -> 19.8 us  [small_call(): pl.pallas_call(body, name=name, out_shape=outs, compiler_params=pltpu.Com...]
    ppermute x18 -> x12, waiting for transfers between devices: 49.4 us -> 33.1 us  [over_y(): return lax.ppermute(block, 'dp', swap(4, 2))]
    pallas_call x12 -> x9, Pallas kernels: 112 us -> 97.5 us  [run(): pl.pallas_call(body, name=name, grid_spec=pltpu.PrefetchScalarGridSpec(nu...]
    all_to_all x1 -> x2, waiting for transfers between devices: 1.06 us -> 14.6 us  [the longest x1 14.6 us: line_shards(): lax.all_to_all(qkv_sum.reshape(HEADS, rows, 768), 'sp', 0, 0, tiled=True)]
    convert_element_type x10 -> x0, other arithmetic: 12.1 us -> none  [the longest x4 4.55 us: pass_on(): got_y_top = over_y((y_top.astype(F32) + far_x.astype(F32)).astype(BF16))]
    all_to_all x1, waiting for transfers between devices: 9.67 us -> 0.01 us  [line_shards(): lax.all_to_all(out_rows, 'sp', 0, 0, tiled=True, axis_index_groups=fours)]
    ppermute x18 -> x12, starting transfers between devices: 18.4 us -> 13.1 us  [over_y(): return lax.ppermute(block, 'dp', swap(4, 2))]
  transfers between devices with their start and end apart: 46 -> 35, of which waited for: 26 -> 13; matrix products, arithmetic and copies ran while one was open for 13% -> 6% of each run, Pallas kernels for 30% -> 34%
where the time goes in v4:
time: 362 us; the launch traced here: 357 us
  waiting for transfers between devices  133 us (37%)
  Pallas kernels  122 us (34%)
  starting transfers between devices  54.4 us (15%)
  local copies, waits for them, and re-layouts  23 us (6%)
  between operations  14.7 us (4%)
  other arithmetic  9.92 us (3%)
    pallas_call x9, Pallas kernels, run(): pl.pallas_call(body, name=name, grid_spec=pltpu.PrefetchScalarGridSpec(nu...  97.5 us
    ppermute x12, waiting for transfers between devices, over_x(): return lax.ppermute(block, 'dp', swap(4, 1))  46.7 us
    ppermute x12, waiting for transfers between devices, over_y(): return lax.ppermute(block, 'dp', swap(4, 2))  33.1 us
    all_to_all x1, waiting for transfers between devices, line_shards(): lax.all_to_all(up_sum.reshape(HEADS, rows, 1024), 'sp', 0, 0, tiled=True)  21.4 us
    pallas_call x6, Pallas kernels, small_call(): pl.pallas_call(body, name=name, out_shape=outs, compiler_params=pltpu.Com...  19.8 us
    all_to_all x1, waiting for transfers between devices, line_shards(): lax.all_to_all(qkv_blocks, 'sp', 0, 0, tiled=True)  16.7 us
    all_to_all x1, waiting for transfers between devices, line_shards(): lax.all_to_all(qkv_sum.reshape(HEADS, rows, 768), 'sp', 0, 0, tiled=True)  14.6 us
    ppermute x12, starting transfers between devices, over_y(): return lax.ppermute(block, 'dp', swap(4, 2))  13.1 us
  transfers between devices with their start and end apart: 35, of which 13 were waited for; matrix products, arithmetic and copies ran while one was open for 6% of the time, Pallas kernels for 34%

profile of v4, /device:TPU:0, one launch (start us, length us, event | category | flops | bytes accessed | tf_op | source)
XLA Modules:
  0.0 357.5 jit_solution(18182831101884116178)
XLA Ops:
  15.5 4.9 %all-to-all-start = ((bf16[8,64,896]{2,1,0:T(8,128)(2,1)}), bf16[8,64,896]{2,1,0:T(8,128)(2,1)S(1)}, u32[]{:S(2)}, u32[]{:S(2)}) async-start(bf16[8,64,896]{2,1,0:T(8,128)(2,1)} %qkv_blocks.1), calls=%async_computation | async-start | bytes 1835008 | tf_op jit(solution)/shard_map/all_to_all | solution.py:872
  20.6 20.7 %collective-permute-done.2.along_x.dx.refs_3_ = bf16[320,2048]{1,0:T(8,128)(2,1)S(1)} collective-permute-done((bf16[320,2048]{1,0:T(8,128)(2,1)S(1)}, bf16[320,2048]{1,0:T(8,128)(2,1)S(1)}, u32[]{:S(2)}, u32[]{:S(2)}) %collective-permute-start.2) | collective-permute-done | bytes 1310752 | tf_op jit(solution)/shard_map/ppermute | solution.py:752
  52.5 16.7 %all-to-all-done = bf16[8,64,896]{2,1,0:T(8,128)(2,1)S(1)} async-done(((bf16[8,64,896]{2,1,0:T(8,128)(2,1)}), bf16[8,64,896]{2,1,0:T(8,128)(2,1)S(1)}, u32[]{:S(2)}, u32[]{:S(2)}) %all-to-all-start) | async-done | bytes 917536 | tf_op jit(solution)/shard_map/all_to_all | solution.py:872
  70.0 3.6 all-to-all-start.1
  77.2 19.1 %collective-permute-done.5.wy.refs_18_ = bf16[512,896]{1,0:T(8,128)(2,1)S(1)} collective-permute-done((bf16[512,896]{1,0:T(8,128)(2,1)S(1)}, bf16[512,896]{1,0:T(8,128)(2,1)S(1)}, u32[]{:S(2)}, u32[]{:S(2)}) %collective-permute-start.5) | collective-permute-done | bytes 917536 | tf_op jit(solution)/shard_map/ppermute | solution.py:756
  99.6 10.8 %collective-permute-done.7.w2.refs_20_ = bf16[256,896]{1,0:T(8,128)(2,1)S(1)} collective-permute-done((bf16[256,896]{1,0:T(8,128)(2,1)S(1)}, bf16[256,896]{1,0:T(8,128)(2,1)S(1)}, u32[]{:S(2)}, u32[]{:S(2)}) %collective-permute-start.7) | collective-permute-done | bytes 458784 | tf_op jit(solution)/shard_map/ppermute | solution.py:756
  121.6 7.7 %norms.1 = (bf16[1024,2048]{1,0:T(8,128)(2,1)}, bf16[1024,2048]{1,0:T(8,128)(2,1)}) custom-call(s32[1]{0:T(128)} %bitcast.1.dp, bf16[1024,2048]{1,0:T(8,128)(2,1)} %bitcast.89, f32[4,2048]{1,0:T(4,128)} %slice.115.vec.refs_10_), custom_call_target="tpu_custom_call" | custom-call | bytes 12615680 | tf_op jit(solution)/shard_map/norms/pallas_call | solution.py:341
  129.3 8.3 %qkv.1 = (bf16[1024,256]{1,0:T(8,128)(2,1)}, bf16[1024,256]{1,0:T(8,128)(2,1)}, bf16[1024,256]{1,0:T(8,128)(2,1)}) custom-call(s32[1]{0:T(128)} %bitcast.1.dp, bf16[1024,2048]{1,0:T(8,128)(2,1)} %get-tuple-element.117.first.refs_13_, bf16[512,896]{1,0:T(8,128)(2,1)} %bitcast.95, bf16[512,896]{1,0:T(8,128)(2,1)} %collective-permute-done.4.wx.refs_17_, ...), custom_call_target="tpu_custom_call" | custom-call | flops 3221225472 | bytes 11013120 | tf_op jit(solution)/shard_map/qkv/pallas_call | solution.py:341
  143.7 5.7 %attend_forward.1 = (f32[1024,256]{1,0:T(8,128)}, bf16[1024,256]{1,0:T(8,128)(2,1)}, f32[1024,1]{1,0:T(8,128)}) custom-call(s32[1]{0:T(128)} %bitcast.1.dp, bf16[1024,256]{1,0:T(8,128)(2,1)} %get-tuple-element.142.q.refs_0_, bf16[1024,256]{1,0:T(8,128)(2,1)} %get-tuple-element.126.k.refs_1_, bf16[1024,256]{1,0:T(8,128)(2,1)} %get-tuple-element.127.v.refs_2_, ...), custom_call_target="tpu_custom_call" | custom-call | flops 805306368 | bytes 3158016 | tf_op jit(solution)/shard_map/attend_forward/pallas_call | solution.py:341
  149.4 4.6 %collective-permute-done.10.u1.refs_24_ = bf16[256,1024]{1,0:T(8,128)(2,1)S(1)} collective-permute-done((bf16[256,1024]{1,0:T(8,128)(2,1)S(1)}, bf16[256,1024]{1,0:T(8,128)(2,1)S(1)}, u32[]{:S(2)}, u32[]{:S(2)}) %collective-permute-start.10) | collective-permute-done | bytes 524320 | tf_op jit(solution)/shard_map/ppermute | solution.py:752
  155.6 10.8 %mlp_forward.1 = (bf16[1024,1024]{1,0:T(8,128)(2,1)}, f32[1024,1024]{1,0:T(8,128)}) custom-call(s32[1]{0:T(128)} %bitcast.1.dp, bf16[1024,2048]{1,0:T(8,128)(2,1)} %get-tuple-element.123.second.refs_7_, bf16[512,1024]{1,0:T(8,128)(2,1)} %bitcast.99, bf16[512,1024]{1,0:T(8,128)(2,1)} %collective-permute-done.8.ux.refs_22_, ...), custom_call_target="tpu_custom_call" | custom-call | flops 4294967296 | bytes 14684160 | tf_op jit(solution)/shard_map/mlp_forward/pallas_call | solution.py:341
  167.4 10.6 %output.1 = bf16[1024,2048]{1,0:T(8,128)(2,1)} custom-call(s32[1]{0:T(128)} %bitcast.1.dp, bf16[1024,256]{1,0:T(8,128)(2,1)} %get-tuple-element.136.ctx.refs_8_, bf16[1024,1024]{1,0:T(8,128)(2,1)} %get-tuple-element.164.active.refs_0_, bf16[256,2048]{1,0:T(8,128)(2,1)} %bitcast.101, bf16[320,2048]{1,0:T(8,128)(2,1)} %copy-done.5, ...), custom_call_target="tpu_custom_call" | custom-call | flops 5368709120 | bytes 13107200 | tf_op jit(solution)/shard_map/output/pallas_call | solution.py:341
  178.1 16.2 %middle.1 = (bf16[1024,1024]{1,0:T(8,128)(2,1)}, f32[1,1024]{1,0:T(1,128)}, bf16[256,2048]{1,0:T(8,128)(2,1)}, bf16[512,1024]{1,0:T(8,128)(2,1)}, bf16[512,1024]...) custom-call(s32[1]{0:T(128)} %bitcast.1.dp, ...), custom_call_target="tpu_custom_call" | custom-call | flops 8589934592 | bytes 25694208 | tf_op jit(solution)/shard_map/middle/pallas_call | solution.py:341
  194.2 4.3 %all-to-all-start.3 = ((bf16[4,64,2048]{2,1,0:T(8,128)(2,1)}), bf16[4,64,2048]{2,1,0:T(8,128)(2,1)}, u32[]{:S(2)}, u32[]{:S(2)}) async-start(bf16[4,64,2048]{2,1,0:T(8,128)(2,1)} %bitcast.103), calls=%async_computation.3 | async-start | bytes 2097152 | tf_op jit(solution)/shard_map/all_to_all | solution.py:929
  201.2 24.8 %last.1 = (f32[1,768]{1,0:T(1,128)}, f32[4,2048]{1,0:T(4,128)}, bf16[1024,2048]{1,0:T(8,128)(2,1)}, bf16[512,768]{1,0:T(8,128)(2,1)}, bf16[512,768]{1,0:T(8,128)...) custom-call(s32[1]{0:T(128)} %bitcast.1.dp, ...), custom_call_target="tpu_custom_call" | custom-call | flops 13421772800 | bytes 35208192 | tf_op jit(solution)/shard_map/last/pallas_call | solution.py:341
  235.1 10.0 %outward.1 = (bf16[320,2048]{1,0:T(8,128)(2,1)}, bf16[320,2048]{1,0:T(8,128)(2,1)}, bf16[160,2048]{1,0:T(8,128)(2,1)}, bf16[160,2048]{1,0:T(8,128)(2,1)}, bf16[320,2048]{1,0:T(8,128)(2,1)}) custom-call(s32[1]{0:T(128)} %bitcast.1.dp, bf16[1024,1024]{1,0:T(8,128)(2,1)} %get-tuple-element.164.active.refs_0_, ...), custom_call_target="tpu_custom_call" | custom-call | flops 4294967296 | bytes 12582912 | tf_op jit(solution)/shard_map/outward/pallas_call | solution.py:341
  245.0 13.2 %collective-permute-done.14.x_low = bf16[256,1024]{1,0:T(8,128)(2,1)S(1)} collective-permute-done((bf16[256,1024]{1,0:T(8,128)(2,1)}, bf16[256,1024]{1,0:T(8,128)(2,1)S(1)}, u32[]{:S(2)}, u32[]{:S(2)}) %collective-permute-start.14) | collective-permute-done | bytes 524320 | tf_op jit(solution)/shard_map/ppermute | solution.py:752
  259.6 3.5 reduce_last.3
  263.2 4.7 %all-to-all-start.4 = ((bf16[8,64,1024]{2,1,0:T(8,128)(2,1)}), bf16[8,64,1024]{2,1,0:T(8,128)(2,1)S(1)}, u32[]{:S(2)}, u32[]{:S(2)}) async-start(bf16[8,64,1024]{2,1,0:T(8,128)(2,1)} %bitcast.88), calls=%async_computation.5 | async-start | bytes 2097152 | tf_op jit(solution)/shard_map/all_to_all | solution.py:979
  274.5 8.1 %collective-permute-done.18.x_low = bf16[256,768]{1,0:T(8,128)(2,1)S(1)} collective-permute-done((bf16[256,768]{1,0:T(8,128)(2,1)}, bf16[256,768]{1,0:T(8,128)(2,1)S(1)}, u32[]{:S(2)}, u32[]{:S(2)}) %collective-permute-start.18) | collective-permute-done | bytes 393248 | tf_op jit(solution)/shard_map/ppermute | solution.py:752
  287.3 21.4 %all-to-all-done.4.source = bf16[8,64,1024]{2,1,0:T(8,128)(2,1)S(1)} async-done(((bf16[8,64,1024]{2,1,0:T(8,128)(2,1)}), bf16[8,64,1024]{2,1,0:T(8,128)(2,1)S(1)}, u32[]{:S(2)}, u32[]{:S(2)}) %all-to-all-start.4) | async-done | bytes 1048608 | tf_op jit(solution)/shard_map/all_to_all | solution.py:979
  308.7 3.5 all-to-all-start.5
  318.6 14.6 %all-to-all-done.5.source = bf16[8,64,768]{2,1,0:T(8,128)(2,1)S(1)} async-done(((bf16[8,64,768]{2,1,0:T(8,128)(2,1)}), bf16[8,64,768]{2,1,0:T(8,128)(2,1)S(1)}, u32[]{:S(2)}, u32[]{:S(2)}) %all-to-all-start.5) | async-done | bytes 786464 | tf_op jit(solution)/shard_map/all_to_all | solution.py:982
  339.3 4.3 %reduce_both.1 = (f32[256,2048]{1,0:T(8,128)}, f32[64,2048]{1,0:T(8,128)}) custom-call(bf16[320,2048]{1,0:T(8,128)(2,1)} %get-tuple-element.189.own, bf16[320,2048]{1,0:T(8,128)(2,1)} %collective-permute-done.20.got_x, bf16[320,2048]{1,0:T(8,128)(2,1)} %collective-permute-done.21.got_y, bf16[160,2048]{1,0:T(8,128)(2,1)} %copy-done.15, ...), custom_call_target="tpu_custom_call" | custom-call | bytes 5242880 | tf_op jit(solution)/shard_map/reduce_both/pallas_call | solution.py:760
  (227 shorter events, 90.6 us)
Async XLA Ops:
  7.2 114.4 %all-gather.6.cloned.1.call-start = ((), (), s32[]{:S(2)}) async-start(), calls=%async_computation.12 | async-start | bytes 4718592 | tf_op jit(solution)/shard_map/all_gather | solution.py:853
  9.4 31.8 %collective-permute-start.2 = (bf16[320,2048]{1,0:T(8,128)(2,1)S(1)}, bf16[320,2048]{1,0:T(8,128)(2,1)S(1)}, u32[]{:S(2)}, u32[]{:S(2)}) collective-permute-start(bf16[320,2048]{1,0:T(8,128)(2,1)S(1)} %constant_dynamic-update-slice_fusion.own.d0.refs_2_), channel_id=1, source_target_pairs={{0,8},{8,0},{16,24},{24,16},{1,9},{9,1},{17,25},{25,17},{2,10},{10... | collective-permute-start | bytes 3932168 | tf_op jit(solution)/shard_map/ppermute | solution.py:752
  12.5 33.7 %collective-permute-start = (bf16[320,2048]{1,0:T(8,128)(2,1)S(1)}, bf16[320,2048]{1,0:T(8,128)(2,1)}, u32[]{:S(2)}, u32[]{:S(2)}) collective-permute-start(bf16[320,2048]{1,0:T(8,128)(2,1)S(1)} %constant_dynamic-update-slice_fusion.own.d0.refs_2_), channel_id=1, source_target_pairs={{0,16},{8,24},{16,0},{24,8},{1,17},{9,25},{17,1},{25,9},{2,18},{10... | collective-permute-start | bytes 3932168 | tf_op jit(solution)/shard_map/ppermute | solution.py:756
  15.5 53.7 %all-to-all-start = ((bf16[8,64,896]{2,1,0:T(8,128)(2,1)}), bf16[8,64,896]{2,1,0:T(8,128)(2,1)S(1)}, u32[]{:S(2)}, u32[]{:S(2)}) async-start(bf16[8,64,896]{2,1,0:T(8,128)(2,1)} %qkv_blocks.1), calls=%async_computation | async-start | bytes 1835008 | tf_op jit(solution)/shard_map/all_to_all | solution.py:872
  42.2 27.0 %collective-permute-start.3 = (bf16[192,2048]{1,0:T(8,128)(2,1)}, bf16[192,2048]{1,0:T(8,128)(2,1)}, u32[]{:S(2)}, u32[]{:S(2)}) collective-permute-start(bf16[192,2048]{1,0:T(8,128)(2,1)} %slice.131), channel_id=1, source_target_pairs={{0,16},{8,24},{16,0},{24,8},{1,17},{9,25},{17,1},{25,9},{2,18},{10... | collective-permute-start | bytes 2359304 | tf_op jit(solution)/shard_map/ppermute | solution.py:756
  70.0 41.2 %all-to-all-start.1 = ((bf16[8,64,1024]{2,1,0:T(8,128)(2,1)}), bf16[8,64,1024]{2,1,0:T(8,128)(2,1)S(1)}, u32[]{:S(2)}, u32[]{:S(2)}) async-start(bf16[8,64,1024]{2,1,0:T(8,128)(2,1)} %up_blocks.1), calls=%async_computation.1 | async-start | bytes 2097152 | tf_op jit(solution)/shard_map/all_to_all | solution.py:883
  73.6 104.5 %all-gather.4.cloned.1.call-start = ((), (), s32[]{:S(2)}) async-start(), calls=%async_computation.9 | async-start | bytes 4718592 | tf_op jit(solution)/shard_map/all_gather | solution.py:895
  112.6 25.1 %collective-permute-start.9 = (bf16[512,1024]{1,0:T(8,128)(2,1)S(1)}, bf16[512,1024]{1,0:T(8,128)(2,1)}, u32[]{:S(2)}, u32[]{:S(2)}) collective-permute-start(bf16[512,1024]{1,0:T(8,128)(2,1)S(1)} %bitcast.97), channel_id=1, source_target_pairs={{0,16},{8,24},{16,0},{24,8},{1,17},{9,25},{17,1},{25,9},{2,18},{10... | collective-permute-start | bytes 3145736 | tf_op jit(solution)/shard_map/ppermute | solution.py:756
  113.7 24.0 %collective-permute-start.8 = (bf16[512,1024]{1,0:T(8,128)(2,1)S(1)}, bf16[512,1024]{1,0:T(8,128)(2,1)}, u32[]{:S(2)}, u32[]{:S(2)}) collective-permute-start(bf16[512,1024]{1,0:T(8,128)(2,1)S(1)} %bitcast.98), channel_id=1, source_target_pairs={{0,8},{8,0},{16,24},{24,16},{1,9},{9,1},{17,25},{25,17},{2,10},{10... | collective-permute-start | bytes 3145736 | tf_op jit(solution)/shard_map/ppermute | solution.py:752
  115.0 51.4 %all-to-all-start.2 = ((bf16[4,64,2048]{2,1,0:T(8,128)(2,1)}), bf16[4,64,2048]{2,1,0:T(8,128)(2,1)S(1)}, u32[]{:S(2)}, u32[]{:S(2)}) async-start(bf16[4,64,2048]{2,1,0:T(8,128)(2,1)} %out_rows.1), calls=%async_computation.2 | async-start | bytes 2097152 | tf_op jit(solution)/shard_map/all_to_all | solution.py:897
  118.5 190.2 %reduce-scatter.3.cloned.1.call-start = ((), (), s32[]{:S(2)}) async-start(), calls=%async_computation.10 | async-start | bytes 4718592 | tf_op jit(solution)/shard_map/reduce_scatter | solution.py:925
  194.2 31.9 %all-to-all-start.3 = ((bf16[4,64,2048]{2,1,0:T(8,128)(2,1)}), bf16[4,64,2048]{2,1,0:T(8,128)(2,1)}, u32[]{:S(2)}, u32[]{:S(2)}) async-start(bf16[4,64,2048]{2,1,0:T(8,128)(2,1)} %bitcast.103), calls=%async_computation.3 | async-start | bytes 2097152 | tf_op jit(solution)/shard_map/all_to_all | solution.py:929
  198.5 148.3 %reduce-scatter.5.cloned.1.call-start = ((), (), s32[]{:S(2)}) async-start(), calls=%async_computation.11 | async-start | bytes 4718592 | tf_op jit(solution)/shard_map/reduce_scatter | solution.py:960
  199.0 27.1 %collective-permute-start.12 = (bf16[512,1024]{1,0:T(8,128)(2,1)}, bf16[512,1024]{1,0:T(8,128)(2,1)S(1)}, u32[]{:S(2)}, u32[]{:S(2)}) collective-permute-start(bf16[512,1024]{1,0:T(8,128)(2,1)} %get-tuple-element.147), channel_id=1, source_target_pairs={{0,8},{8,0},{16,24},{24,16},{1,9},{9,1},{17,25},{25,17},{2,10},{10... | collective-permute-start | bytes 3145736 | tf_op jit(solution)/shard_map/ppermute | solution.py:752
  200.1 26.0 %collective-permute-start.13 = (bf16[512,1024]{1,0:T(8,128)(2,1)}, bf16[512,1024]{1,0:T(8,128)(2,1)S(1)}, u32[]{:S(2)}, u32[]{:S(2)}) collective-permute-start(bf16[512,1024]{1,0:T(8,128)(2,1)} %get-tuple-element.148), channel_id=1, source_target_pairs={{0,16},{8,24},{16,0},{24,8},{1,17},{9,25},{17,1},{25,9},{2,18},{10... | collective-permute-start | bytes 3145736 | tf_op jit(solution)/shard_map/ppermute | solution.py:756
  227.4 31.4 %collective-permute-start.16 = (bf16[512,768]{1,0:T(8,128)(2,1)}, bf16[512,768]{1,0:T(8,128)(2,1)S(1)}, u32[]{:S(2)}, u32[]{:S(2)}) collective-permute-start(bf16[512,768]{1,0:T(8,128)(2,1)} %get-tuple-element.162), channel_id=1, source_target_pairs={{0,8},{8,0},{16,24},{24,16},{1,9},{9,1},{17,25},{25,17},{2,10},{10... | collective-permute-start | bytes 2359304 | tf_op jit(solution)/shard_map/ppermute | solution.py:752
  228.4 30.5 %collective-permute-start.17 = (bf16[512,768]{1,0:T(8,128)(2,1)}, bf16[512,768]{1,0:T(8,128)(2,1)S(1)}, u32[]{:S(2)}, u32[]{:S(2)}) collective-permute-start(bf16[512,768]{1,0:T(8,128)(2,1)} %get-tuple-element.163), channel_id=1, source_target_pairs={{0,16},{8,24},{16,0},{24,8},{1,17},{9,25},{17,1},{25,9},{2,18},{10... | collective-permute-start | bytes 2359304 | tf_op jit(solution)/shard_map/ppermute | solution.py:756
  232.3 25.9 %collective-permute-start.14 = (bf16[256,1024]{1,0:T(8,128)(2,1)}, bf16[256,1024]{1,0:T(8,128)(2,1)S(1)}, u32[]{:S(2)}, u32[]{:S(2)}) collective-permute-start(bf16[256,1024]{1,0:T(8,128)(2,1)} %get-tuple-element.160), channel_id=1, source_target_pairs={{0,8},{8,0},{16,24},{24,16},{1,9},{9,1},{17,25},{25,17},{2,10},{10... | collective-permute-start | bytes 1572872 | tf_op jit(solution)/shard_map/ppermute | solution.py:752
  233.3 25.6 %collective-permute-start.15 = (bf16[256,1024]{1,0:T(8,128)(2,1)}, bf16[256,1024]{1,0:T(8,128)(2,1)S(1)}, u32[]{:S(2)}, u32[]{:S(2)}) collective-permute-start(bf16[256,1024]{1,0:T(8,128)(2,1)} %get-tuple-element.161), channel_id=1, source_target_pairs={{0,16},{8,24},{16,0},{24,8},{1,17},{9,25},{17,1},{25,9},{2,18},{10... | collective-permute-start | bytes 1572872 | tf_op jit(solution)/shard_map/ppermute | solution.py:756
  263.2 45.5 %all-to-all-start.4 = ((bf16[8,64,1024]{2,1,0:T(8,128)(2,1)}), bf16[8,64,1024]{2,1,0:T(8,128)(2,1)S(1)}, u32[]{:S(2)}, u32[]{:S(2)}) async-start(bf16[8,64,1024]{2,1,0:T(8,128)(2,1)} %bitcast.88), calls=%async_computation.5 | async-start | bytes 2097152 | tf_op jit(solution)/shard_map/all_to_all | solution.py:979
  272.5 39.9 %collective-permute-start.20 = (bf16[320,2048]{1,0:T(8,128)(2,1)}, bf16[320,2048]{1,0:T(8,128)(2,1)}, u32[]{:S(2)}, u32[]{:S(2)}) collective-permute-start(bf16[320,2048]{1,0:T(8,128)(2,1)} %get-tuple-element.190), channel_id=1, source_target_pairs={{0,8},{8,0},{16,24},{24,16},{1,9},{9,1},{17,25},{25,17},{2,10},{10... | collective-permute-start | bytes 3932168 | tf_op jit(solution)/shard_map/ppermute | solution.py:752
  273.6 38.9 %collective-permute-start.21 = (bf16[320,2048]{1,0:T(8,128)(2,1)}, bf16[320,2048]{1,0:T(8,128)(2,1)}, u32[]{:S(2)}, u32[]{:S(2)}) collective-permute-start(bf16[320,2048]{1,0:T(8,128)(2,1)} %get-tuple-element.191), channel_id=1, source_target_pairs={{0,16},{8,24},{16,0},{24,8},{1,17},{9,25},{17,1},{25,9},{2,18},{10... | collective-permute-start | bytes 3932168 | tf_op jit(solution)/shard_map/ppermute | solution.py:756
  308.7 24.5 %all-to-all-start.5 = ((bf16[8,64,768]{2,1,0:T(8,128)(2,1)}), bf16[8,64,768]{2,1,0:T(8,128)(2,1)S(1)}, u32[]{:S(2)}, u32[]{:S(2)}) async-start(bf16[8,64,768]{2,1,0:T(8,128)(2,1)} %bitcast.91), calls=%async_computation.7 | async-start | bytes 1572864 | tf_op jit(solution)/shard_map/all_to_all | solution.py:982
  315.8 22.7 %collective-permute-start.22 = (bf16[160,2048]{1,0:T(8,128)(2,1)}, bf16[160,2048]{1,0:T(8,128)(2,1)S(1)}, u32[]{:S(2)}, u32[]{:S(2)}) collective-permute-start(bf16[160,2048]{1,0:T(8,128)(2,1)} %get-tuple-element.196), channel_id=1, source_target_pairs={{0,8},{8,0},{16,24},{24,16},{1,9},{9,1},{17,25},{25,17},{2,10},{10... | collective-permute-start | bytes 1966088 | tf_op jit(solution)/shard_map/ppermute | solution.py:752
  (52 other events, 405.5 us)
Sparse Core Ops, SparseCore 0:
  9.6 69.3 all-gather.5
  111.4 56.5 all-gather.3
  178.2 61.4 reduce-scatter.2
  241.8 63.8 reduce-scatter.4

commit v5 on v4

--- a/solution.py
+++ b/solution.py
@@ -761,7 +761,7 @@
         body,
         name=name,
         out_shape=outs,
-        compiler_params=pltpu.CompilerParams(vmem_limit_bytes=56 * 2**20),
+        compiler_params=pltpu.CompilerParams(vmem_limit_bytes=24 * 2**20),
         cost_estimate=pl.CostEstimate(flops=0, bytes_accessed=sources[0].size * 8, transcendentals=0),
     )(*sources)
 
@@ -779,7 +779,7 @@
 def pass_on(terms, got):
     out = jax.ShapeDtypeStruct(terms[2].shape, BF16)
     to_x, to_y = small_call(pass_on_body, "pass_on", (out, out), terms[2], terms[3], *got)
-    return over_x(to_x), over_y(to_y)
+    return (over_x(to_x), over_y(to_y)), to_x
 
 
 def reduce_last_body(own, got_x, got_y, x_low, y_top, out):
@@ -955,7 +955,8 @@
     u_terms, up_got, qkv_terms, down_left, norm_sums, attn_sent = stage(
         (u_terms, up_got, qkv_terms, active, norm_sums, attn_sent), ()
     )
-    up_then = pass_on(up_terms, up_got)
+    up_then, passed = pass_on(up_terms, up_got)
+    qkv_terms = stage(qkv_terms, (passed,))
     qkv_got = send_both(qkv_terms)
     u_sum = lax.psum_scatter(u_terms, "sp", scatter_dimension=0, tiled=True)
     sum_qkv = lax.dynamic_update_slice(
@@ -970,19 +971,19 @@
         ],
         axis=1,
     )
-    down_terms = outward(dp, down_left, g_all, attn_sent)
-
-    up_then, qkv_got, down_terms, totals = stage((up_then, qkv_got, down_terms, totals), ())
-    qkv_then = pass_on(qkv_terms, qkv_got)
+    up_sum = reduce_last(up_terms, up_got, up_then)
+    down_terms = outward(dp, tie(down_left, up_sum), g_all, attn_sent)
+
+    qkv_got, down_terms, totals = stage((qkv_got, down_terms, totals), (up_sum,))
+    qkv_then, _ = pass_on(qkv_terms, qkv_got)
     down_got = send_both(down_terms)
-    up_sum = reduce_last(up_terms, up_got, up_then)
     up_back = lax.all_to_all(up_sum.reshape(HEADS, rows, 1024), "sp", 0, 0, tiled=True)
     qkv_sum = reduce_last(qkv_terms, qkv_got, qkv_then)
     qkv_sum, out_sum = stage((qkv_sum, out_sum), (up_back,))
     qkv_back = lax.all_to_all(qkv_sum.reshape(HEADS, rows, 768), "sp", 0, 0, tiled=True)
 
     down_got = stage(down_got, (qkv_sum,))
-    down_then = pass_on(down_terms, down_got)
+    down_then, _ = pass_on(down_terms, down_got)
     grad_up = repack(
         up_rows_body, "up_rows", jax.ShapeDtypeStruct((rows, HEADS * 1024), F32), up_back
     )

time: 362 us -> 356 us (0.983)
  Pallas kernels: 122 us -> 110 us
  local copies, waits for them, and re-layouts: 23 us -> 28.3 us
    all_to_all x1, waiting for transfers between devices: 21.4 us -> 8.08 us  [line_shards(): lax.all_to_all(up_sum.reshape(HEADS, rows, 1024), 'sp', 0, 0, tiled=True)]
    pallas_call x6, Pallas kernels: 19.8 us -> 6.48 us  [small_call(): pl.pallas_call(body, name=name, out_shape=outs, compiler_params=pltpu.Com...]
    ppermute x12, waiting for transfers between devices: 33.1 us -> 44.8 us  [over_y(): return lax.ppermute(block, 'dp', swap(4, 2))]
    all_to_all x1, waiting for transfers between devices: 14.6 us -> 8.18 us  [line_shards(): lax.all_to_all(qkv_sum.reshape(HEADS, rows, 768), 'sp', 0, 0, tiled=True)]
    ppermute x12, waiting for transfers between devices: 46.7 us -> 52.2 us  [over_x(): return lax.ppermute(block, 'dp', swap(4, 1))]
    unnamed x80 -> x102, local copies, waits for them, and re-layouts: 8.97 us -> 12.7 us
  transfers between devices with their start and end apart: 35 -> 35, of which waited for: 13 -> 19; matrix products, arithmetic and copies ran while one was open for 6% -> 8% of each run, Pallas kernels for 34% -> 31%
where the time goes in v5:
time: 356 us; the launch traced here: 351 us
  waiting for transfers between devices  131 us (37%)
  Pallas kernels  110 us (31%)
  starting transfers between devices  54 us (15%)
  local copies, waits for them, and re-layouts  28.3 us (8%)
  between operations  14.7 us (4%)
  other arithmetic  13.1 us (4%)
    pallas_call x9, Pallas kernels, run(): pl.pallas_call(body, name=name, grid_spec=pltpu.PrefetchScalarGridSpec(nu...  97.5 us
    ppermute x12, waiting for transfers between devices, over_x(): return lax.ppermute(block, 'dp', swap(4, 1))  52.2 us
    ppermute x12, waiting for transfers between devices, over_y(): return lax.ppermute(block, 'dp', swap(4, 2))  44.8 us
    all_to_all x1, waiting for transfers between devices, line_shards(): lax.all_to_all(qkv_blocks, 'sp', 0, 0, tiled=True)  16.7 us
    ppermute x12, starting transfers between devices, over_x(): return lax.ppermute(block, 'dp', swap(4, 1))  13.8 us
    unnamed x102, local copies, waits for them, and re-layouts  12.7 us
    ppermute x12, starting transfers between devices, over_y(): return lax.ppermute(block, 'dp', swap(4, 2))  11.7 us
    all_to_all x1, waiting for transfers between devices, line_shards(): lax.all_to_all(qkv_sum.reshape(HEADS, rows, 768), 'sp', 0, 0, tiled=True)  8.18 us
  transfers between devices with their start and end apart: 35, of which 19 were waited for; matrix products, arithmetic and copies ran while one was open for 8% of the time, Pallas kernels for 31%

profile of v5, /device:TPU:0, one launch (start us, length us, event | category | flops | bytes accessed | tf_op | source)
XLA Modules:
  0.0 351.2 jit_solution(6517225796007721496)
XLA Ops:
  15.5 4.9 %all-to-all-start = ((bf16[8,64,896]{2,1,0:T(8,128)(2,1)}), bf16[8,64,896]{2,1,0:T(8,128)(2,1)S(1)}, u32[]{:S(2)}, u32[]{:S(2)}) async-start(bf16[8,64,896]{2,1,0:T(8,128)(2,1)} %qkv_blocks.1), calls=%async_computation | async-start | bytes 1835008 | tf_op jit(solution)/shard_map/all_to_all | solution.py:872
  20.6 20.7 %collective-permute-done.2.along_x.dx.refs_3_ = bf16[320,2048]{1,0:T(8,128)(2,1)S(1)} collective-permute-done((bf16[320,2048]{1,0:T(8,128)(2,1)S(1)}, bf16[320,2048]{1,0:T(8,128)(2,1)S(1)}, u32[]{:S(2)}, u32[]{:S(2)}) %collective-permute-start.2) | collective-permute-done | bytes 1310752 | tf_op jit(solution)/shard_map/ppermute | solution.py:752
  52.5 16.7 %all-to-all-done = bf16[8,64,896]{2,1,0:T(8,128)(2,1)S(1)} async-done(((bf16[8,64,896]{2,1,0:T(8,128)(2,1)}), bf16[8,64,896]{2,1,0:T(8,128)(2,1)S(1)}, u32[]{:S(2)}, u32[]{:S(2)}) %all-to-all-start) | async-done | bytes 917536 | tf_op jit(solution)/shard_map/all_to_all | solution.py:872
  70.0 3.6 %all-to-all-start.1 = ((bf16[8,64,1024]{2,1,0:T(8,128)(2,1)}), bf16[8,64,1024]{2,1,0:T(8,128)(2,1)S(1)}, u32[]{:S(2)}, u32[]{:S(2)}) async-start(bf16[8,64,1024]{2,1,0:T(8,128)(2,1)} %up_blocks.1), calls=%async_computation.1 | async-start | bytes 2097152 | tf_op jit(solution)/shard_map/all_to_all | solution.py:883
  77.2 19.1 %collective-permute-done.5.wy.refs_18_ = bf16[512,896]{1,0:T(8,128)(2,1)S(1)} collective-permute-done((bf16[512,896]{1,0:T(8,128)(2,1)S(1)}, bf16[512,896]{1,0:T(8,128)(2,1)S(1)}, u32[]{:S(2)}, u32[]{:S(2)}) %collective-permute-start.5) | collective-permute-done | bytes 917536 | tf_op jit(solution)/shard_map/ppermute | solution.py:756
  99.6 10.8 %collective-permute-done.7.w2.refs_20_ = bf16[256,896]{1,0:T(8,128)(2,1)S(1)} collective-permute-done((bf16[256,896]{1,0:T(8,128)(2,1)S(1)}, bf16[256,896]{1,0:T(8,128)(2,1)S(1)}, u32[]{:S(2)}, u32[]{:S(2)}) %collective-permute-start.7) | collective-permute-done | bytes 458784 | tf_op jit(solution)/shard_map/ppermute | solution.py:756
  115.8 3.5 %all-to-all-start.2 = ((bf16[4,64,2048]{2,1,0:T(8,128)(2,1)}), bf16[4,64,2048]{2,1,0:T(8,128)(2,1)S(1)}, u32[]{:S(2)}, u32[]{:S(2)}) async-start(bf16[4,64,2048]{2,1,0:T(8,128)(2,1)} %out_rows.1), calls=%async_computation.2 | async-start | bytes 2097152 | tf_op jit(solution)/shard_map/all_to_all | solution.py:897
  122.5 7.8 %norms.1 = (bf16[1024,2048]{1,0:T(8,128)(2,1)}, bf16[1024,2048]{1,0:T(8,128)(2,1)}) custom-call(s32[1]{0:T(128)} %bitcast.1.dp, bf16[1024,2048]{1,0:T(8,128)(2,1)} %bitcast.89, f32[4,2048]{1,0:T(4,128)} %slice.115.vec.refs_10_), custom_call_target="tpu_custom_call" | custom-call | bytes 12615680 | tf_op jit(solution)/shard_map/norms/pallas_call | solution.py:341
  130.2 8.2 %qkv.1 = (bf16[1024,256]{1,0:T(8,128)(2,1)}, bf16[1024,256]{1,0:T(8,128)(2,1)}, bf16[1024,256]{1,0:T(8,128)(2,1)}) custom-call(s32[1]{0:T(128)} %bitcast.1.dp, bf16[1024,2048]{1,0:T(8,128)(2,1)} %get-tuple-element.121.first.refs_13_, bf16[512,896]{1,0:T(8,128)(2,1)} %bitcast.94, bf16[512,896]{1,0:T(8,128)(2,1)} %collective-permute-done.4.wx.refs_17_, ...), custom_call_target="tpu_custom_call" | custom-call | flops 3221225472 | bytes 11013120 | tf_op jit(solution)/shard_map/qkv/pallas_call | solution.py:341
  144.2 5.7 %attend_forward.1 = (f32[1024,256]{1,0:T(8,128)}, bf16[1024,256]{1,0:T(8,128)(2,1)}, f32[1024,1]{1,0:T(8,128)}) custom-call(s32[1]{0:T(128)} %bitcast.1.dp, bf16[1024,256]{1,0:T(8,128)(2,1)} %get-tuple-element.146.q.refs_0_, bf16[1024,256]{1,0:T(8,128)(2,1)} %get-tuple-element.130.k.refs_1_, bf16[1024,256]{1,0:T(8,128)(2,1)} %get-tuple-element.131.v.refs_2_, ...), custom_call_target="tpu_custom_call" | custom-call | flops 805306368 | bytes 3158016 | tf_op jit(solution)/shard_map/attend_forward/pallas_call | solution.py:341
  149.9 5.1 %collective-permute-done.10.u1.refs_24_ = bf16[256,1024]{1,0:T(8,128)(2,1)S(1)} collective-permute-done((bf16[256,1024]{1,0:T(8,128)(2,1)S(1)}, bf16[256,1024]{1,0:T(8,128)(2,1)S(1)}, u32[]{:S(2)}, u32[]{:S(2)}) %collective-permute-start.10) | collective-permute-done | bytes 524320 | tf_op jit(solution)/shard_map/ppermute | solution.py:752
  157.3 10.8 %mlp_forward.1 = (bf16[1024,1024]{1,0:T(8,128)(2,1)}, f32[1024,1024]{1,0:T(8,128)}) custom-call(s32[1]{0:T(128)} %bitcast.1.dp, bf16[1024,2048]{1,0:T(8,128)(2,1)} %get-tuple-element.127.second.refs_7_, bf16[512,1024]{1,0:T(8,128)(2,1)} %bitcast.98, bf16[512,1024]{1,0:T(8,128)(2,1)} %collective-permute-done.8.ux.refs_22_, ...), custom_call_target="tpu_custom_call" | custom-call | flops 4294967296 | bytes 14684160 | tf_op jit(solution)/shard_map/mlp_forward/pallas_call | solution.py:341
  169.1 10.7 %output.1 = bf16[1024,2048]{1,0:T(8,128)(2,1)} custom-call(s32[1]{0:T(128)} %bitcast.1.dp, bf16[1024,256]{1,0:T(8,128)(2,1)} %get-tuple-element.140.ctx.refs_8_, bf16[1024,1024]{1,0:T(8,128)(2,1)} %get-tuple-element.175.active.refs_0_, bf16[256,2048]{1,0:T(8,128)(2,1)} %bitcast.100, bf16[320,2048]{1,0:T(8,128)(2,1)} %copy-done.18, ...), custom_call_target="tpu_custom_call" | custom-call | flops 5368709120 | bytes 13107200 | tf_op jit(solution)/shard_map/output/pallas_call | solution.py:341
  179.9 16.1 %middle.1 = (bf16[1024,1024]{1,0:T(8,128)(2,1)}, f32[1,1024]{1,0:T(1,128)}, bf16[256,2048]{1,0:T(8,128)(2,1)}, bf16[512,1024]{1,0:T(8,128)(2,1)}, bf16[512,1024]...) custom-call(s32[1]{0:T(128)} %bitcast.1.dp, ...), custom_call_target="tpu_custom_call" | custom-call | flops 8589934592 | bytes 25694208 | tf_op jit(solution)/shard_map/middle/pallas_call | solution.py:341
  201.0 24.8 %last.1 = (f32[1,768]{1,0:T(1,128)}, f32[4,2048]{1,0:T(4,128)}, bf16[1024,2048]{1,0:T(8,128)(2,1)}, bf16[512,768]{1,0:T(8,128)(2,1)}, bf16[512,768]{1,0:T(8,128)...) custom-call(s32[1]{0:T(128)} %bitcast.1.dp, ...), custom_call_target="tpu_custom_call" | custom-call | flops 13421772800 | bytes 35208192 | tf_op jit(solution)/shard_map/last/pallas_call | solution.py:341
  231.4 10.9 %collective-permute-done.17.y_top = bf16[256,1024]{1,0:T(8,128)(2,1)S(1)} collective-permute-done((bf16[256,1024]{1,0:T(8,128)(2,1)S(1)}, bf16[256,1024]{1,0:T(8,128)(2,1)S(1)}, u32[]{:S(2)}, u32[]{:S(2)}) %collective-permute-start.17) | collective-permute-done | bytes 524320 | tf_op jit(solution)/shard_map/ppermute | solution.py:756
  244.6 4.9 %all-to-all-start.4 = ((bf16[8,64,1024]{2,1,0:T(8,128)(2,1)}), bf16[8,64,1024]{2,1,0:T(8,128)(2,1)}, u32[]{:S(2)}, u32[]{:S(2)}) async-start(bf16[8,64,1024]{2,1,0:T(8,128)(2,1)} %bitcast.32), calls=%async_computation.5 | async-start | bytes 2097152 | tf_op jit(solution)/shard_map/all_to_all | solution.py:980
  253.0 10.1 %outward.1 = (bf16[320,2048]{1,0:T(8,128)(2,1)}, bf16[320,2048]{1,0:T(8,128)(2,1)}, bf16[160,2048]{1,0:T(8,128)(2,1)}, bf16[160,2048]{1,0:T(8,128)(2,1)}, bf16[320,2048]{1,0:T(8,128)(2,1)}) custom-call(s32[1]{0:T(128)} %bitcast.1.dp, bf16[1024,1024]{1,0:T(8,128)(2,1)} %get-tuple-element.175.active.refs_0_, ...), custom_call_target="tpu_custom_call" | custom-call | flops 4294967296 | bytes 12582912 | tf_op jit(solution)/shard_map/outward/pallas_call | solution.py:341
  263.1 6.3 %collective-permute-done.14.got_x = bf16[512,768]{1,0:T(8,128)(2,1)S(1)} collective-permute-done((bf16[512,768]{1,0:T(8,128)(2,1)S(1)}, bf16[512,768]{1,0:T(8,128)(2,1)S(1)}, u32[]{:S(2)}, u32[]{:S(2)}) %collective-permute-start.14) | collective-permute-done | bytes 786464 | tf_op jit(solution)/shard_map/ppermute | solution.py:752
  275.0 8.0 %collective-permute-done.18.x_low = bf16[256,768]{1,0:T(8,128)(2,1)S(1)} collective-permute-done((bf16[256,768]{1,0:T(8,128)(2,1)S(1)}, bf16[256,768]{1,0:T(8,128)(2,1)S(1)}, u32[]{:S(2)}, u32[]{:S(2)}) %collective-permute-start.18) | collective-permute-done | bytes 393248 | tf_op jit(solution)/shard_map/ppermute | solution.py:752
  285.9 8.1 %all-to-all-done.4.source = bf16[8,64,1024]{2,1,0:T(8,128)(2,1)} async-done(((bf16[8,64,1024]{2,1,0:T(8,128)(2,1)}), bf16[8,64,1024]{2,1,0:T(8,128)(2,1)}, u32[]{:S(2)}, u32[]{:S(2)}) %all-to-all-start.4) | async-done | bytes 1048608 | tf_op jit(solution)/shard_map/all_to_all | solution.py:980
  298.8 10.6 %collective-permute-done.20.got_x = bf16[320,2048]{1,0:T(8,128)(2,1)S(1)} collective-permute-done((bf16[320,2048]{1,0:T(8,128)(2,1)}, bf16[320,2048]{1,0:T(8,128)(2,1)S(1)}, u32[]{:S(2)}, u32[]{:S(2)}) %collective-permute-start.20) | collective-permute-done | bytes 1310752 | tf_op jit(solution)/shard_map/ppermute | solution.py:752
  316.2 8.2 %all-to-all-done.5.source = bf16[8,64,768]{2,1,0:T(8,128)(2,1)S(1)} async-done(((bf16[8,64,768]{2,1,0:T(8,128)(2,1)}), bf16[8,64,768]{2,1,0:T(8,128)(2,1)S(1)}, u32[]{:S(2)}, u32[]{:S(2)}) %all-to-all-start.5) | async-done | bytes 786464 | tf_op jit(solution)/shard_map/all_to_all | solution.py:983
  326.0 3.8 %all-to-all-start.6 = ((f32[32,1,768]{2,1,0:T(1,128)}), f32[32,1,768]{2,1,0:T(1,128)}, u32[]{:S(2)}, u32[]{:S(2)}) async-start(f32[32,1,768]{2,1,0:T(1,128)} %copy.44), calls=%async_computation.8 | async-start | bytes 196608 | tf_op jit(solution)/shard_map/all_to_all | solution.py:990
  (248 shorter events, 97.1 us)
Async XLA Ops:
  7.2 115.3 %all-gather.6.cloned.1.call-start = ((), (), s32[]{:S(2)}) async-start(), calls=%async_computation.12 | async-start | bytes 4718592 | tf_op jit(solution)/shard_map/all_gather | solution.py:853
  9.4 31.8 %collective-permute-start.2 = (bf16[320,2048]{1,0:T(8,128)(2,1)S(1)}, bf16[320,2048]{1,0:T(8,128)(2,1)S(1)}, u32[]{:S(2)}, u32[]{:S(2)}) collective-permute-start(bf16[320,2048]{1,0:T(8,128)(2,1)S(1)} %constant_dynamic-update-slice_fusion.own.d0.refs_2_), channel_id=1, source_target_pairs={{0,8},{8,0},{16,24},{24,16},{1,9},{9,1},{17,25},{25,17},{2,10},{10... | collective-permute-start | bytes 3932168 | tf_op jit(solution)/shard_map/ppermute | solution.py:752
  12.5 33.8 %collective-permute-start = (bf16[320,2048]{1,0:T(8,128)(2,1)S(1)}, bf16[320,2048]{1,0:T(8,128)(2,1)}, u32[]{:S(2)}, u32[]{:S(2)}) collective-permute-start(bf16[320,2048]{1,0:T(8,128)(2,1)S(1)} %constant_dynamic-update-slice_fusion.own.d0.refs_2_), channel_id=1, source_target_pairs={{0,16},{8,24},{16,0},{24,8},{1,17},{9,25},{17,1},{25,9},{2,18},{10... | collective-permute-start | bytes 3932168 | tf_op jit(solution)/shard_map/ppermute | solution.py:756
  15.5 53.7 %all-to-all-start = ((bf16[8,64,896]{2,1,0:T(8,128)(2,1)}), bf16[8,64,896]{2,1,0:T(8,128)(2,1)S(1)}, u32[]{:S(2)}, u32[]{:S(2)}) async-start(bf16[8,64,896]{2,1,0:T(8,128)(2,1)} %qkv_blocks.1), calls=%async_computation | async-start | bytes 1835008 | tf_op jit(solution)/shard_map/all_to_all | solution.py:872
  42.2 27.0 %collective-permute-start.3 = (bf16[192,2048]{1,0:T(8,128)(2,1)}, bf16[192,2048]{1,0:T(8,128)(2,1)}, u32[]{:S(2)}, u32[]{:S(2)}) collective-permute-start(bf16[192,2048]{1,0:T(8,128)(2,1)} %slice.131), channel_id=1, source_target_pairs={{0,16},{8,24},{16,0},{24,8},{1,17},{9,25},{17,1},{25,9},{2,18},{10... | collective-permute-start | bytes 2359304 | tf_op jit(solution)/shard_map/ppermute | solution.py:756
  47.3 21.9 %collective-permute-start.1 = (bf16[128,2048]{1,0:T(8,128)(2,1)S(1)}, bf16[128,2048]{1,0:T(8,128)(2,1)S(1)}, u32[]{:S(2)}, u32[]{:S(2)}) collective-permute-start(bf16[128,2048]{1,0:T(8,128)(2,1)S(1)} %slice.130), channel_id=1, source_target_pairs={{0,8},{8,0},{16,24},{24,16},{1,9},{9,1},{17,25},{25,17},{2,10},{10... | collective-permute-start | bytes 1572872 | tf_op jit(solution)/shard_map/ppermute | solution.py:752
  70.0 40.8 %all-to-all-start.1 = ((bf16[8,64,1024]{2,1,0:T(8,128)(2,1)}), bf16[8,64,1024]{2,1,0:T(8,128)(2,1)S(1)}, u32[]{:S(2)}, u32[]{:S(2)}) async-start(bf16[8,64,1024]{2,1,0:T(8,128)(2,1)} %up_blocks.1), calls=%async_computation.1 | async-start | bytes 2097152 | tf_op jit(solution)/shard_map/all_to_all | solution.py:883
  73.6 106.3 %all-gather.4.cloned.1.call-start = ((), (), s32[]{:S(2)}) async-start(), calls=%async_computation.9 | async-start | bytes 4718592 | tf_op jit(solution)/shard_map/all_gather | solution.py:895
  73.7 22.6 %collective-permute-start.5 = (bf16[512,896]{1,0:T(8,128)(2,1)S(1)}, bf16[512,896]{1,0:T(8,128)(2,1)S(1)}, u32[]{:S(2)}, u32[]{:S(2)}) collective-permute-start(bf16[512,896]{1,0:T(8,128)(2,1)S(1)} %bitcast.91), channel_id=1, source_target_pairs={{0,16},{8,24},{16,0},{24,8},{1,17},{9,25},{17,1},{25,9},{2,18},{10... | collective-permute-start | bytes 2752520 | tf_op jit(solution)/shard_map/ppermute | solution.py:756
  73.7 22.7 %collective-permute-start.4 = (bf16[512,896]{1,0:T(8,128)(2,1)S(1)}, bf16[512,896]{1,0:T(8,128)(2,1)}, u32[]{:S(2)}, u32[]{:S(2)}) collective-permute-start(bf16[512,896]{1,0:T(8,128)(2,1)S(1)} %bitcast.92), channel_id=1, source_target_pairs={{0,8},{8,0},{16,24},{24,16},{1,9},{9,1},{17,25},{25,17},{2,10},{10... | collective-permute-start | bytes 2752520 | tf_op jit(solution)/shard_map/ppermute | solution.py:752
  112.3 26.1 %collective-permute-start.9 = (bf16[512,1024]{1,0:T(8,128)(2,1)S(1)}, bf16[512,1024]{1,0:T(8,128)(2,1)}, u32[]{:S(2)}, u32[]{:S(2)}) collective-permute-start(bf16[512,1024]{1,0:T(8,128)(2,1)S(1)} %bitcast.96), channel_id=1, source_target_pairs={{0,16},{8,24},{16,0},{24,8},{1,17},{9,25},{17,1},{25,9},{2,18},{10... | collective-permute-start | bytes 3145736 | tf_op jit(solution)/shard_map/ppermute | solution.py:756
  113.7 24.7 %collective-permute-start.8 = (bf16[512,1024]{1,0:T(8,128)(2,1)S(1)}, bf16[512,1024]{1,0:T(8,128)(2,1)}, u32[]{:S(2)}, u32[]{:S(2)}) collective-permute-start(bf16[512,1024]{1,0:T(8,128)(2,1)S(1)} %bitcast.97), channel_id=1, source_target_pairs={{0,8},{8,0},{16,24},{24,16},{1,9},{9,1},{17,25},{25,17},{2,10},{10... | collective-permute-start | bytes 3145736 | tf_op jit(solution)/shard_map/ppermute | solution.py:752
  115.8 52.3 %all-to-all-start.2 = ((bf16[4,64,2048]{2,1,0:T(8,128)(2,1)}), bf16[4,64,2048]{2,1,0:T(8,128)(2,1)S(1)}, u32[]{:S(2)}, u32[]{:S(2)}) async-start(bf16[4,64,2048]{2,1,0:T(8,128)(2,1)} %out_rows.1), calls=%async_computation.2 | async-start | bytes 2097152 | tf_op jit(solution)/shard_map/all_to_all | solution.py:897
  119.4 174.6 %reduce-scatter.3.cloned.1.call-start = ((), (), s32[]{:S(2)}) async-start(), calls=%async_computation.10 | async-start | bytes 4718592 | tf_op jit(solution)/shard_map/reduce_scatter | solution.py:925
  196.0 30.1 %all-to-all-start.3 = ((bf16[4,64,2048]{2,1,0:T(8,128)(2,1)}), bf16[4,64,2048]{2,1,0:T(8,128)(2,1)S(1)}, u32[]{:S(2)}, u32[]{:S(2)}) async-start(bf16[4,64,2048]{2,1,0:T(8,128)(2,1)} %bitcast.102), calls=%async_computation.3 | async-start | bytes 2097152 | tf_op jit(solution)/shard_map/all_to_all | solution.py:929
  199.5 141.0 %reduce-scatter.5.cloned.1.call-start = ((), (), s32[]{:S(2)}) async-start(), calls=%async_computation.11 | async-start | bytes 4718592 | tf_op jit(solution)/shard_map/reduce_scatter | solution.py:961
  200.0 25.9 %collective-permute-start.12 = (bf16[512,1024]{1,0:T(8,128)(2,1)}, bf16[512,1024]{1,0:T(8,128)(2,1)S(1)}, u32[]{:S(2)}, u32[]{:S(2)}) collective-permute-start(bf16[512,1024]{1,0:T(8,128)(2,1)} %get-tuple-element.151), channel_id=1, source_target_pairs={{0,8},{8,0},{16,24},{24,16},{1,9},{9,1},{17,25},{25,17},{2,10},{10... | collective-permute-start | bytes 3145736 | tf_op jit(solution)/shard_map/ppermute | solution.py:752
  200.4 25.5 %collective-permute-start.13 = (bf16[512,1024]{1,0:T(8,128)(2,1)}, bf16[512,1024]{1,0:T(8,128)(2,1)S(1)}, u32[]{:S(2)}, u32[]{:S(2)}) collective-permute-start(bf16[512,1024]{1,0:T(8,128)(2,1)} %get-tuple-element.152), channel_id=1, source_target_pairs={{0,16},{8,24},{16,0},{24,8},{1,17},{9,25},{17,1},{25,9},{2,18},{10... | collective-permute-start | bytes 3145736 | tf_op jit(solution)/shard_map/ppermute | solution.py:756
  244.6 49.4 %all-to-all-start.4 = ((bf16[8,64,1024]{2,1,0:T(8,128)(2,1)}), bf16[8,64,1024]{2,1,0:T(8,128)(2,1)}, u32[]{:S(2)}, u32[]{:S(2)}) async-start(bf16[8,64,1024]{2,1,0:T(8,128)(2,1)} %bitcast.32), calls=%async_computation.5 | async-start | bytes 2097152 | tf_op jit(solution)/shard_map/all_to_all | solution.py:980
  249.5 19.9 %collective-permute-start.14 = (bf16[512,768]{1,0:T(8,128)(2,1)S(1)}, bf16[512,768]{1,0:T(8,128)(2,1)S(1)}, u32[]{:S(2)}, u32[]{:S(2)}) collective-permute-start(bf16[512,768]{1,0:T(8,128)(2,1)S(1)} %copy-done.43), channel_id=1, source_target_pairs={{0,8},{8,0},{16,24},{24,16},{1,9},{9,1},{17,25},{25,17},{2,10},{10... | collective-permute-start | bytes 2359304 | tf_op jit(solution)/shard_map/ppermute | solution.py:752
  272.2 37.2 %collective-permute-start.20 = (bf16[320,2048]{1,0:T(8,128)(2,1)}, bf16[320,2048]{1,0:T(8,128)(2,1)S(1)}, u32[]{:S(2)}, u32[]{:S(2)}) collective-permute-start(bf16[320,2048]{1,0:T(8,128)(2,1)} %get-tuple-element.198), channel_id=1, source_target_pairs={{0,8},{8,0},{16,24},{24,16},{1,9},{9,1},{17,25},{25,17},{2,10},{10... | collective-permute-start | bytes 3932168 | tf_op jit(solution)/shard_map/ppermute | solution.py:752
  273.7 36.4 %collective-permute-start.21 = (bf16[320,2048]{1,0:T(8,128)(2,1)}, bf16[320,2048]{1,0:T(8,128)(2,1)S(1)}, u32[]{:S(2)}, u32[]{:S(2)}) collective-permute-start(bf16[320,2048]{1,0:T(8,128)(2,1)} %get-tuple-element.199), channel_id=1, source_target_pairs={{0,16},{8,24},{16,0},{24,8},{1,17},{9,25},{17,1},{25,9},{2,18},{10... | collective-permute-start | bytes 3932168 | tf_op jit(solution)/shard_map/ppermute | solution.py:756
  294.0 30.4 %all-to-all-start.5 = ((bf16[8,64,768]{2,1,0:T(8,128)(2,1)}), bf16[8,64,768]{2,1,0:T(8,128)(2,1)S(1)}, u32[]{:S(2)}, u32[]{:S(2)}) async-start(bf16[8,64,768]{2,1,0:T(8,128)(2,1)} %bitcast.87), calls=%async_computation.7 | async-start | bytes 1572864 | tf_op jit(solution)/shard_map/all_to_all | solution.py:983
  313.6 19.7 %collective-permute-start.22 = (bf16[160,2048]{1,0:T(8,128)(2,1)}, bf16[160,2048]{1,0:T(8,128)(2,1)}, u32[]{:S(2)}, u32[]{:S(2)}) collective-permute-start(bf16[160,2048]{1,0:T(8,128)(2,1)} %get-tuple-element.204), channel_id=1, source_target_pairs={{0,8},{8,0},{16,24},{24,16},{1,9},{9,1},{17,25},{25,17},{2,10},{10... | collective-permute-start | bytes 1966088 | tf_op jit(solution)/shard_map/ppermute | solution.py:752
  (62 other events, 473.0 us)
Sparse Core Ops, SparseCore 0:
  9.6 69.3 all-gather.5
  111.0 56.9 all-gather.3
  180.0 60.4 reduce-scatter.2
  242.6 73.8 reduce-scatter.4

commit v6 on v5

--- a/solution.py
+++ b/solution.py
@@ -987,7 +987,7 @@
     grad_up = repack(
         up_rows_body, "up_rows", jax.ShapeDtypeStruct((rows, HEADS * 1024), F32), up_back
     )
-    owned = lax.all_to_all(tie(totals, qkv_back), everywhere, 0, 0, tiled=True)
+    owned = lax.all_to_all(tie(totals, qkv_back, grad_up), everywhere, 0, 0, tiled=True)
     down_then = stage(down_then, (owned, grad_up))
     grad_down, grad_out = reduce_both(
         down_terms, down_got, down_then, w_down.shape[0], w_attn_out.shape[0]

time: 356 us -> 356 us (level)
  transfers between devices with their start and end apart: 35 -> 35, of which waited for: 19 -> 20; matrix products, arithmetic and copies ran while one was open for 8% -> 8% of each run, Pallas kernels for 31% -> 31%
where the time goes in v6:
time: 356 us; the launch traced here: 351 us
  waiting for transfers between devices  130 us (37%)
  Pallas kernels  110 us (31%)
  starting transfers between devices  54 us (15%)
  local copies, waits for them, and re-layouts  29.6 us (8%)
  between operations  14.7 us (4%)
  other arithmetic  13.1 us (4%)
    pallas_call x9, Pallas kernels, run(): pl.pallas_call(body, name=name, grid_spec=pltpu.PrefetchScalarGridSpec(nu...  97.5 us
    ppermute x12, waiting for transfers between devices, over_x(): return lax.ppermute(block, 'dp', swap(4, 1))  52.2 us
    ppermute x12, waiting for transfers between devices, over_y(): return lax.ppermute(block, 'dp', swap(4, 2))  44.8 us
    all_to_all x1, waiting for transfers between devices, line_shards(): lax.all_to_all(qkv_blocks, 'sp', 0, 0, tiled=True)  16.7 us
    unnamed x102, local copies, waits for them, and re-layouts  14 us
    ppermute x12, starting transfers between devices, over_x(): return lax.ppermute(block, 'dp', swap(4, 1))  13.8 us
    ppermute x12, starting transfers between devices, over_y(): return lax.ppermute(block, 'dp', swap(4, 2))  11.7 us
    all_to_all x1, waiting for transfers between devices, line_shards(): lax.all_to_all(up_sum.reshape(HEADS, rows, 1024), 'sp', 0, 0, tiled=True)  8.08 us
  transfers between devices with their start and end apart: 35, of which 20 were waited for; matrix products, arithmetic and copies ran while one was open for 8% of the time, Pallas kernels for 31%

profile of v6, /device:TPU:0, one launch (start us, length us, event | category | flops | bytes accessed | tf_op | source)
XLA Modules:
  0.0 351.1 jit_solution(867540881538348901)
XLA Ops:
  15.5 4.9 %all-to-all-start = ((bf16[8,64,896]{2,1,0:T(8,128)(2,1)}), bf16[8,64,896]{2,1,0:T(8,128)(2,1)S(1)}, u32[]{:S(2)}, u32[]{:S(2)}) async-start(bf16[8,64,896]{2,1,0:T(8,128)(2,1)} %qkv_blocks.1), calls=%async_computation | async-start | bytes 1835008 | tf_op jit(solution)/shard_map/all_to_all | solution.py:872
  20.6 20.7 %collective-permute-done.2.along_x.dx.refs_3_ = bf16[320,2048]{1,0:T(8,128)(2,1)S(1)} collective-permute-done((bf16[320,2048]{1,0:T(8,128)(2,1)S(1)}, bf16[320,2048]{1,0:T(8,128)(2,1)S(1)}, u32[]{:S(2)}, u32[]{:S(2)}) %collective-permute-start.2) | collective-permute-done | bytes 1310752 | tf_op jit(solution)/shard_map/ppermute | solution.py:752
  52.5 16.7 %all-to-all-done = bf16[8,64,896]{2,1,0:T(8,128)(2,1)S(1)} async-done(((bf16[8,64,896]{2,1,0:T(8,128)(2,1)}), bf16[8,64,896]{2,1,0:T(8,128)(2,1)S(1)}, u32[]{:S(2)}, u32[]{:S(2)}) %all-to-all-start) | async-done | bytes 917536 | tf_op jit(solution)/shard_map/all_to_all | solution.py:872
  70.0 3.6 %all-to-all-start.1 = ((bf16[8,64,1024]{2,1,0:T(8,128)(2,1)}), bf16[8,64,1024]{2,1,0:T(8,128)(2,1)S(1)}, u32[]{:S(2)}, u32[]{:S(2)}) async-start(bf16[8,64,1024]{2,1,0:T(8,128)(2,1)} %up_blocks.1), calls=%async_computation.1 | async-start | bytes 2097152 | tf_op jit(solution)/shard_map/all_to_all | solution.py:883
  77.2 19.1 %collective-permute-done.5.wy.refs_18_ = bf16[512,896]{1,0:T(8,128)(2,1)S(1)} collective-permute-done((bf16[512,896]{1,0:T(8,128)(2,1)S(1)}, bf16[512,896]{1,0:T(8,128)(2,1)S(1)}, u32[]{:S(2)}, u32[]{:S(2)}) %collective-permute-start.5) | collective-permute-done | bytes 917536 | tf_op jit(solution)/shard_map/ppermute | solution.py:756
  99.6 10.8 %collective-permute-done.7.w2.refs_20_ = bf16[256,896]{1,0:T(8,128)(2,1)S(1)} collective-permute-done((bf16[256,896]{1,0:T(8,128)(2,1)S(1)}, bf16[256,896]{1,0:T(8,128)(2,1)S(1)}, u32[]{:S(2)}, u32[]{:S(2)}) %collective-permute-start.7) | collective-permute-done | bytes 458784 | tf_op jit(solution)/shard_map/ppermute | solution.py:756
  115.8 3.5 %all-to-all-start.2 = ((bf16[4,64,2048]{2,1,0:T(8,128)(2,1)}), bf16[4,64,2048]{2,1,0:T(8,128)(2,1)S(1)}, u32[]{:S(2)}, u32[]{:S(2)}) async-start(bf16[4,64,2048]{2,1,0:T(8,128)(2,1)} %out_rows.1), calls=%async_computation.2 | async-start | bytes 2097152 | tf_op jit(solution)/shard_map/all_to_all | solution.py:897
  122.5 7.8 %norms.1 = (bf16[1024,2048]{1,0:T(8,128)(2,1)}, bf16[1024,2048]{1,0:T(8,128)(2,1)}) custom-call(s32[1]{0:T(128)} %bitcast.1.dp, bf16[1024,2048]{1,0:T(8,128)(2,1)} %bitcast.89, f32[4,2048]{1,0:T(4,128)} %slice.115.vec.refs_10_), custom_call_target="tpu_custom_call" | custom-call | bytes 12615680 | tf_op jit(solution)/shard_map/norms/pallas_call | solution.py:341
  130.2 8.2 %qkv.1 = (bf16[1024,256]{1,0:T(8,128)(2,1)}, bf16[1024,256]{1,0:T(8,128)(2,1)}, bf16[1024,256]{1,0:T(8,128)(2,1)}) custom-call(s32[1]{0:T(128)} %bitcast.1.dp, bf16[1024,2048]{1,0:T(8,128)(2,1)} %get-tuple-element.121.first.refs_13_, bf16[512,896]{1,0:T(8,128)(2,1)} %bitcast.94, bf16[512,896]{1,0:T(8,128)(2,1)} %collective-permute-done.4.wx.refs_17_, ...), custom_call_target="tpu_custom_call" | custom-call | flops 3221225472 | bytes 11013120 | tf_op jit(solution)/shard_map/qkv/pallas_call | solution.py:341
  144.2 5.7 %attend_forward.1 = (f32[1024,256]{1,0:T(8,128)}, bf16[1024,256]{1,0:T(8,128)(2,1)}, f32[1024,1]{1,0:T(8,128)}) custom-call(s32[1]{0:T(128)} %bitcast.1.dp, bf16[1024,256]{1,0:T(8,128)(2,1)} %get-tuple-element.146.q.refs_0_, bf16[1024,256]{1,0:T(8,128)(2,1)} %get-tuple-element.130.k.refs_1_, bf16[1024,256]{1,0:T(8,128)(2,1)} %get-tuple-element.131.v.refs_2_, ...), custom_call_target="tpu_custom_call" | custom-call | flops 805306368 | bytes 3158016 | tf_op jit(solution)/shard_map/attend_forward/pallas_call | solution.py:341
  149.9 5.1 %collective-permute-done.10.u1.refs_24_ = bf16[256,1024]{1,0:T(8,128)(2,1)S(1)} collective-permute-done((bf16[256,1024]{1,0:T(8,128)(2,1)S(1)}, bf16[256,1024]{1,0:T(8,128)(2,1)S(1)}, u32[]{:S(2)}, u32[]{:S(2)}) %collective-permute-start.10) | collective-permute-done | bytes 524320 | tf_op jit(solution)/shard_map/ppermute | solution.py:752
  157.3 10.8 %mlp_forward.1 = (bf16[1024,1024]{1,0:T(8,128)(2,1)}, f32[1024,1024]{1,0:T(8,128)}) custom-call(s32[1]{0:T(128)} %bitcast.1.dp, bf16[1024,2048]{1,0:T(8,128)(2,1)} %get-tuple-element.127.second.refs_7_, bf16[512,1024]{1,0:T(8,128)(2,1)} %bitcast.98, bf16[512,1024]{1,0:T(8,128)(2,1)} %collective-permute-done.8.ux.refs_22_, ...), custom_call_target="tpu_custom_call" | custom-call | flops 4294967296 | bytes 14684160 | tf_op jit(solution)/shard_map/mlp_forward/pallas_call | solution.py:341
  169.1 10.7 %output.1 = bf16[1024,2048]{1,0:T(8,128)(2,1)} custom-call(s32[1]{0:T(128)} %bitcast.1.dp, bf16[1024,256]{1,0:T(8,128)(2,1)} %get-tuple-element.140.ctx.refs_8_, bf16[1024,1024]{1,0:T(8,128)(2,1)} %get-tuple-element.175.active.refs_0_, bf16[256,2048]{1,0:T(8,128)(2,1)} %bitcast.100, bf16[320,2048]{1,0:T(8,128)(2,1)} %copy-done.18, ...), custom_call_target="tpu_custom_call" | custom-call | flops 5368709120 | bytes 13107200 | tf_op jit(solution)/shard_map/output/pallas_call | solution.py:341
  179.9 16.1 %middle.1 = (bf16[1024,1024]{1,0:T(8,128)(2,1)}, f32[1,1024]{1,0:T(1,128)}, bf16[256,2048]{1,0:T(8,128)(2,1)}, bf16[512,1024]{1,0:T(8,128)(2,1)}, bf16[512,1024]...) custom-call(s32[1]{0:T(128)} %bitcast.1.dp, ...), custom_call_target="tpu_custom_call" | custom-call | flops 8589934592 | bytes 25694208 | tf_op jit(solution)/shard_map/middle/pallas_call | solution.py:341
  201.0 24.8 %last.1 = (f32[1,768]{1,0:T(1,128)}, f32[4,2048]{1,0:T(4,128)}, bf16[1024,2048]{1,0:T(8,128)(2,1)}, bf16[512,768]{1,0:T(8,128)(2,1)}, bf16[512,768]{1,0:T(8,128)...) custom-call(s32[1]{0:T(128)} %bitcast.1.dp, ...), custom_call_target="tpu_custom_call" | custom-call | flops 13421772800 | bytes 35208192 | tf_op jit(solution)/shard_map/last/pallas_call | solution.py:341
  231.4 10.9 %collective-permute-done.17.y_top = bf16[256,1024]{1,0:T(8,128)(2,1)S(1)} collective-permute-done((bf16[256,1024]{1,0:T(8,128)(2,1)S(1)}, bf16[256,1024]{1,0:T(8,128)(2,1)S(1)}, u32[]{:S(2)}, u32[]{:S(2)}) %collective-permute-start.17) | collective-permute-done | bytes 524320 | tf_op jit(solution)/shard_map/ppermute | solution.py:756
  244.6 4.9 %all-to-all-start.4 = ((bf16[8,64,1024]{2,1,0:T(8,128)(2,1)}), bf16[8,64,1024]{2,1,0:T(8,128)(2,1)}, u32[]{:S(2)}, u32[]{:S(2)}) async-start(bf16[8,64,1024]{2,1,0:T(8,128)(2,1)} %bitcast.32), calls=%async_computation.5 | async-start | bytes 2097152 | tf_op jit(solution)/shard_map/all_to_all | solution.py:980
  253.0 10.1 %outward.1 = (bf16[320,2048]{1,0:T(8,128)(2,1)}, bf16[320,2048]{1,0:T(8,128)(2,1)}, bf16[160,2048]{1,0:T(8,128)(2,1)}, bf16[160,2048]{1,0:T(8,128)(2,1)}, bf16[320,2048]{1,0:T(8,128)(2,1)}) custom-call(s32[1]{0:T(128)} %bitcast.1.dp, bf16[1024,1024]{1,0:T(8,128)(2,1)} %get-tuple-element.175.active.refs_0_, ...), custom_call_target="tpu_custom_call" | custom-call | flops 4294967296 | bytes 12582912 | tf_op jit(solution)/shard_map/outward/pallas_call | solution.py:341
  263.1 6.3 %collective-permute-done.14.got_x = bf16[512,768]{1,0:T(8,128)(2,1)S(1)} collective-permute-done((bf16[512,768]{1,0:T(8,128)(2,1)S(1)}, bf16[512,768]{1,0:T(8,128)(2,1)S(1)}, u32[]{:S(2)}, u32[]{:S(2)}) %collective-permute-start.14) | collective-permute-done | bytes 786464 | tf_op jit(solution)/shard_map/ppermute | solution.py:752
  275.0 8.0 %collective-permute-done.18.x_low = bf16[256,768]{1,0:T(8,128)(2,1)S(1)} collective-permute-done((bf16[256,768]{1,0:T(8,128)(2,1)S(1)}, bf16[256,768]{1,0:T(8,128)(2,1)S(1)}, u32[]{:S(2)}, u32[]{:S(2)}) %collective-permute-start.18) | collective-permute-done | bytes 393248 | tf_op jit(solution)/shard_map/ppermute | solution.py:752
  285.9 8.1 %all-to-all-done.4.source = bf16[8,64,1024]{2,1,0:T(8,128)(2,1)} async-done(((bf16[8,64,1024]{2,1,0:T(8,128)(2,1)}), bf16[8,64,1024]{2,1,0:T(8,128)(2,1)}, u32[]{:S(2)}, u32[]{:S(2)}) %all-to-all-start.4) | async-done | bytes 1048608 | tf_op jit(solution)/shard_map/all_to_all | solution.py:980
  298.8 10.6 %collective-permute-done.20.got_x = bf16[320,2048]{1,0:T(8,128)(2,1)S(1)} collective-permute-done((bf16[320,2048]{1,0:T(8,128)(2,1)}, bf16[320,2048]{1,0:T(8,128)(2,1)S(1)}, u32[]{:S(2)}, u32[]{:S(2)}) %collective-permute-start.20) | collective-permute-done | bytes 1310752 | tf_op jit(solution)/shard_map/ppermute | solution.py:752
  318.9 5.5 %all-to-all-done.5.source = bf16[8,64,768]{2,1,0:T(8,128)(2,1)S(1)} async-done(((bf16[8,64,768]{2,1,0:T(8,128)(2,1)}), bf16[8,64,768]{2,1,0:T(8,128)(2,1)S(1)}, u32[]{:S(2)}, u32[]{:S(2)}) %all-to-all-start.5) | async-done | bytes 786464 | tf_op jit(solution)/shard_map/all_to_all | solution.py:983
  326.0 3.8 %all-to-all-start.6 = ((f32[32,1,768]{2,1,0:T(1,128)}), f32[32,1,768]{2,1,0:T(1,128)}, u32[]{:S(2)}, u32[]{:S(2)}) async-start(f32[32,1,768]{2,1,0:T(1,128)} %copy.44), calls=%async_computation.8 | async-start | bytes 196608 | tf_op jit(solution)/shard_map/all_to_all | solution.py:990
  (248 shorter events, 99.6 us)
Async XLA Ops:
  7.2 115.3 %all-gather.6.cloned.1.call-start = ((), (), s32[]{:S(2)}) async-start(), calls=%async_computation.12 | async-start | bytes 4718592 | tf_op jit(solution)/shard_map/all_gather | solution.py:853
  9.4 31.8 %collective-permute-start.2 = (bf16[320,2048]{1,0:T(8,128)(2,1)S(1)}, bf16[320,2048]{1,0:T(8,128)(2,1)S(1)}, u32[]{:S(2)}, u32[]{:S(2)}) collective-permute-start(bf16[320,2048]{1,0:T(8,128)(2,1)S(1)} %constant_dynamic-update-slice_fusion.own.d0.refs_2_), channel_id=1, source_target_pairs={{0,8},{8,0},{16,24},{24,16},{1,9},{9,1},{17,25},{25,17},{2,10},{10... | collective-permute-start | bytes 3932168 | tf_op jit(solution)/shard_map/ppermute | solution.py:752
  12.5 33.8 %collective-permute-start = (bf16[320,2048]{1,0:T(8,128)(2,1)S(1)}, bf16[320,2048]{1,0:T(8,128)(2,1)}, u32[]{:S(2)}, u32[]{:S(2)}) collective-permute-start(bf16[320,2048]{1,0:T(8,128)(2,1)S(1)} %constant_dynamic-update-slice_fusion.own.d0.refs_2_), channel_id=1, source_target_pairs={{0,16},{8,24},{16,0},{24,8},{1,17},{9,25},{17,1},{25,9},{2,18},{10... | collective-permute-start | bytes 3932168 | tf_op jit(solution)/shard_map/ppermute | solution.py:756
  15.5 53.7 %all-to-all-start = ((bf16[8,64,896]{2,1,0:T(8,128)(2,1)}), bf16[8,64,896]{2,1,0:T(8,128)(2,1)S(1)}, u32[]{:S(2)}, u32[]{:S(2)}) async-start(bf16[8,64,896]{2,1,0:T(8,128)(2,1)} %qkv_blocks.1), calls=%async_computation | async-start | bytes 1835008 | tf_op jit(solution)/shard_map/all_to_all | solution.py:872
  42.2 27.0 %collective-permute-start.3 = (bf16[192,2048]{1,0:T(8,128)(2,1)}, bf16[192,2048]{1,0:T(8,128)(2,1)}, u32[]{:S(2)}, u32[]{:S(2)}) collective-permute-start(bf16[192,2048]{1,0:T(8,128)(2,1)} %slice.131), channel_id=1, source_target_pairs={{0,16},{8,24},{16,0},{24,8},{1,17},{9,25},{17,1},{25,9},{2,18},{10... | collective-permute-start | bytes 2359304 | tf_op jit(solution)/shard_map/ppermute | solution.py:756
  47.3 21.9 %collective-permute-start.1 = (bf16[128,2048]{1,0:T(8,128)(2,1)S(1)}, bf16[128,2048]{1,0:T(8,128)(2,1)S(1)}, u32[]{:S(2)}, u32[]{:S(2)}) collective-permute-start(bf16[128,2048]{1,0:T(8,128)(2,1)S(1)} %slice.130), channel_id=1, source_target_pairs={{0,8},{8,0},{16,24},{24,16},{1,9},{9,1},{17,25},{25,17},{2,10},{10... | collective-permute-start | bytes 1572872 | tf_op jit(solution)/shard_map/ppermute | solution.py:752
  70.0 40.8 %all-to-all-start.1 = ((bf16[8,64,1024]{2,1,0:T(8,128)(2,1)}), bf16[8,64,1024]{2,1,0:T(8,128)(2,1)S(1)}, u32[]{:S(2)}, u32[]{:S(2)}) async-start(bf16[8,64,1024]{2,1,0:T(8,128)(2,1)} %up_blocks.1), calls=%async_computation.1 | async-start | bytes 2097152 | tf_op jit(solution)/shard_map/all_to_all | solution.py:883
  73.6 106.3 %all-gather.4.cloned.1.call-start = ((), (), s32[]{:S(2)}) async-start(), calls=%async_computation.9 | async-start | bytes 4718592 | tf_op jit(solution)/shard_map/all_gather | solution.py:895
  73.7 22.6 %collective-permute-start.5 = (bf16[512,896]{1,0:T(8,128)(2,1)S(1)}, bf16[512,896]{1,0:T(8,128)(2,1)S(1)}, u32[]{:S(2)}, u32[]{:S(2)}) collective-permute-start(bf16[512,896]{1,0:T(8,128)(2,1)S(1)} %bitcast.91), channel_id=1, source_target_pairs={{0,16},{8,24},{16,0},{24,8},{1,17},{9,25},{17,1},{25,9},{2,18},{10... | collective-permute-start | bytes 2752520 | tf_op jit(solution)/shard_map/ppermute | solution.py:756
  73.7 22.7 %collective-permute-start.4 = (bf16[512,896]{1,0:T(8,128)(2,1)S(1)}, bf16[512,896]{1,0:T(8,128)(2,1)}, u32[]{:S(2)}, u32[]{:S(2)}) collective-permute-start(bf16[512,896]{1,0:T(8,128)(2,1)S(1)} %bitcast.92), channel_id=1, source_target_pairs={{0,8},{8,0},{16,24},{24,16},{1,9},{9,1},{17,25},{25,17},{2,10},{10... | collective-permute-start | bytes 2752520 | tf_op jit(solution)/shard_map/ppermute | solution.py:752
  112.3 26.1 %collective-permute-start.9 = (bf16[512,1024]{1,0:T(8,128)(2,1)S(1)}, bf16[512,1024]{1,0:T(8,128)(2,1)}, u32[]{:S(2)}, u32[]{:S(2)}) collective-permute-start(bf16[512,1024]{1,0:T(8,128)(2,1)S(1)} %bitcast.96), channel_id=1, source_target_pairs={{0,16},{8,24},{16,0},{24,8},{1,17},{9,25},{17,1},{25,9},{2,18},{10... | collective-permute-start | bytes 3145736 | tf_op jit(solution)/shard_map/ppermute | solution.py:756
  113.7 24.7 %collective-permute-start.8 = (bf16[512,1024]{1,0:T(8,128)(2,1)S(1)}, bf16[512,1024]{1,0:T(8,128)(2,1)}, u32[]{:S(2)}, u32[]{:S(2)}) collective-permute-start(bf16[512,1024]{1,0:T(8,128)(2,1)S(1)} %bitcast.97), channel_id=1, source_target_pairs={{0,8},{8,0},{16,24},{24,16},{1,9},{9,1},{17,25},{25,17},{2,10},{10... | collective-permute-start | bytes 3145736 | tf_op jit(solution)/shard_map/ppermute | solution.py:752
  115.8 52.3 %all-to-all-start.2 = ((bf16[4,64,2048]{2,1,0:T(8,128)(2,1)}), bf16[4,64,2048]{2,1,0:T(8,128)(2,1)S(1)}, u32[]{:S(2)}, u32[]{:S(2)}) async-start(bf16[4,64,2048]{2,1,0:T(8,128)(2,1)} %out_rows.1), calls=%async_computation.2 | async-start | bytes 2097152 | tf_op jit(solution)/shard_map/all_to_all | solution.py:897
  119.4 174.6 %reduce-scatter.3.cloned.1.call-start = ((), (), s32[]{:S(2)}) async-start(), calls=%async_computation.10 | async-start | bytes 4718592 | tf_op jit(solution)/shard_map/reduce_scatter | solution.py:925
  196.0 30.1 %all-to-all-start.3 = ((bf16[4,64,2048]{2,1,0:T(8,128)(2,1)}), bf16[4,64,2048]{2,1,0:T(8,128)(2,1)S(1)}, u32[]{:S(2)}, u32[]{:S(2)}) async-start(bf16[4,64,2048]{2,1,0:T(8,128)(2,1)} %bitcast.102), calls=%async_computation.3 | async-start | bytes 2097152 | tf_op jit(solution)/shard_map/all_to_all | solution.py:929
  199.5 140.8 %reduce-scatter.5.cloned.1.call-start = ((), (), s32[]{:S(2)}) async-start(), calls=%async_computation.11 | async-start | bytes 4718592 | tf_op jit(solution)/shard_map/reduce_scatter | solution.py:961
  200.0 25.9 %collective-permute-start.12 = (bf16[512,1024]{1,0:T(8,128)(2,1)}, bf16[512,1024]{1,0:T(8,128)(2,1)S(1)}, u32[]{:S(2)}, u32[]{:S(2)}) collective-permute-start(bf16[512,1024]{1,0:T(8,128)(2,1)} %get-tuple-element.151), channel_id=1, source_target_pairs={{0,8},{8,0},{16,24},{24,16},{1,9},{9,1},{17,25},{25,17},{2,10},{10... | collective-permute-start | bytes 3145736 | tf_op jit(solution)/shard_map/ppermute | solution.py:752
  200.4 25.5 %collective-permute-start.13 = (bf16[512,1024]{1,0:T(8,128)(2,1)}, bf16[512,1024]{1,0:T(8,128)(2,1)S(1)}, u32[]{:S(2)}, u32[]{:S(2)}) collective-permute-start(bf16[512,1024]{1,0:T(8,128)(2,1)} %get-tuple-element.152), channel_id=1, source_target_pairs={{0,16},{8,24},{16,0},{24,8},{1,17},{9,25},{17,1},{25,9},{2,18},{10... | collective-permute-start | bytes 3145736 | tf_op jit(solution)/shard_map/ppermute | solution.py:756
  244.6 49.4 %all-to-all-start.4 = ((bf16[8,64,1024]{2,1,0:T(8,128)(2,1)}), bf16[8,64,1024]{2,1,0:T(8,128)(2,1)}, u32[]{:S(2)}, u32[]{:S(2)}) async-start(bf16[8,64,1024]{2,1,0:T(8,128)(2,1)} %bitcast.32), calls=%async_computation.5 | async-start | bytes 2097152 | tf_op jit(solution)/shard_map/all_to_all | solution.py:980
  249.5 19.9 %collective-permute-start.14 = (bf16[512,768]{1,0:T(8,128)(2,1)S(1)}, bf16[512,768]{1,0:T(8,128)(2,1)S(1)}, u32[]{:S(2)}, u32[]{:S(2)}) collective-permute-start(bf16[512,768]{1,0:T(8,128)(2,1)S(1)} %copy-done.43), channel_id=1, source_target_pairs={{0,8},{8,0},{16,24},{24,16},{1,9},{9,1},{17,25},{25,17},{2,10},{10... | collective-permute-start | bytes 2359304 | tf_op jit(solution)/shard_map/ppermute | solution.py:752
  251.1 19.6 %collective-permute-start.15 = (bf16[512,768]{1,0:T(8,128)(2,1)S(1)}, bf16[512,768]{1,0:T(8,128)(2,1)S(1)}, u32[]{:S(2)}, u32[]{:S(2)}) collective-permute-start(bf16[512,768]{1,0:T(8,128)(2,1)S(1)} %copy-done.42), channel_id=1, source_target_pairs={{0,16},{8,24},{16,0},{24,8},{1,17},{9,25},{17,1},{25,9},{2,18},{10... | collective-permute-start | bytes 2359304 | tf_op jit(solution)/shard_map/ppermute | solution.py:756
  272.2 37.2 %collective-permute-start.20 = (bf16[320,2048]{1,0:T(8,128)(2,1)}, bf16[320,2048]{1,0:T(8,128)(2,1)S(1)}, u32[]{:S(2)}, u32[]{:S(2)}) collective-permute-start(bf16[320,2048]{1,0:T(8,128)(2,1)} %get-tuple-element.198), channel_id=1, source_target_pairs={{0,8},{8,0},{16,24},{24,16},{1,9},{9,1},{17,25},{25,17},{2,10},{10... | collective-permute-start | bytes 3932168 | tf_op jit(solution)/shard_map/ppermute | solution.py:752
  273.7 36.4 %collective-permute-start.21 = (bf16[320,2048]{1,0:T(8,128)(2,1)}, bf16[320,2048]{1,0:T(8,128)(2,1)S(1)}, u32[]{:S(2)}, u32[]{:S(2)}) collective-permute-start(bf16[320,2048]{1,0:T(8,128)(2,1)} %get-tuple-element.199), channel_id=1, source_target_pairs={{0,16},{8,24},{16,0},{24,8},{1,17},{9,25},{17,1},{25,9},{2,18},{10... | collective-permute-start | bytes 3932168 | tf_op jit(solution)/shard_map/ppermute | solution.py:756
  294.0 30.4 %all-to-all-start.5 = ((bf16[8,64,768]{2,1,0:T(8,128)(2,1)}), bf16[8,64,768]{2,1,0:T(8,128)(2,1)S(1)}, u32[]{:S(2)}, u32[]{:S(2)}) async-start(bf16[8,64,768]{2,1,0:T(8,128)(2,1)} %bitcast.87), calls=%async_computation.7 | async-start | bytes 1572864 | tf_op jit(solution)/shard_map/all_to_all | solution.py:983
  (62 other events, 472.8 us)
Sparse Core Ops, SparseCore 0:
  9.6 69.3 all-gather.5
  111.0 56.9 all-gather.3
  180.0 60.4 reduce-scatter.2
  242.6 73.8 reduce-scatter.4
